TPU v7x, 32 devices: a whole 2x2x4 slice. The times are simulated.
32 devices in a mesh: row: 8 (over y, x, core), col: 4 (over z).
Axes of the slice: x: 2, y: 2, z: 4, core: 2. Of those that a mesh axis runs over, the one named last changes fastest.
Arguments:
- momentum: float32 [8192, 16384], P('row', 'col'), may hold values from -6 to 6
- right_factor: float32 [16384, 256], P('col'), may hold values from -0.046875 to 0.046875
Outputs:
- new_momentum: float32 [8192, 16384], P('row', 'col')
- update: float32 [8192, 16384], P('row', 'col')
All inputs are finite; a program needn't handle non-finite values.
Results may differ from a plain program's by a relative error of at most 0.0001.
Values sent between devices are 32-bit elements; how exact they have to be, the bound alone decides.
No kernel may reach another device: no remote copies, remote signals or barrier semaphores. Data moves between devices by JAX's collectives and lax.ppermute only.
A program may use at most 128 MiB of HBM per device.

v0:
```python
import math

import jax
import jax.numpy as jnp
from jax import lax
from jax.experimental import pallas as pl
from jax.experimental.pallas import tpu as pltpu
from jax.sharding import PartitionSpec as P

F32 = jnp.float32
BF16 = jnp.bfloat16
HIGHEST = lax.Precision.HIGHEST
VMEM_LIMIT = 20 * 1024 * 1024
SMEM = pl.BlockSpec(memory_space=pltpu.SMEM)
VMEM = pl.BlockSpec(memory_space=pltpu.VMEM)
HBM = pl.BlockSpec(memory_space=pltpu.HBM)
ANY = pl.BlockSpec(memory_space=pl.ANY)
LINE = 4
RING = 8


def split(x):
    high = x.astype(BF16)
    return high, (x - high.astype(F32)).astype(BF16)


def dot(a, b):
    return jnp.dot(a, b, preferred_element_type=F32)


def params():
    return pltpu.CompilerParams(vmem_limit_bytes=VMEM_LIMIT)


def cost(flops, bytes_accessed):
    return pl.CostEstimate(flops=int(flops), bytes_accessed=int(bytes_accessed), transcendentals=0)


def in_vmem(x):
    return pltpu.with_memory_space_constraint(x, pltpu.VMEM)


def in_hbm(x):
    return pltpu.with_memory_space_constraint(x, pltpu.HBM)


def three(high, low, axis):
    return jnp.concatenate([high, high, low], axis=axis)


def three_other(high, low, axis):
    return jnp.concatenate([high, low, high], axis=axis)


def fetch_kernel(m_hbm, q_hbm, m_ref, high_ref, low_ref, q_ref, m_sem, q_sem):
    half = q_ref.shape[0] // 2
    spans = [pl.ds(k * half, half) for k in range(2)]
    copies = [pltpu.make_async_copy(q_hbm.at[span], q_ref.at[span], q_sem.at[k]) for k, span in enumerate(spans)]
    whole = pltpu.make_async_copy(m_hbm, m_ref, m_sem)
    for copy in copies:
        copy.start()
    whole.start()
    for copy, span in zip(copies, spans):
        copy.wait()
        high_ref[span, :], low_ref[span, :] = split(q_ref[span, :])
    whole.wait()


def fetch(momentum, factor):
    cols, rank = factor.shape
    return pl.pallas_call(
        fetch_kernel,
        in_specs=[HBM, HBM],
        out_specs=[ANY, VMEM, VMEM],
        out_shape=[
            pltpu.VMEM(momentum.shape, F32),
            pltpu.VMEM((cols, rank), BF16),
            pltpu.VMEM((cols, rank), BF16),
        ],
        scratch_shapes=[pltpu.VMEM((cols, rank), F32), pltpu.SemaphoreType.DMA, pltpu.SemaphoreType.DMA((2,))],
        compiler_params=params(),
        cost_estimate=cost(cols * rank, 4 * cols * (momentum.shape[0] + rank)),
        name="fetch",
    )(in_hbm(momentum), in_hbm(factor))


def left_kernel(at, m_ref, high_ref, low_ref, out_ref):
    half = high_ref.shape[0] // 2
    total = None
    for k in range(2):
        span = pl.ds(k * half, half)
        piece = m_ref[pl.ds(at, out_ref.shape[0]), span]
        part = dot(three(*split(piece), 1), three_other(high_ref[span, :], low_ref[span, :], 0))
        total = part if total is None else total + part
    out_ref[...] = total


def left_piece(momentum, high, low, at, size):
    cols, rank = high.shape
    return pl.pallas_call(
        lambda *refs: left_kernel(at, *refs),
        in_specs=[VMEM] * 3,
        out_specs=VMEM,
        out_shape=jax.ShapeDtypeStruct((size, rank), F32),
        compiler_params=params(),
        cost_estimate=cost(6 * size * cols * rank, 2**20),
        name="left",
    )(in_vmem(momentum), in_vmem(high), in_vmem(low))


def raw_kernel(at, groups, added, with_gram, order_ref, left_ref, m_ref, *refs):
    count = len(groups) + with_gram
    before_refs, out_refs = refs[: count * added], refs[count * added :]
    left = left_ref[...]
    lhs = three(*split(left.T), 1)
    if with_gram:
        gram = full_dot(left, left, ((0,), (0,)))
        out_refs[-1][...] = before_refs[-1][...] + gram if added else gram
    for g, places in enumerate(groups):
        width = out_refs[g].shape[2]
        for s, place in enumerate(places):
            span = pl.ds(pl.multiple_of(order_ref[place] * width, width), width)
            part = dot(lhs, three_other(*split(m_ref[pl.ds(at, left.shape[0]), span]), 0))
            out_refs[g][s] = before_refs[g][s] + part if added else part


def raw_pieces(order, groups, left, momentum, at, before, with_gram):
    rows, rank = left.shape
    width = momentum.shape[1] // order.shape[0]
    chunks = sum(len(places) for places in groups)
    shapes = [jax.ShapeDtypeStruct((len(places), rank, width), F32) for places in groups]
    shapes += [jax.ShapeDtypeStruct((rank, rank), F32)] * with_gram
    return pl.pallas_call(
        lambda *refs: raw_kernel(at, groups, bool(before), with_gram, *refs),
        in_specs=[SMEM] + [VMEM] * (2 + len(before)),
        out_specs=[VMEM] * len(shapes),
        out_shape=shapes,
        compiler_params=params(),
        cost_estimate=cost(6 * rows * rank * width * chunks, 2**20),
        name="raw_right",
    )(order, left, in_vmem(momentum), *before)


def gram_kernel(chunks, order_ref, left_ref, before_ref, out_ref):
    left = left_ref[...]
    total = before_ref[...] + full_dot(left, left, ((0,), (0,)))
    half = total.shape[0] // 2
    first = order_ref[0] < chunks
    out_ref[0] = jnp.where(first, total[:half], total[half:])
    out_ref[1] = jnp.where(first, total[half:], total[:half])


def gram_halves(order, left, before):
    rank = left.shape[1]
    return pl.pallas_call(
        lambda *refs: gram_kernel(order.shape[0] // 2, *refs),
        in_specs=[SMEM, VMEM, VMEM],
        out_specs=VMEM,
        out_shape=jax.ShapeDtypeStruct((2, rank // 2, rank), F32),
        compiler_params=params(),
        cost_estimate=cost(12 * rank * rank * left.shape[0], 2**20),
        name="gram",
    )(order, left, before)


def full_dot(a, b, contract=((1,), (0,))):
    return lax.dot_general(a, b, (contract, ((), ())), precision=HIGHEST, preferred_element_type=F32)


def rough_dot(a, b, contract=((1,), (0,))):
    return lax.dot_general(a.astype(BF16), b.astype(BF16), (contract, ((), ())), preferred_element_type=F32)


def newton(gram_ref, x_ref):
    rank = gram_ref.shape[0]
    rows = lax.broadcasted_iota(jnp.int32, (rank, rank), 0)
    cols = lax.broadcasted_iota(jnp.int32, (rank, rank), 1)
    eye = jnp.where(rows == cols, 1.0, 0.0).astype(F32)
    gram = gram_ref[...]
    x = eye * lax.rsqrt(jnp.sum(gram * eye, axis=1, keepdims=True))
    for times in (rough_dot, rough_dot, full_dot, full_dot):
        error = times(times(x, gram), x, ((1,), (1,))) - eye
        x = x - times(jnp.where(rows > cols, error, 0.5 * eye * error), x)
    x_ref[...] = x
    return jnp.sum(error * error), jnp.min(jnp.where(rows == cols, x, 1.0))


def eliminate(work_ref):
    rank = work_ref.shape[0]
    rows = lax.broadcasted_iota(jnp.int32, (rank, 2 * rank), 0)
    cols = lax.broadcasted_iota(jnp.int32, (rank, 2 * rank), 1)

    def step(j, carry):
        work = work_ref[...]
        row = work_ref[pl.ds(j, 1), :]
        pivot = jnp.sum(jnp.where(cols[:1] == j, row, 0.0), axis=1, keepdims=True)
        column = jnp.sum(jnp.where(cols == j, work, 0.0), axis=1, keepdims=True)
        ratio = jnp.where(rows[:, :1] > j, column * (1.0 / pivot), 0.0)
        work_ref[...] = work - ratio * row
        return carry

    lax.fori_loop(0, rank, step, 0)
    work = work_ref[...]
    pivots = jnp.sum(jnp.where(rows == cols, work, 0.0), axis=1, keepdims=True)
    return jnp.where(rows + rank >= cols, work / jnp.sqrt(pivots), 0.0)[:, rank:]


def factor_kernel(pieces, chunks, order_ref, kept_ref, sent_ref, *refs):
    left_refs = refs[:pieces]
    inv_ref, orth_ref, operand_ref, gram_ref, work_ref = refs[pieces:]
    half, rank = kept_ref.shape
    first = order_ref[0] < chunks
    gram_ref[:half] = jnp.where(first, kept_ref[...], sent_ref[...])
    gram_ref[half:] = jnp.where(first, sent_ref[...], kept_ref[...])
    before, least = newton(gram_ref, inv_ref)

    @pl.when(jnp.logical_not((before < 1e-6) & (least > 0.0)))
    def _():
        rows = lax.broadcasted_iota(jnp.int32, (rank, rank), 0)
        cols = lax.broadcasted_iota(jnp.int32, (rank, rank), 1)
        work_ref[:, :rank] = gram_ref[...]
        work_ref[:, rank:] = jnp.where(rows == cols, 1.0, 0.0).astype(F32)
        inv_ref[...] = eliminate(work_ref)

    inverse = three_other(*split(inv_ref[...]), 1)
    at = 0
    for ref in left_refs:
        size = ref.shape[0]
        orth = lax.dot_general(
            three(*split(ref[...]), 1), inverse, (((1,), (1,)), ((), ())), preferred_element_type=F32
        )
        orth_ref[at : at + size, :] = orth
        operand_ref[at : at + size, :] = three(*split(-0.5 * orth), 1)
        at += size


def factor(order, kept, sent, lefts):
    rank = kept.shape[1]
    rows = sum(x.shape[0] for x in lefts)
    return pl.pallas_call(
        lambda *refs: factor_kernel(len(lefts), order.shape[0] // 2, *refs),
        in_specs=[SMEM] + [VMEM] * (2 + len(lefts)),
        out_specs=[VMEM] * 3,
        out_shape=[
            jax.ShapeDtypeStruct((rank, rank), F32),
            jax.ShapeDtypeStruct((rows, rank), F32),
            jax.ShapeDtypeStruct((rows, 3 * rank), BF16),
        ],
        scratch_shapes=[pltpu.VMEM((rank, rank), F32), pltpu.VMEM((rank, 2 * rank), F32)],
        compiler_params=params(),
        cost_estimate=cost(5 * 10**9, 2**22),
        name="factor",
    )(order, kept, sent, *lefts)


def square_kernel(inv_ref, raw_ref, out_ref):
    right = jnp.dot(inv_ref[...], raw_ref[0], precision=HIGHEST, preferred_element_type=F32)
    ones = jnp.ones((8, right.shape[1]), F32)
    out_ref[...] = lax.dot_general(
        ones, right * right, (((1,), (1,)), ((), ())), precision=HIGHEST, preferred_element_type=F32
    )


def square_row(inverse, raw):
    rank = inverse.shape[0]
    return pl.pallas_call(
        square_kernel,
        out_shape=jax.ShapeDtypeStruct((8, rank), F32),
        compiler_params=params(),
        cost_estimate=cost(12 * rank * rank * raw.shape[2], 2**20),
        name="squares",
    )(inverse, raw)


def operand_kernel(count, scale, *refs):
    square_refs = refs[:count]
    orth_ref, operand_ref = refs[count:]
    squares = square_refs[0][...]
    for ref in square_refs[1:]:
        squares = squares + ref[...]
    norm = scale / jnp.sqrt(squares[:1] + 1e-06)
    operand_ref[...] = three(*split(orth_ref[...] * norm), 1)


def update_operand(squares, orth, scale):
    rows, rank = orth.shape
    return pl.pallas_call(
        lambda *refs: operand_kernel(len(squares), scale, *refs),
        out_shape=jax.ShapeDtypeStruct((rows, 3 * rank), BF16),
        compiler_params=params(),
        cost_estimate=cost(rows * rank * 10, rows * rank * 12),
        name="operand",
    )(*squares, orth)


def new_kernel(places, chained, order_ref, operand_ref, inv_ref, m_ref, *refs):
    count = len(places)
    raw_refs, refs = refs[:count], refs[count + chained :]
    out_hbm, right_refs, (out_ref, sem) = refs[0], refs[1 : 1 + count], refs[1 + count :]
    _, rows, width = out_ref.shape
    parts = sem.shape[1]
    tile = rows // parts
    inverse = three(*split(inv_ref[...]), 1)
    for raw_ref, right_ref in zip(raw_refs, right_refs):
        right = dot(inverse, three_other(*split(raw_ref[0]), 0))
        right_ref[...] = three_other(*split(right), 0)
    copies = []
    for s, right_ref in enumerate(right_refs):
        span = pl.ds(pl.multiple_of(order_ref[places[s]] * width, width), width)
        right = right_ref[...]
        for part in range(parts):
            at = pl.ds(part * tile, tile)
            out_ref[s, at] = m_ref[at, span] + dot(operand_ref[at, :], right)
            copies.append(pltpu.make_async_copy(out_ref.at[s, at], out_hbm.at[at, span], sem.at[s, part]))
            copies[-1].start()
    for copy in copies:
        copy.wait()


def new_chunks(order, places, operand, inverse, raws, momentum, before):
    rows, cols = momentum.shape
    _, rank, width = raws[0].shape
    count, parts = len(raws), 4
    outs = pl.pallas_call(
        lambda *refs: new_kernel(places, len(before), *refs),
        in_specs=[SMEM] + [VMEM] * (3 + count) + [HBM] * len(before),
        out_specs=[HBM] + [VMEM] * count,
        out_shape=[jax.ShapeDtypeStruct((rows, cols), F32)]
        + [jax.ShapeDtypeStruct((3 * rank, width), BF16)] * count,
        scratch_shapes=[pltpu.VMEM((count, rows, width), F32), pltpu.SemaphoreType.DMA((count, parts))],
        input_output_aliases={4 + count: 0} if before else {},
        compiler_params=params(),
        cost_estimate=cost(6 * count * rows * rank * width, 4 * count * rows * width),
        name="new_momentum",
    )(order, operand, inverse, in_vmem(momentum), *raws, *before)
    return [outs[0]], list(outs[1:])


def update_kernel(places, chained, order_ref, operand_ref, *refs):
    count = len(places)
    right_refs, (out_hbm, out_ref, sem) = refs[:count], refs[count + chained :]
    _, rows, width = out_ref.shape
    parts = sem.shape[1]
    tile = rows // parts
    copies = []
    for s, right_ref in enumerate(right_refs):
        span = pl.ds(pl.multiple_of(order_ref[places[s]] * width, width), width)
        right = right_ref[...]
        for part in range(parts):
            at = pl.ds(part * tile, tile)
            out_ref[s, at] = dot(operand_ref[at, :], right)
            copies.append(pltpu.make_async_copy(out_ref.at[s, at], out_hbm.at[at, span], sem.at[s, part]))
            copies[-1].start()
    for copy in copies:
        copy.wait()


def update_chunks(order, places, operand, rights, before, cols):
    rows = operand.shape[0]
    width = rights[0].shape[1]
    rank = rights[0].shape[0] // 3
    count, parts = len(rights), 4
    return [
        pl.pallas_call(
            lambda *refs: update_kernel(places, len(before), *refs),
            in_specs=[SMEM] + [VMEM] * (1 + count) + [HBM] * len(before),
            out_specs=HBM,
            out_shape=jax.ShapeDtypeStruct((rows, cols), F32),
            scratch_shapes=[pltpu.VMEM((count, rows, width), F32), pltpu.SemaphoreType.DMA((count, parts))],
            input_output_aliases={2 + count: 0} if before else {},
            compiler_params=params(),
            cost_estimate=cost(6 * count * rows * rank * width, 4 * count * rows * width),
            name="update",
        )(order, operand, *rights, *before)
    ]


PAIR = [(r, r ^ 1) for r in range(RING)]
NEAR = [(r, r ^ (2 if r % 2 == 0 else 4)) for r in range(RING)]
FAR = [(r, r ^ (4 if r % 2 == 0 else 2)) for r in range(RING)]
ACROSS = [(r, r ^ 6) for r in range(RING)]


def along(x, pairs):
    return lax.ppermute(x, "row", pairs)


def together(*values):
    return lax.optimization_barrier(values)


def local(momentum, right_factor, scale):
    rows, cols = momentum.shape
    me, at = lax.axis_index("row"), lax.axis_index("col")
    core, first, second = me % 2, me // 2 % 2, me // 4
    low_id = jnp.where(core == 0, 2 * first + second, 2 * second + first)
    pair_id = jnp.where(core == 0, 2 * second + first, 2 * first + second)
    slots = jnp.arange(RING, dtype=jnp.int32)
    order = jnp.where(slots < 4, 4 * core + (slots ^ low_id), 4 * (1 - core) + ((slots - 4) ^ pair_id))
    order = order.astype(jnp.int32)
    inner = (at > 0) & (at < LINE - 1)

    pieces = 4
    size = rows // pieces
    starts = [k * size for k in range(pieces)]
    resident, high, low = fetch(momentum, right_factor)
    arrived, crossed, lefts = [], [], []
    for k in range(pieces):
        if k == pieces - 1:
            high, arrived[0] = together(high, arrived[0])
        left = left_piece(resident, high, low, starts[k], size)
        arrived.append(left + lax.ppermute(left, "col", [(0, 1), (3, 2)]))
    for k in range(pieces):
        if k == pieces - 1:
            arrived[k], crossed[0] = together(arrived[k], crossed[0])
        crossed.append(arrived[k] + lax.ppermute(arrived[k], "col", [(1, 2), (2, 1)]))
    for held in crossed:
        lefts.append(jnp.where(inner, held, lax.ppermute(held, "col", [(1, 0), (2, 3)])))

    groups = ((7, 6), (3, 2), (5, 4), (1, 0))
    sums = []
    for k in range(pieces - 1):
        sums = raw_pieces(order, groups, lefts[k], resident, starts[k], sums, 1)

    def last(order, group):
        return raw_pieces(order, groups[group : group + 1], lefts[-1], resident, starts[-1], [sums[group]], 0)[0]

    sent_far = last(order, 0)
    order_1, sent_far = together(order, sent_far)
    halves = gram_halves(order_1, lefts[-1], sums[-1])
    order_2, halves = together(order_1, halves)
    kept_far = last(order_2, 1)
    order_3, kept_far = together(order_2, kept_far)
    sent_near, kept_near = last(order_3, 2), last(order_3, 3)

    got = along(sent_far, PAIR)
    slot_3, slot_2 = kept_far[:1] + got[:1], kept_far[1:] + got[1:]
    got_1 = along(slot_3, NEAR)
    kept = halves[0] + along(halves[1], PAIR)
    slot_2, kept = together(slot_2, kept)
    kept = kept + along(kept, NEAR) + along(kept, FAR) + along(kept, ACROSS)
    other = along(kept, PAIR)
    got_0 = along(slot_2, NEAR)
    got = along(sent_near, PAIR)
    slot_1 = kept_near[:1] + got[:1] + got_1
    got_own = along(slot_1, FAR)
    inverse, orth, operand = factor(order, kept, other, lefts)
    got_own, inverse = together(got_own, inverse)
    own = kept_near[1:] + got[1:] + got_0 + got_own

    chunk_1, chunk_2 = along(own, FAR), along(own, NEAR)
    chunks = [own, chunk_1, chunk_2, along(chunk_1, NEAR)]
    others = [along(chunk, PAIR) for chunk in chunks]

    squares = square_row(inverse, own)
    new, rights = [], []
    for slot, step in enumerate((1, 2, 4, 0)):
        if step:
            squares = squares + along(squares, [(r, r ^ step) for r in range(RING)])
        else:
            squares = [squares] + [
                lax.ppermute(squares, "col", [(c, c ^ d) for c in range(LINE)]) for d in range(1, LINE)
            ]
        raws = [chunks[slot], others[slot]]
        new, right = new_chunks(order, (slot, slot + 4), operand, inverse, raws, resident, new)
        rights += right
        if step:
            squares, new[0] = together(squares, new[0])
    operand = update_operand(squares, orth, scale)
    update = update_chunks(order, (0, 4, 1, 5), operand, rights[:4], [], cols)
    update = update_chunks(order, (2, 6, 3, 7), operand, rights[4:], update, cols)
    return new[0], update[0]


def general(momentum, right_factor, scale):
    left = lax.psum(jnp.dot(momentum, right_factor, precision=HIGHEST), "col")
    gram_part = jnp.dot(left.T, left, precision=HIGHEST)
    raw_part = jnp.dot(left.T, momentum, precision=HIGHEST)
    gram, raw = lax.psum((gram_part, raw_part), "row")
    lower = jnp.linalg.cholesky(gram)
    orth = jax.scipy.linalg.solve_triangular(lower, left.T, lower=True).T
    right = jax.scipy.linalg.solve_triangular(lower, raw, lower=True)
    squares = lax.psum(jnp.sum(right * right, axis=1, keepdims=True), "col")
    factor_q = right / jnp.sqrt(squares + 1e-06)
    new = momentum - 0.5 * jnp.dot(orth, right, precision=HIGHEST)
    return new, scale * jnp.dot(orth, factor_q, precision=HIGHEST)


def solution(mesh):
    by_hand = mesh.shape["row"] == RING and mesh.shape["col"] == LINE
    program = local if by_hand else general

    def run(momentum, right_factor):
        rows, cols = momentum.shape
        scale = math.sqrt(rows * cols / right_factor.shape[1])
        return jax.shard_map(
            lambda m, q: program(m, q, scale),
            mesh=mesh,
            in_specs=(P("row", "col"), P("col", None)),
            out_specs=(P("row", "col"), P("row", "col")),
            check_vma=False,
        )(momentum, right_factor)

    return run
```

profile of v0, /device:TPU:0, one launch (start us, length us, event | category | flops | bytes accessed | tf_op | source)
XLA Modules:
  0.0 191.2 jit_solution(11365235924481268483)
XLA Ops:
  0.6 7.1 %fetch.1 = (f32[1024,4096]{1,0:T(8,128)S(1)}, bf16[4096,256]{1,0:T(8,128)(2,1)S(1)}, bf16[4096,256]{1,0:T(8,128)(2,1)S(1)}) custom-call(f32[1024,4096]{1,0:T(8,128)} %m_hbm.1, f32[4096,256]{1,0:T(8,128)} %q_hbm.1), custom_call_target="tpu_custom_call" | custom-call | flops 1048576 | bytes 20971520 | tf_op jit(solution)/shard_map/fetch/pallas_call | solution.py:71
  7.7 1.8 left.4
  9.5 4.9 %collective-permute-start = (f32[256,256]{1,0:T(8,128)S(1)}, f32[256,256]{1,0:T(8,128)S(1)}, u32[]{:S(2)}, u32[]{:S(2)}) collective-permute-start(f32[256,256]{1,0:T(8,128)S(1)} %left.4), channel_id=1, source_target_pairs={{0,1},{3,2},{4,5},{7,6},{8,9},{11,10},{12,13},{15,14},{16,17},{19,... | collective-permute-start | bytes 786440 | tf_op jit(solution)/shard_map/ppermute | solution.py:412
  14.5 1.8 left.6
  17.6 1.8 left.7
  21.2 1.8 left.5
  23.0 4.4 %collective-permute-start.1 = (f32[256,256]{1,0:T(8,128)S(1)}, f32[256,256]{1,0:T(8,128)S(1)}, u32[]{:S(2)}, u32[]{:S(2)}) collective-permute-start(f32[256,256]{1,0:T(8,128)S(1)} %left.5), channel_id=1, source_target_pairs={{0,1},{3,2},{4,5},{7,6},{8,9},{11,10},{12,13},{15,14},{16,17},{19,... | collective-permute-start | bytes 786440 | tf_op jit(solution)/shard_map/ppermute | solution.py:412
  28.8 3.6 %collective-permute-done.8 = f32[256,256]{1,0:T(8,128)S(1)} collective-permute-done((f32[256,256]{1,0:T(8,128)S(1)}, f32[256,256]{1,0:T(8,128)S(1)}, u32[]{:S(2)}, u32[]{:S(2)}) %collective-permute-start.8) | collective-permute-done | bytes 262176 | tf_op jit(solution)/shard_map/ppermute | solution.py:412
  33.1 3.7 %collective-permute-done.1 = f32[256,256]{1,0:T(8,128)S(1)} collective-permute-done((f32[256,256]{1,0:T(8,128)S(1)}, f32[256,256]{1,0:T(8,128)S(1)}, u32[]{:S(2)}, u32[]{:S(2)}) %collective-permute-start.1) | collective-permute-done | bytes 262176 | tf_op jit(solution)/shard_map/ppermute | solution.py:412
  41.8 1.5 collective-permute-start.4
  43.2 8.2 %collective-permute-done.11 = f32[256,256]{1,0:T(8,128)S(1)} collective-permute-done((f32[256,256]{1,0:T(8,128)S(1)}, f32[256,256]{1,0:T(8,128)S(1)}, u32[]{:S(2)}, u32[]{:S(2)}) %collective-permute-start.11) | collective-permute-done | bytes 262176 | tf_op jit(solution)/shard_map/ppermute | solution.py:418
  51.5 5.8 %copy-done.1 = f32[1024,4096]{1,0:T(8,128)S(1)} copy-done((f32[1024,4096]{1,0:T(8,128)S(1)}, f32[1024,4096]{1,0:T(8,128)}, u32[]{:S(2)}) %copy-start.1) | copy-done | bytes 16777240
  57.2 2.6 %raw_right.7 = (f32[2,256,512]{2,1,0:T(8,128)S(1)}, f32[2,256,512]{2,1,0:T(8,128)S(1)}, f32[2,256,512]{2,1,0:T(8,128)S(1)}, f32[2,256,512]{2,1,0:T(8,128)S(1)}, f32[256,256]{1,0:T(8,128)S(1)}) custom-call(s32[8]{0:T(128)S(1)} %compare_select_fusion.refs_0_, f32[256,256]{1,0:T(8,128)S(1)} %broadcast_select_fusion.refs_1_.refs_3_, f32[1024,4096]{1,0:T(8,128)S(1)} %copy-done.1), custom_call_target="tpu_custom_call" | custom-call | flops 1610612736 | bytes 1048576 | tf_op jit(solution)/shard_map/raw_right/pallas_call | solution.py:133
  59.9 2.7 %collective-permute-done.10 = f32[256,256]{1,0:T(8,128)S(1)} collective-permute-done((f32[256,256]{1,0:T(8,128)S(1)}, f32[256,256]{1,0:T(8,128)S(1)}, u32[]{:S(2)}, u32[]{:S(2)}) %collective-permute-start.10) | collective-permute-done | bytes 262176 | tf_op jit(solution)/shard_map/ppermute | solution.py:418
  62.7 2.7 %raw_right.8 = (f32[2,256,512]{2,1,0:T(8,128)S(1)}, f32[2,256,512]{2,1,0:T(8,128)S(1)}, f32[2,256,512]{2,1,0:T(8,128)S(1)}, f32[2,256,512]{2,1,0:T(8,128)S(1)}, f32[256,256]{1,0:T(8,128)S(1)}) custom-call(s32[8]{0:T(128)S(1)} %compare_select_fusion.refs_0_, f32[256,256]{1,0:T(8,128)S(1)} %broadcast_select_fusion.1.refs_1_.refs_4_, ...), custom_call_target="tpu_custom_call" | custom-call | flops 1610612736 | bytes 1048576 | tf_op jit(solution)/shard_map/raw_right/pallas_call | solution.py:133
  65.4 2.7 %raw_right.9 = (f32[2,256,512]{2,1,0:T(8,128)S(1)}, f32[2,256,512]{2,1,0:T(8,128)S(1)}, f32[2,256,512]{2,1,0:T(8,128)S(1)}, f32[2,256,512]{2,1,0:T(8,128)S(1)}, f32[256,256]{1,0:T(8,128)S(1)}) custom-call(s32[8]{0:T(128)S(1)} %compare_select_fusion.refs_0_, f32[256,256]{1,0:T(8,128)S(1)} %broadcast_select_fusion.2.refs_1_.refs_5_, ...), custom_call_target="tpu_custom_call" | custom-call | flops 1610612736 | bytes 1048576 | tf_op jit(solution)/shard_map/raw_right/pallas_call | solution.py:133
  74.8 1.6 collective-permute-start.19
  76.9 2.5 %collective-permute-start.16 = (f32[128,256]{1,0:T(8,128)S(1)}, f32[128,256]{1,0:T(8,128)S(1)}, u32[]{:S(2)}, u32[]{:S(2)}) collective-permute-start(f32[128,256]{1,0:T(8,128)S(1)} %bitcast_add_fusion), channel_id=1, source_target_pairs={{0,24},{4,28},{8,16},{12,20},{16,8},{20,12},{24,0},{28,4},{1,25},{... | collective-permute-start | bytes 393224 | tf_op jit(solution)/shard_map/ppermute | solution.py:385
  81.6 7.6 %collective-permute-done.16 = f32[128,256]{1,0:T(8,128)S(1)} collective-permute-done((f32[128,256]{1,0:T(8,128)S(1)}, f32[128,256]{1,0:T(8,128)S(1)}, u32[]{:S(2)}, u32[]{:S(2)}) %collective-permute-start.16) | collective-permute-done | bytes 131104 | tf_op jit(solution)/shard_map/ppermute | solution.py:385
  90.0 1.5 collective-permute-start.20
  91.6 1.5 collective-permute-start.21
  93.0 44.0 %factor.1 = (f32[256,256]{1,0:T(8,128)S(1)}, f32[1024,256]{1,0:T(8,128)S(1)}, bf16[1024,768]{1,0:T(8,128)(2,1)S(1)}) custom-call(s32[8]{0:T(128)S(1)} %compare_select_fusion.refs_0_, f32[128,256]{1,0:T(8,128)S(1)} %add_add_fusion.refs_1_, f32[128,256]{1,0:T(8,128)S(1)} %collective-permute-done.17.refs_2_, ...), custom_call_target="tpu_custom_call" | custom-call | flops 5000000000 | bytes 4194304 | tf_op jit(solution)/shard_map/factor/pallas_call | solution.py:240
  138.4 12.9 %collective-permute-done.22.refs_4_ = f32[1,256,512]{2,1,0:T(8,128)S(1)} collective-permute-done((f32[1,256,512]{2,1,0:T(8,128)S(1)}, f32[1,256,512]{2,1,0:T(8,128)S(1)}, u32[]{:S(2)}, u32[]{:S(2)}) %collective-permute-start.22) | collective-permute-done | bytes 524320 | tf_op jit(solution)/shard_map/ppermute | solution.py:385
  155.6 3.7 %new_momentum.4 = (f32[1024,4096]{1,0:T(8,128)}, bf16[768,512]{1,0:T(8,128)(2,1)S(1)}, bf16[768,512]{1,0:T(8,128)(2,1)S(1)}) custom-call(s32[8]{0:T(128)S(1)} %compare_select_fusion.refs_0_, bf16[1024,768]{1,0:T(8,128)(2,1)S(1)} %get-tuple-element.81.refs_1_, f32[256,256]{1,0:T(8,128)S(1)} %get-tuple-element.86.inv_ref.refs_2_, f32[1024,4096]{1,0:T(8,128)S(1)} %bitcast.5, ...), custom_call_target="tpu_custom_call" | custom-call | flops 1610612736 | bytes 4194304 | tf_op jit(solution)/shard_map/new_momentum/pallas_call | solution.py:324
  160.2 2.8 %collective-permute-done.27 = f32[8,256]{1,0:T(8,128)S(1)} collective-permute-done((f32[8,256]{1,0:T(8,128)S(1)}, f32[8,256]{1,0:T(8,128)S(1)}, u32[]{:S(2)}, u32[]{:S(2)}) %collective-permute-start.27) | collective-permute-done | bytes 8224 | tf_op jit(solution)/shard_map/ppermute | solution.py:385
  163.0 3.7 %new_momentum.5 = (f32[1024,4096]{1,0:T(8,128)}, bf16[768,512]{1,0:T(8,128)(2,1)S(1)}, bf16[768,512]{1,0:T(8,128)(2,1)S(1)}) custom-call(s32[8]{0:T(128)S(1)} %compare_select_fusion.refs_0_, bf16[1024,768]{1,0:T(8,128)(2,1)S(1)} %get-tuple-element.81.refs_1_, f32[256,256]{1,0:T(8,128)S(1)} %get-tuple-element.86.inv_ref.refs_2_, ...), custom_call_target="tpu_custom_call", output_to_operand_aliasing={{0}: (6, {})} | custom-call | flops 1610612736 | bytes 4194304 | tf_op jit(solution)/shard_map/new_momentum/pallas_call | solution.py:324
  167.3 3.7 %new_momentum.6 = (f32[1024,4096]{1,0:T(8,128)}, bf16[768,512]{1,0:T(8,128)(2,1)S(1)}, bf16[768,512]{1,0:T(8,128)(2,1)S(1)}) custom-call(s32[8]{0:T(128)S(1)} %compare_select_fusion.refs_0_, bf16[1024,768]{1,0:T(8,128)(2,1)S(1)} %get-tuple-element.81.refs_1_, f32[256,256]{1,0:T(8,128)S(1)} %get-tuple-element.86.inv_ref.refs_2_, ...), custom_call_target="tpu_custom_call", output_to_operand_aliasing={{0}: (6, {})} | custom-call | flops 1610612736 | bytes 4194304 | tf_op jit(solution)/shard_map/new_momentum/pallas_call | solution.py:324
  171.0 1.4 collective-permute-start.34
  172.4 3.1 %collective-permute-start.32 = (f32[8,256]{1,0:T(8,128)S(1)}, f32[8,256]{1,0:T(8,128)S(1)}, u32[]{:S(2)}, u32[]{:S(2)}) collective-permute-start(f32[8,256]{1,0:T(8,128)S(1)} %add.125.refs_0_), channel_id=1, source_target_pairs={{0,1},{1,0},{2,3},{3,2},{4,5},{5,4},{6,7},{7,6},{8,9},{9,8},{10,11... | collective-permute-start | bytes 24584 | tf_op jit(solution)/shard_map/ppermute | solution.py:462
  177.3 4.9 %update.2.refs_6_ = f32[1024,4096]{1,0:T(8,128)} custom-call(s32[8]{0:T(128)S(1)} %compare_select_fusion.refs_0_, bf16[1024,768]{1,0:T(8,128)(2,1)S(1)} %operand.1.refs_1_, bf16[768,512]{1,0:T(8,128)(2,1)S(1)} %get-tuple-element.104.refs_2_, bf16[768,512]{1,0:T(8,128)(2,1)S(1)} %get-tuple-element.105.refs_3_, ...), custom_call_target="tpu_custom_call" | custom-call | flops 3221225472 | bytes 8388608 | tf_op jit(solution)/shard_map/update/pallas_call | solution.py:364
  182.2 3.9 %new_momentum.7 = (f32[1024,4096]{1,0:T(8,128)}, bf16[768,512]{1,0:T(8,128)(2,1)S(1)}, bf16[768,512]{1,0:T(8,128)(2,1)S(1)}) custom-call(s32[8]{0:T(128)S(1)} %compare_select_fusion.refs_0_, bf16[1024,768]{1,0:T(8,128)(2,1)S(1)} %get-tuple-element.81.refs_1_, f32[256,256]{1,0:T(8,128)S(1)} %get-tuple-element.86.inv_ref.refs_2_, ...), custom_call_target="tpu_custom_call", output_to_operand_aliasing={{0}: (6, {})} | custom-call | flops 1610612736 | bytes 4194304 | tf_op jit(solution)/shard_map/new_momentum/pallas_call | solution.py:324
  186.1 4.9 %update.3 = f32[1024,4096]{1,0:T(8,128)} custom-call(s32[8]{0:T(128)S(1)} %compare_select_fusion.refs_0_, bf16[1024,768]{1,0:T(8,128)(2,1)S(1)} %operand.1.refs_1_, bf16[768,512]{1,0:T(8,128)(2,1)S(1)} %get-tuple-element.100.refs_2_, bf16[768,512]{1,0:T(8,128)(2,1)S(1)} %get-tuple-element.101.refs_3_, ...), custom_call_target="tpu_custom_call", output_to_operand_aliasing={{}: (6, {})} | custom-call | flops 3221225472 | bytes 8388608 | tf_op jit(solution)/shard_map/update/pallas_call | solution.py:364
  (95 shorter events, 29.2 us)
Async XLA Ops:
  9.5 11.6 %collective-permute-start = (f32[256,256]{1,0:T(8,128)S(1)}, f32[256,256]{1,0:T(8,128)S(1)}, u32[]{:S(2)}, u32[]{:S(2)}) collective-permute-start(f32[256,256]{1,0:T(8,128)S(1)} %left.4), channel_id=1, source_target_pairs={{0,1},{3,2},{4,5},{7,6},{8,9},{11,10},{12,13},{15,14},{16,17},{19,... | collective-permute-start | bytes 786440 | tf_op jit(solution)/shard_map/ppermute | solution.py:412
  16.3 11.8 %collective-permute-start.5 = (f32[256,256]{1,0:T(8,128)S(1)}, f32[256,256]{1,0:T(8,128)S(1)}, u32[]{:S(2)}, u32[]{:S(2)}) collective-permute-start(f32[256,256]{1,0:T(8,128)S(1)} %left.6), channel_id=1, source_target_pairs={{0,1},{3,2},{4,5},{7,6},{8,9},{11,10},{12,13},{15,14},{16,17},{19,... | collective-permute-start | bytes 786440 | tf_op jit(solution)/shard_map/ppermute | solution.py:412
  19.4 13.0 %collective-permute-start.8 = (f32[256,256]{1,0:T(8,128)S(1)}, f32[256,256]{1,0:T(8,128)S(1)}, u32[]{:S(2)}, u32[]{:S(2)}) collective-permute-start(f32[256,256]{1,0:T(8,128)S(1)} %left.7), channel_id=1, source_target_pairs={{0,1},{3,2},{4,5},{7,6},{8,9},{11,10},{12,13},{15,14},{16,17},{19,... | collective-permute-start | bytes 786440 | tf_op jit(solution)/shard_map/ppermute | solution.py:412
  23.0 13.9 %collective-permute-start.1 = (f32[256,256]{1,0:T(8,128)S(1)}, f32[256,256]{1,0:T(8,128)S(1)}, u32[]{:S(2)}, u32[]{:S(2)}) collective-permute-start(f32[256,256]{1,0:T(8,128)S(1)} %left.5), channel_id=1, source_target_pairs={{0,1},{3,2},{4,5},{7,6},{8,9},{11,10},{12,13},{15,14},{16,17},{19,... | collective-permute-start | bytes 786440 | tf_op jit(solution)/shard_map/ppermute | solution.py:412
  27.4 9.5 %collective-permute-start.2 = (f32[256,256]{1,0:T(8,128)S(1)}, f32[256,256]{1,0:T(8,128)S(1)}, u32[]{:S(2)}, u32[]{:S(2)}) collective-permute-start(f32[256,256]{1,0:T(8,128)S(1)} %add.104), channel_id=1, source_target_pairs={{1,2},{2,1},{5,6},{6,5},{9,10},{10,9},{13,14},{14,13},{17,18},{18,... | collective-permute-start | bytes 786440 | tf_op jit(solution)/shard_map/ppermute | solution.py:416
  28.1 10.9 %collective-permute-start.6 = (f32[256,256]{1,0:T(8,128)S(1)}, f32[256,256]{1,0:T(8,128)S(1)}, u32[]{:S(2)}, u32[]{:S(2)}) collective-permute-start(f32[256,256]{1,0:T(8,128)S(1)} %add.108), channel_id=1, source_target_pairs={{1,2},{2,1},{5,6},{6,5},{9,10},{10,9},{13,14},{14,13},{17,18},{18,... | collective-permute-start | bytes 786440 | tf_op jit(solution)/shard_map/ppermute | solution.py:416
  32.4 7.9 %collective-permute-start.9 = (f32[256,256]{1,0:T(8,128)S(1)}, f32[256,256]{1,0:T(8,128)S(1)}, u32[]{:S(2)}, u32[]{:S(2)}) collective-permute-start(f32[256,256]{1,0:T(8,128)S(1)} %add.110), channel_id=1, source_target_pairs={{1,2},{2,1},{5,6},{6,5},{9,10},{10,9},{13,14},{14,13},{17,18},{18,... | collective-permute-start | bytes 786440 | tf_op jit(solution)/shard_map/ppermute | solution.py:416
  36.9 4.8 %collective-permute-start.3 = (f32[256,256]{1,0:T(8,128)S(1)}, f32[256,256]{1,0:T(8,128)S(1)}, u32[]{:S(2)}, u32[]{:S(2)}) collective-permute-start(f32[256,256]{1,0:T(8,128)S(1)} %add.105), channel_id=1, source_target_pairs={{1,2},{2,1},{5,6},{6,5},{9,10},{10,9},{13,14},{14,13},{17,18},{18,... | collective-permute-start | bytes 786440 | tf_op jit(solution)/shard_map/ppermute | solution.py:416
  37.6 13.8 %collective-permute-start.11 = (f32[256,256]{1,0:T(8,128)S(1)}, f32[256,256]{1,0:T(8,128)S(1)}, u32[]{:S(2)}, u32[]{:S(2)}) collective-permute-start(f32[256,256]{1,0:T(8,128)S(1)} %add.106), channel_id=1, source_target_pairs={{1,0},{2,3},{5,4},{6,7},{9,8},{10,11},{13,12},{14,15},{17,16},{18,... | collective-permute-start | bytes 786440 | tf_op jit(solution)/shard_map/ppermute | solution.py:418
  39.0 20.8 %collective-permute-start.7 = (f32[256,256]{1,0:T(8,128)S(1)}, f32[256,256]{1,0:T(8,128)S(1)}, u32[]{:S(2)}, u32[]{:S(2)}) collective-permute-start(f32[256,256]{1,0:T(8,128)S(1)} %add.109), channel_id=1, source_target_pairs={{1,0},{2,3},{5,4},{6,7},{9,8},{10,11},{13,12},{14,15},{17,16},{18,... | collective-permute-start | bytes 786440 | tf_op jit(solution)/shard_map/ppermute | solution.py:418
  40.4 22.2 %collective-permute-start.10 = (f32[256,256]{1,0:T(8,128)S(1)}, f32[256,256]{1,0:T(8,128)S(1)}, u32[]{:S(2)}, u32[]{:S(2)}) collective-permute-start(f32[256,256]{1,0:T(8,128)S(1)} %add.111), channel_id=1, source_target_pairs={{1,0},{2,3},{5,4},{6,7},{9,8},{10,11},{13,12},{14,15},{17,16},{18,... | collective-permute-start | bytes 786440 | tf_op jit(solution)/shard_map/ppermute | solution.py:418
  41.8 26.4 %collective-permute-start.4 = (f32[256,256]{1,0:T(8,128)S(1)}, f32[256,256]{1,0:T(8,128)S(1)}, u32[]{:S(2)}, u32[]{:S(2)}) collective-permute-start(f32[256,256]{1,0:T(8,128)S(1)} %add.107), channel_id=1, source_target_pairs={{1,0},{2,3},{5,4},{6,7},{9,8},{10,11},{13,12},{14,15},{17,16},{18,... | collective-permute-start | bytes 786440 | tf_op jit(solution)/shard_map/ppermute | solution.py:418
  69.4 5.2 %collective-permute-start.12 = (f32[2,256,512]{2,1,0:T(8,128)S(1)}, f32[2,256,512]{2,1,0:T(8,128)S(1)}, u32[]{:S(2)}, u32[]{:S(2)}) collective-permute-start(f32[2,256,512]{2,1,0:T(8,128)S(1)} %raw_right.10), channel_id=1, source_target_pairs={{0,4},{4,0},{8,12},{12,8},{16,20},{20,16},{24,28},{28,24},{1,5},{5... | collective-permute-start | bytes 3145736 | tf_op jit(solution)/shard_map/ppermute | solution.py:385
  73.9 15.9 %collective-permute-start.18 = (f32[2,256,512]{2,1,0:T(8,128)S(1)}, f32[2,256,512]{2,1,0:T(8,128)S(1)}, u32[]{:S(2)}, u32[]{:S(2)}) collective-permute-start(f32[2,256,512]{2,1,0:T(8,128)S(1)} %raw_right.13), channel_id=1, source_target_pairs={{0,4},{4,0},{8,12},{12,8},{16,20},{20,16},{24,28},{28,24},{1,5},{5... | collective-permute-start | bytes 3145736 | tf_op jit(solution)/shard_map/ppermute | solution.py:385
  74.8 15.0 %collective-permute-start.19 = (f32[1,256,512]{2,1,0:T(8,128)S(1)}, f32[1,256,512]{2,1,0:T(8,128)S(1)}, u32[]{:S(2)}, u32[]{:S(2)}) collective-permute-start(f32[1,256,512]{2,1,0:T(8,128)S(1)} %get-tuple-element.108), channel_id=1, source_target_pairs={{0,8},{4,20},{8,0},{12,28},{16,24},{20,4},{24,16},{28,12},{1,9},{5... | collective-permute-start | bytes 1572872 | tf_op jit(solution)/shard_map/ppermute | solution.py:385
  76.9 12.4 %collective-permute-start.16 = (f32[128,256]{1,0:T(8,128)S(1)}, f32[128,256]{1,0:T(8,128)S(1)}, u32[]{:S(2)}, u32[]{:S(2)}) collective-permute-start(f32[128,256]{1,0:T(8,128)S(1)} %bitcast_add_fusion), channel_id=1, source_target_pairs={{0,24},{4,28},{8,16},{12,20},{16,8},{20,12},{24,0},{28,4},{1,25},{... | collective-permute-start | bytes 393224 | tf_op jit(solution)/shard_map/ppermute | solution.py:385
  79.4 9.8 %collective-permute-start.15 = (f32[128,256]{1,0:T(8,128)S(1)}, f32[128,256]{1,0:T(8,128)S(1)}, u32[]{:S(2)}, u32[]{:S(2)}) collective-permute-start(f32[128,256]{1,0:T(8,128)S(1)} %bitcast_add_fusion), channel_id=1, source_target_pairs={{0,16},{4,12},{8,24},{12,4},{16,0},{20,28},{24,8},{28,20},{1,17},{... | collective-permute-start | bytes 393224 | tf_op jit(solution)/shard_map/ppermute | solution.py:385
  79.9 9.8 %collective-permute-start.14 = (f32[128,256]{1,0:T(8,128)S(1)}, f32[128,256]{1,0:T(8,128)S(1)}, u32[]{:S(2)}, u32[]{:S(2)}) collective-permute-start(f32[128,256]{1,0:T(8,128)S(1)} %bitcast_add_fusion), channel_id=1, source_target_pairs={{0,8},{4,20},{8,0},{12,28},{16,24},{20,4},{24,16},{28,12},{1,9},{5... | collective-permute-start | bytes 393224 | tf_op jit(solution)/shard_map/ppermute | solution.py:385
  90.0 47.0 %collective-permute-start.20 = (f32[1,256,512]{2,1,0:T(8,128)S(1)}, f32[1,256,512]{2,1,0:T(8,128)S(1)}, u32[]{:S(2)}, u32[]{:S(2)}) collective-permute-start(f32[1,256,512]{2,1,0:T(8,128)S(1)} %fusion.2), channel_id=1, source_target_pairs={{0,16},{4,12},{8,24},{12,4},{16,0},{20,28},{24,8},{28,20},{1,17},{... | collective-permute-start | bytes 1572872 | tf_op jit(solution)/shard_map/ppermute | solution.py:385
  91.6 45.5 %collective-permute-start.21 = (f32[1,256,512]{2,1,0:T(8,128)S(1)}, f32[1,256,512]{2,1,0:T(8,128)S(1)}, u32[]{:S(2)}, u32[]{:S(2)}) collective-permute-start(f32[1,256,512]{2,1,0:T(8,128)S(1)} %get-tuple-element.87), channel_id=1, source_target_pairs={{0,8},{4,20},{8,0},{12,28},{16,24},{20,4},{24,16},{28,12},{1,9},{5... | collective-permute-start | bytes 1572872 | tf_op jit(solution)/shard_map/ppermute | solution.py:385
  137.3 14.1 %collective-permute-start.22 = (f32[1,256,512]{2,1,0:T(8,128)S(1)}, f32[1,256,512]{2,1,0:T(8,128)S(1)}, u32[]{:S(2)}, u32[]{:S(2)}) collective-permute-start(f32[1,256,512]{2,1,0:T(8,128)S(1)} %fusion.1.raw_ref.refs_4_), channel_id=1, source_target_pairs={{0,16},{4,12},{8,24},{12,4},{16,0},{20,28},{24,8},{28,20},{1,17},{... | collective-permute-start | bytes 1572872 | tf_op jit(solution)/shard_map/ppermute | solution.py:385
  137.9 14.6 %collective-permute-start.30 = (f32[1,256,512]{2,1,0:T(8,128)S(1)}, f32[1,256,512]{2,1,0:T(8,128)S(1)}, u32[]{:S(2)}, u32[]{:S(2)}) collective-permute-start(f32[1,256,512]{2,1,0:T(8,128)S(1)} %fusion.1.raw_ref.refs_4_), channel_id=1, source_target_pairs={{0,8},{4,20},{8,0},{12,28},{16,24},{20,4},{24,16},{28,12},{1,9},{5... | collective-permute-start | bytes 1572872 | tf_op jit(solution)/shard_map/ppermute | solution.py:385
  138.4 17.2 %collective-permute-start.26 = (f32[1,256,512]{2,1,0:T(8,128)S(1)}, f32[1,256,512]{2,1,0:T(8,128)S(1)}, u32[]{:S(2)}, u32[]{:S(2)}) collective-permute-start(f32[1,256,512]{2,1,0:T(8,128)S(1)} %fusion.1.raw_ref.refs_4_), channel_id=1, source_target_pairs={{0,4},{4,0},{8,12},{12,8},{16,20},{20,16},{24,28},{28,24},{1,5},{5... | collective-permute-start | bytes 1572872 | tf_op jit(solution)/shard_map/ppermute | solution.py:385
  151.4 11.6 %collective-permute-start.23 = (f32[1,256,512]{2,1,0:T(8,128)S(1)}, f32[1,256,512]{2,1,0:T(8,128)S(1)}, u32[]{:S(2)}, u32[]{:S(2)}) collective-permute-start(f32[1,256,512]{2,1,0:T(8,128)S(1)} %collective-permute-done.22.refs_4_), channel_id=1, source_target_pairs={{0,8},{4,20},{8,0},{12,28},{16,24},{20,4},{24,16},{28,12},{1,9},{5... | collective-permute-start | bytes 1572872 | tf_op jit(solution)/shard_map/ppermute | solution.py:385
  152.5 10.5 %collective-permute-start.28 = (f32[1,256,512]{2,1,0:T(8,128)S(1)}, f32[1,256,512]{2,1,0:T(8,128)S(1)}, u32[]{:S(2)}, u32[]{:S(2)}) collective-permute-start(f32[1,256,512]{2,1,0:T(8,128)S(1)} %collective-permute-done.22.refs_4_), channel_id=1, source_target_pairs={{0,4},{4,0},{8,12},{12,8},{16,20},{20,16},{24,28},{28,24},{1,5},{5... | collective-permute-start | bytes 1572872 | tf_op jit(solution)/shard_map/ppermute | solution.py:385
  152.5 14.8 %collective-permute-start.31 = (f32[1,256,512]{2,1,0:T(8,128)S(1)}, f32[1,256,512]{2,1,0:T(8,128)S(1)}, u32[]{:S(2)}, u32[]{:S(2)}) collective-permute-start(f32[1,256,512]{2,1,0:T(8,128)S(1)} %collective-permute-done.30.refs_4_), channel_id=1, source_target_pairs={{0,4},{4,0},{8,12},{12,8},{16,20},{20,16},{24,28},{28,24},{1,5},{5... | collective-permute-start | bytes 1572872 | tf_op jit(solution)/shard_map/ppermute | solution.py:385
  159.3 3.7 %collective-permute-start.27 = (f32[8,256]{1,0:T(8,128)S(1)}, f32[8,256]{1,0:T(8,128)S(1)}, u32[]{:S(2)}, u32[]{:S(2)}) collective-permute-start(f32[8,256]{1,0:T(8,128)S(1)} %add.123), channel_id=1, source_target_pairs={{0,8},{4,12},{8,0},{12,4},{16,24},{20,28},{24,16},{28,20},{1,9},{5... | collective-permute-start | bytes 24584 | tf_op jit(solution)/shard_map/ppermute | solution.py:385
  163.0 19.2 %collective-permute-start.24 = (f32[1,256,512]{2,1,0:T(8,128)S(1)}, f32[1,256,512]{2,1,0:T(8,128)S(1)}, u32[]{:S(2)}, u32[]{:S(2)}) collective-permute-start(f32[1,256,512]{2,1,0:T(8,128)S(1)} %collective-permute-done.23.refs_4_), channel_id=1, source_target_pairs={{0,4},{4,0},{8,12},{12,8},{16,20},{20,16},{24,28},{28,24},{1,5},{5... | collective-permute-start | bytes 1572872 | tf_op jit(solution)/shard_map/ppermute | solution.py:385
  166.7 4.3 %collective-permute-start.29 = (f32[8,256]{1,0:T(8,128)S(1)}, f32[8,256]{1,0:T(8,128)S(1)}, u32[]{:S(2)}, u32[]{:S(2)}) collective-permute-start(f32[8,256]{1,0:T(8,128)S(1)} %add.124), channel_id=1, source_target_pairs={{0,16},{4,20},{8,24},{12,28},{16,0},{20,4},{24,8},{28,12},{1,17},{... | collective-permute-start | bytes 24584 | tf_op jit(solution)/shard_map/ppermute | solution.py:385
  171.0 5.5 %collective-permute-start.34 = (f32[8,256]{1,0:T(8,128)S(1)}, f32[8,256]{1,0:T(8,128)S(1)}, u32[]{:S(2)}, u32[]{:S(2)}) collective-permute-start(f32[8,256]{1,0:T(8,128)S(1)} %add.125.refs_0_), channel_id=1, source_target_pairs={{0,3},{1,2},{2,1},{3,0},{4,7},{5,6},{6,5},{7,4},{8,11},{9,10},{10,... | collective-permute-start | bytes 24584 | tf_op jit(solution)/shard_map/ppermute | solution.py:462
  172.4 4.5 %collective-permute-start.33 = (f32[8,256]{1,0:T(8,128)S(1)}, f32[8,256]{1,0:T(8,128)S(1)}, u32[]{:S(2)}, u32[]{:S(2)}) collective-permute-start(f32[8,256]{1,0:T(8,128)S(1)} %add.125.refs_0_), channel_id=1, source_target_pairs={{0,2},{1,3},{2,0},{3,1},{4,6},{5,7},{6,4},{7,5},{8,10},{9,11},{10,... | collective-permute-start | bytes 24584 | tf_op jit(solution)/shard_map/ppermute | solution.py:462
  172.4 4.7 %collective-permute-start.32 = (f32[8,256]{1,0:T(8,128)S(1)}, f32[8,256]{1,0:T(8,128)S(1)}, u32[]{:S(2)}, u32[]{:S(2)}) collective-permute-start(f32[8,256]{1,0:T(8,128)S(1)} %add.125.refs_0_), channel_id=1, source_target_pairs={{0,1},{1,0},{2,3},{3,2},{4,5},{5,4},{6,7},{7,6},{8,9},{9,8},{10,11... | collective-permute-start | bytes 24584 | tf_op jit(solution)/shard_map/ppermute | solution.py:462
  (9 other events, 45.1 us)
where the time goes:
time: 192 us; the launch traced here: 191 us
  Pallas kernels  98.3 us (51%)
  waiting for transfers between devices  45.8 us (24%)
  starting transfers between devices  37.8 us (20%)
  local copies, waits for them, and re-layouts  6.76 us (4%)
    pallas_call x1, Pallas kernels, factor(): pl.pallas_call(lambda *refs: factor_kernel(len(lefts), order.shape[0] //...  44 us
    ppermute x20, waiting for transfers between devices, along(): return lax.ppermute(x, 'row', pairs)  25.5 us
    pallas_call x4, Pallas kernels, new_chunks(): pl.pallas_call(lambda *refs: new_kernel(places, len(before), *refs), in_s...  14.9 us
    ppermute x20, starting transfers between devices, along(): return lax.ppermute(x, 'row', pairs)  13.3 us
    pallas_call x7, Pallas kernels, raw_pieces(): pl.pallas_call(lambda *refs: raw_kernel(at, groups, bool(before), with_gr...  12.9 us
    ppermute x4, starting transfers between devices, local(): arrived.append(left + lax.ppermute(left, 'col', [(0, 1), (3, 2)]))  12 us
    ppermute x4, waiting for transfers between devices, local(): lax.ppermute(held, 'col', [(1, 0), (2, 3)])  10.9 us
    pallas_call x2, Pallas kernels, update_chunks(): pl.pallas_call(lambda *refs: update_kernel(places, len(before), *refs), i...  9.8 us
  transfers between devices with their start and end apart: 35, of which 14 were waited for; matrix products, arithmetic and copies ran while one was open for 0% of the time, Pallas kernels for 42%

commit v1 on v0

--- a/solution.py
+++ b/solution.py
@@ -126,7 +126,7 @@
 
 def raw_pieces(order, groups, left, momentum, at, before, with_gram):
     rows, rank = left.shape
-    width = momentum.shape[1] // order.shape[0]
+    width = momentum.shape[1] // RING
     chunks = sum(len(places) for places in groups)
     shapes = [jax.ShapeDtypeStruct((len(places), rank, width), F32) for places in groups]
     shapes += [jax.ShapeDtypeStruct((rank, rank), F32)] * with_gram
@@ -153,7 +153,7 @@
 def gram_halves(order, left, before):
     rank = left.shape[1]
     return pl.pallas_call(
-        lambda *refs: gram_kernel(order.shape[0] // 2, *refs),
+        lambda *refs: gram_kernel(RING // 2, *refs),
         in_specs=[SMEM, VMEM, VMEM],
         out_specs=VMEM,
         out_shape=jax.ShapeDtypeStruct((2, rank // 2, rank), F32),
@@ -238,7 +238,7 @@
     rank = kept.shape[1]
     rows = sum(x.shape[0] for x in lefts)
     return pl.pallas_call(
-        lambda *refs: factor_kernel(len(lefts), order.shape[0] // 2, *refs),
+        lambda *refs: factor_kernel(len(lefts), RING // 2, *refs),
         in_specs=[SMEM] + [VMEM] * (2 + len(lefts)),
         out_specs=[VMEM] * 3,
         out_shape=[
@@ -248,7 +248,7 @@
         ],
         scratch_shapes=[pltpu.VMEM((rank, rank), F32), pltpu.VMEM((rank, 2 * rank), F32)],
         compiler_params=params(),
-        cost_estimate=cost(5 * 10**9, 2**22),
+        cost_estimate=cost(1, 1),
         name="factor",
     )(order, kept, sent, *lefts)
 
@@ -375,6 +375,59 @@
     ]
 
 
+def add_kernel(*refs):
+    refs[-1][...] = sum((ref[...] for ref in refs[1:-1]), refs[0][...])
+
+
+def add(*values):
+    return pl.pallas_call(
+        add_kernel,
+        in_specs=[VMEM] * len(values),
+        out_specs=VMEM,
+        out_shape=jax.ShapeDtypeStruct(values[0].shape, F32),
+        compiler_params=params(),
+        cost_estimate=cost(values[0].size, 1),
+        name="add",
+    )(*values)
+
+
+def half_kernel(*refs):
+    *value_refs, second_ref, first_ref = refs
+    half = first_ref.shape[0]
+    second_ref[...] = sum((ref[half:] for ref in value_refs[1:]), value_refs[0][half:])
+    first_ref[...] = sum((ref[:half] for ref in value_refs[1:]), value_refs[0][:half])
+
+
+def add_halves(*values):
+    half = values[0].shape[0] // 2
+    shape = jax.ShapeDtypeStruct((half, *values[0].shape[1:]), F32)
+    return pl.pallas_call(
+        half_kernel,
+        in_specs=[VMEM] * len(values),
+        out_specs=[VMEM] * 2,
+        out_shape=[shape] * 2,
+        compiler_params=params(),
+        cost_estimate=cost(values[0].size, 1),
+        name="add_halves",
+    )(*values)
+
+
+def choose_kernel(order_ref, a_ref, b_ref, out_ref):
+    out_ref[...] = jnp.where(order_ref[RING] > 0, a_ref[...], b_ref[...])
+
+
+def choose(order, a, b):
+    return pl.pallas_call(
+        choose_kernel,
+        in_specs=[SMEM, VMEM, VMEM],
+        out_specs=VMEM,
+        out_shape=jax.ShapeDtypeStruct(a.shape, F32),
+        compiler_params=params(),
+        cost_estimate=cost(a.size, 1),
+        name="choose",
+    )(order, a, b)
+
+
 PAIR = [(r, r ^ 1) for r in range(RING)]
 NEAR = [(r, r ^ (2 if r % 2 == 0 else 4)) for r in range(RING)]
 FAR = [(r, r ^ (4 if r % 2 == 0 else 2)) for r in range(RING)]
@@ -395,80 +448,89 @@
     core, first, second = me % 2, me // 2 % 2, me // 4
     low_id = jnp.where(core == 0, 2 * first + second, 2 * second + first)
     pair_id = jnp.where(core == 0, 2 * second + first, 2 * first + second)
-    slots = jnp.arange(RING, dtype=jnp.int32)
+    slots = jnp.arange(RING + 1, dtype=jnp.int32)
     order = jnp.where(slots < 4, 4 * core + (slots ^ low_id), 4 * (1 - core) + ((slots - 4) ^ pair_id))
-    order = order.astype(jnp.int32)
-    inner = (at > 0) & (at < LINE - 1)
-
-    pieces = 4
-    size = rows // pieces
-    starts = [k * size for k in range(pieces)]
+    order = jnp.where(slots < RING, order, (at > 0) & (at < LINE - 1)).astype(jnp.int32)
+    order, right_factor = together(order, right_factor)
+
+    size = rows // 4
     resident, high, low = fetch(momentum, right_factor)
-    arrived, crossed, lefts = [], [], []
-    for k in range(pieces):
-        if k == pieces - 1:
-            high, arrived[0] = together(high, arrived[0])
-        left = left_piece(resident, high, low, starts[k], size)
-        arrived.append(left + lax.ppermute(left, "col", [(0, 1), (3, 2)]))
-    for k in range(pieces):
-        if k == pieces - 1:
-            arrived[k], crossed[0] = together(arrived[k], crossed[0])
-        crossed.append(arrived[k] + lax.ppermute(arrived[k], "col", [(1, 2), (2, 1)]))
-    for held in crossed:
-        lefts.append(jnp.where(inner, held, lax.ppermute(held, "col", [(1, 0), (2, 3)])))
+
+    def left_of(k, high):
+        return left_piece(resident, high, low, k * size, size)
+
+    def inward(x):
+        return lax.ppermute(x, "col", [(0, 1), (3, 2)])
+
+    def across(x):
+        return lax.ppermute(x, "col", [(1, 2), (2, 1)])
+
+    def outward(x):
+        return lax.ppermute(x, "col", [(1, 0), (2, 3)])
+
+    parts = [left_of(k, high) for k in range(3)]
+    held = [add(part, inward(part)) for part in parts]
+    high, held[0] = together(high, held[0])
+    part = left_of(3, high)
+    held.append(add(part, inward(part)))
+    crossed = [add(x, across(x)) for x in held[:3]]
+    held[3], crossed[0] = together(held[3], crossed[0])
+    crossed.append(add(held[3], across(held[3])))
+    lefts = [choose(order, x, outward(x)) for x in crossed]
 
     groups = ((7, 6), (3, 2), (5, 4), (1, 0))
     sums = []
-    for k in range(pieces - 1):
-        sums = raw_pieces(order, groups, lefts[k], resident, starts[k], sums, 1)
-
-    def last(order, group):
-        return raw_pieces(order, groups[group : group + 1], lefts[-1], resident, starts[-1], [sums[group]], 0)[0]
+    for k in range(3):
+        sums = raw_pieces(order, groups, lefts[k], resident, k * size, sums, 1)
+    *sums, gram = sums
+
+    def last(order, g):
+        return raw_pieces(order, groups[g : g + 1], lefts[3], resident, 3 * size, [sums[g]], 0)[0]
 
     sent_far = last(order, 0)
     order_1, sent_far = together(order, sent_far)
-    halves = gram_halves(order_1, lefts[-1], sums[-1])
+    halves = gram_halves(order_1, lefts[3], gram)
     order_2, halves = together(order_1, halves)
     kept_far = last(order_2, 1)
-    order_3, kept_far = together(order_2, kept_far)
+    kept_far = add(kept_far, along(sent_far, PAIR))
+    got_near = along(kept_far, NEAR)
+    kept = add(halves[0], along(halves[1], PAIR))
+    order_3, kept_far, kept = together(order_2, kept_far, kept)
     sent_near, kept_near = last(order_3, 2), last(order_3, 3)
-
-    got = along(sent_far, PAIR)
-    slot_3, slot_2 = kept_far[:1] + got[:1], kept_far[1:] + got[1:]
-    got_1 = along(slot_3, NEAR)
-    kept = halves[0] + along(halves[1], PAIR)
-    slot_2, kept = together(slot_2, kept)
-    kept = kept + along(kept, NEAR) + along(kept, FAR) + along(kept, ACROSS)
-    other = along(kept, PAIR)
-    got_0 = along(slot_2, NEAR)
-    got = along(sent_near, PAIR)
-    slot_1 = kept_near[:1] + got[:1] + got_1
+    kept = add(kept, *[along(kept, pairs) for pairs in (NEAR, FAR, ACROSS)])
+    got_near, kept = together(got_near, kept)
+    slot_0, slot_1 = add_halves(kept_near, along(sent_near, PAIR), got_near)
     got_own = along(slot_1, FAR)
-    inverse, orth, operand = factor(order, kept, other, lefts)
+    inverse, orth, operand = factor(order, kept, along(kept, PAIR), lefts)
     got_own, inverse = together(got_own, inverse)
-    own = kept_near[1:] + got[1:] + got_0 + got_own
-
-    chunk_1, chunk_2 = along(own, FAR), along(own, NEAR)
-    chunks = [own, chunk_1, chunk_2, along(chunk_1, NEAR)]
-    others = [along(chunk, PAIR) for chunk in chunks]
-
+    own = add(slot_0, got_own)
+
+    def new_pair(slot, raws, before):
+        return new_chunks(order, (slot, slot + 4), operand, inverse, raws, resident, before)
+
+    chunk_1, pair = along(own, FAR), along(own, PAIR)
     squares = square_row(inverse, own)
-    new, rights = [], []
-    for slot, step in enumerate((1, 2, 4, 0)):
-        if step:
-            squares = squares + along(squares, [(r, r ^ step) for r in range(RING)])
-        else:
-            squares = [squares] + [
-                lax.ppermute(squares, "col", [(c, c ^ d) for c in range(LINE)]) for d in range(1, LINE)
-            ]
-        raws = [chunks[slot], others[slot]]
-        new, right = new_chunks(order, (slot, slot + 4), operand, inverse, raws, resident, new)
-        rights += right
-        if step:
-            squares, new[0] = together(squares, new[0])
-    operand = update_operand(squares, orth, scale)
-    update = update_chunks(order, (0, 4, 1, 5), operand, rights[:4], [], cols)
-    update = update_chunks(order, (2, 6, 3, 7), operand, rights[4:], update, cols)
+    squares = add(squares, along(squares, PAIR))
+    squares, again = together(squares, own)
+    got, chunk_2 = along(squares, NEAR), along(again, NEAR)
+    new, rights = new_chunks(order, (0, 4), operand, inverse, [own, pair], resident, [])
+    got, chunk_1, new[0] = together(got, chunk_1, new[0])
+    chunk_3, pair_1 = along(chunk_1, NEAR), along(chunk_1, PAIR)
+    squares = add(squares, got)
+    got = along(squares, FAR)
+    pair_1, chunk_2 = together(pair_1, chunk_2)
+    new, right = new_chunks(order, (1, 5), operand, inverse, [chunk_1, pair_1], resident, new)
+    rights += right
+    got, chunk_2, chunk_3, new[0] = together(got, chunk_2, chunk_3, new[0])
+    pair_2, pair_3 = along(chunk_2, PAIR), along(chunk_3, PAIR)
+    squares = add(squares, got)
+    gots = [lax.ppermute(squares, "col", [(c, c ^ d) for c in range(LINE)]) for d in range(1, LINE)]
+    *gots, new[0] = together(*gots, new[0])
+    raws = [chunk_2, pair_2, chunk_3, pair_3]
+    new, right = new_chunks(order, (2, 6, 3, 7), operand, inverse, raws, resident, new)
+    rights += right
+    scaled = update_operand([squares] + gots, orth, scale)
+    update = update_chunks(order, (0, 4, 1, 5, 2, 6, 3, 7), scaled, rights, [], cols)
     return new[0], update[0]
 
 

time: 192 us -> 186 us (0.969)
  local copies, waits for them, and re-layouts: 6.76 us -> 0.02 us
    unnamed x12 -> x0, local copies, waits for them, and re-layouts: 6.75 us -> none
    ppermute x20 -> x19, waiting for transfers between devices: 25.5 us -> 19.3 us  [along(): return lax.ppermute(x, 'row', pairs)]
    ppermute x12, waiting for transfers between devices: 18.7 us -> 23.6 us  [the longest x4 16.3 us: outward(): return lax.ppermute(x, 'col', [(1, 0), (2, 3)])]
    pallas_call x2 -> x22, Pallas kernels: 44.9 us -> 47.9 us  [the longest x1 44.1 us: factor(): pl.pallas_call(lambda *refs: factor_kernel(len(lefts), RING // 2, *refs),...]
    pallas_call x4 -> x3, Pallas kernels: 14.9 us -> 13.2 us  [new_chunks(): pl.pallas_call(lambda *refs: new_kernel(places, len(before), *refs), in_s...]
    ppermute x20 -> x19, starting transfers between devices: 13.3 us -> 14.6 us  [along(): return lax.ppermute(x, 'row', pairs)]
    pallas_call x2 -> x1, Pallas kernels: 9.8 us -> 8.58 us  [update_chunks(): pl.pallas_call(lambda *refs: update_kernel(places, len(before), *refs), i...]
  transfers between devices with their start and end apart: 35 -> 34, of which waited for: 14 -> 15; matrix products, arithmetic and copies ran while one was open for 0% -> 0% of each run, Pallas kernels for 42% -> 40%
where the time goes in v1:
time: 186 us
  Pallas kernels  99.2 us (53%)
  waiting for transfers between devices  46 us (25%)
  starting transfers between devices  39 us (21%)
    pallas_call x1, Pallas kernels, factor(): pl.pallas_call(lambda *refs: factor_kernel(len(lefts), RING // 2, *refs),...  44.1 us
    ppermute x19, waiting for transfers between devices, along(): return lax.ppermute(x, 'row', pairs)  19.3 us
    ppermute x4, waiting for transfers between devices, outward(): return lax.ppermute(x, 'col', [(1, 0), (2, 3)])  16.3 us
    ppermute x19, starting transfers between devices, along(): return lax.ppermute(x, 'row', pairs)  14.6 us
    pallas_call x3, Pallas kernels, new_chunks(): pl.pallas_call(lambda *refs: new_kernel(places, len(before), *refs), in_s...  13.2 us
    pallas_call x7, Pallas kernels, raw_pieces(): pl.pallas_call(lambda *refs: raw_kernel(at, groups, bool(before), with_gr...  13 us
    ppermute x4, starting transfers between devices, inward(): return lax.ppermute(x, 'col', [(0, 1), (3, 2)])  12 us
    pallas_call x1, Pallas kernels, update_chunks(): pl.pallas_call(lambda *refs: update_kernel(places, len(before), *refs), i...  8.58 us
  transfers between devices with their start and end apart: 34, of which 15 were waited for; matrix products, arithmetic and copies ran while one was open for 0% of the time, Pallas kernels for 40%

profile of v1, /device:TPU:0, one launch (start us, length us, event | category | flops | bytes accessed | tf_op | source)
XLA Modules:
  0.0 185.6 jit_solution(5372349241252327238)
XLA Ops:
  0.7 7.1 %fetch.1 = (f32[1024,4096]{1,0:T(8,128)S(1)}, bf16[4096,256]{1,0:T(8,128)(2,1)S(1)}, bf16[4096,256]{1,0:T(8,128)(2,1)S(1)}) custom-call(f32[1024,4096]{1,0:T(8,128)} %m_hbm.1, f32[4096,256]{1,0:T(8,128)} %q_hbm), custom_call_target="tpu_custom_call" | custom-call | flops 1048576 | bytes 20971520 | tf_op jit(solution)/shard_map/fetch/pallas_call | solution.py:71
  7.8 2.0 %left.4.refs_0_ = f32[256,256]{1,0:T(8,128)S(1)} custom-call(f32[1024,4096]{1,0:T(8,128)S(1)} %get-tuple-element.69.refs_0_.refs_2_.refs_3_, bf16[4096,256]{1,0:T(8,128)(2,1)S(1)} %get-tuple-element.72.refs_1_, bf16[4096,256]{1,0:T(8,128)(2,1)S(1)} %get-tuple-element.71.refs_2_), custom_call_target="tpu_custom_call" | custom-call | flops 1610612736 | bytes 1048576 | tf_op jit(solution)/shard_map/left/pallas_call | solution.py:100
  9.7 4.9 %collective-permute-start = (f32[256,256]{1,0:T(8,128)S(1)}, f32[256,256]{1,0:T(8,128)S(1)}, u32[]{:S(2)}, u32[]{:S(2)}) collective-permute-start(f32[256,256]{1,0:T(8,128)S(1)} %left.4.refs_0_), channel_id=1, source_target_pairs={{0,1},{3,2},{4,5},{7,6},{8,9},{11,10},{12,13},{15,14},{16,17},{19,... | collective-permute-start | bytes 786440 | tf_op jit(solution)/shard_map/ppermute | solution.py:463
  14.7 2.0 %left.6.refs_0_ = f32[256,256]{1,0:T(8,128)S(1)} custom-call(f32[1024,4096]{1,0:T(8,128)S(1)} %get-tuple-element.69.refs_0_.refs_2_.refs_3_, bf16[4096,256]{1,0:T(8,128)(2,1)S(1)} %get-tuple-element.72.refs_1_, bf16[4096,256]{1,0:T(8,128)(2,1)S(1)} %get-tuple-element.71.refs_2_), custom_call_target="tpu_custom_call" | custom-call | flops 1610612736 | bytes 1048576 | tf_op jit(solution)/shard_map/left/pallas_call | solution.py:100
  18.0 2.0 %left.7.refs_0_ = f32[256,256]{1,0:T(8,128)S(1)} custom-call(f32[1024,4096]{1,0:T(8,128)S(1)} %get-tuple-element.69.refs_0_.refs_2_.refs_3_, bf16[4096,256]{1,0:T(8,128)(2,1)S(1)} %get-tuple-element.72.refs_1_, bf16[4096,256]{1,0:T(8,128)(2,1)S(1)} %get-tuple-element.71.refs_2_), custom_call_target="tpu_custom_call" | custom-call | flops 1610612736 | bytes 1048576 | tf_op jit(solution)/shard_map/left/pallas_call | solution.py:100
  21.4 2.0 %left.5.refs_0_ = f32[256,256]{1,0:T(8,128)S(1)} custom-call(f32[1024,4096]{1,0:T(8,128)S(1)} %get-tuple-element.69.refs_0_.refs_2_.refs_3_, bf16[4096,256]{1,0:T(8,128)(2,1)S(1)} %get-tuple-element.72.refs_1_, bf16[4096,256]{1,0:T(8,128)(2,1)S(1)} %get-tuple-element.71.refs_2_), custom_call_target="tpu_custom_call" | custom-call | flops 1610612736 | bytes 1048576 | tf_op jit(solution)/shard_map/left/pallas_call | solution.py:100
  23.4 4.4 %collective-permute-start.1 = (f32[256,256]{1,0:T(8,128)S(1)}, f32[256,256]{1,0:T(8,128)S(1)}, u32[]{:S(2)}, u32[]{:S(2)}) collective-permute-start(f32[256,256]{1,0:T(8,128)S(1)} %left.5.refs_0_), channel_id=1, source_target_pairs={{0,1},{3,2},{4,5},{7,6},{8,9},{11,10},{12,13},{15,14},{16,17},{19,... | collective-permute-start | bytes 786440 | tf_op jit(solution)/shard_map/ppermute | solution.py:463
  29.2 3.4 %collective-permute-done.8.refs_1_ = f32[256,256]{1,0:T(8,128)S(1)} collective-permute-done((f32[256,256]{1,0:T(8,128)S(1)}, f32[256,256]{1,0:T(8,128)S(1)}, u32[]{:S(2)}, u32[]{:S(2)}) %collective-permute-start.8) | collective-permute-done | bytes 262176 | tf_op jit(solution)/shard_map/ppermute | solution.py:463
  33.3 3.8 %collective-permute-done.1.refs_1_ = f32[256,256]{1,0:T(8,128)S(1)} collective-permute-done((f32[256,256]{1,0:T(8,128)S(1)}, f32[256,256]{1,0:T(8,128)S(1)}, u32[]{:S(2)}, u32[]{:S(2)}) %collective-permute-start.1) | collective-permute-done | bytes 262176 | tf_op jit(solution)/shard_map/ppermute | solution.py:463
  41.9 1.5 collective-permute-start.4
  43.4 8.9 %collective-permute-done.7.b_ref = f32[256,256]{1,0:T(8,128)S(1)} collective-permute-done((f32[256,256]{1,0:T(8,128)S(1)}, f32[256,256]{1,0:T(8,128)S(1)}, u32[]{:S(2)}, u32[]{:S(2)}) %collective-permute-start.7) | collective-permute-done | bytes 262176 | tf_op jit(solution)/shard_map/ppermute | solution.py:469
  52.9 5.0 %collective-permute-done.11.b_ref = f32[256,256]{1,0:T(8,128)S(1)} collective-permute-done((f32[256,256]{1,0:T(8,128)S(1)}, f32[256,256]{1,0:T(8,128)S(1)}, u32[]{:S(2)}, u32[]{:S(2)}) %collective-permute-start.11) | collective-permute-done | bytes 262176 | tf_op jit(solution)/shard_map/ppermute | solution.py:469
  58.5 2.7 %raw_right.7 = (f32[2,256,512]{2,1,0:T(8,128)S(1)}, f32[2,256,512]{2,1,0:T(8,128)S(1)}, f32[2,256,512]{2,1,0:T(8,128)S(1)}, f32[2,256,512]{2,1,0:T(8,128)S(1)}, f32[256,256]{1,0:T(8,128)S(1)}) custom-call(s32[9]{0:T(128)S(1)} %compare_select_fusion.1.order_ref.refs_0_, f32[256,256]{1,0:T(8,128)S(1)} %choose.7.refs_1_.refs_3_, ...), custom_call_target="tpu_custom_call" | custom-call | flops 1610612736 | bytes 1048576 | tf_op jit(solution)/shard_map/raw_right/pallas_call | solution.py:133
  61.2 2.4 %collective-permute-done.10.b_ref = f32[256,256]{1,0:T(8,128)S(1)} collective-permute-done((f32[256,256]{1,0:T(8,128)S(1)}, f32[256,256]{1,0:T(8,128)S(1)}, u32[]{:S(2)}, u32[]{:S(2)}) %collective-permute-start.10) | collective-permute-done | bytes 262176 | tf_op jit(solution)/shard_map/ppermute | solution.py:469
  64.1 2.7 %raw_right.8 = (f32[2,256,512]{2,1,0:T(8,128)S(1)}, f32[2,256,512]{2,1,0:T(8,128)S(1)}, f32[2,256,512]{2,1,0:T(8,128)S(1)}, f32[2,256,512]{2,1,0:T(8,128)S(1)}, f32[256,256]{1,0:T(8,128)S(1)}) custom-call(s32[9]{0:T(128)S(1)} %compare_select_fusion.1.order_ref.refs_0_, f32[256,256]{1,0:T(8,128)S(1)} %choose.6.refs_1_.refs_4_, ...), custom_call_target="tpu_custom_call" | custom-call | flops 1610612736 | bytes 1048576 | tf_op jit(solution)/shard_map/raw_right/pallas_call | solution.py:133
  66.8 2.7 %raw_right.9 = (f32[2,256,512]{2,1,0:T(8,128)S(1)}, f32[2,256,512]{2,1,0:T(8,128)S(1)}, f32[2,256,512]{2,1,0:T(8,128)S(1)}, f32[2,256,512]{2,1,0:T(8,128)S(1)}, f32[256,256]{1,0:T(8,128)S(1)}) custom-call(s32[9]{0:T(128)S(1)} %compare_select_fusion.1.order_ref.refs_0_, f32[256,256]{1,0:T(8,128)S(1)} %choose.5.refs_1_.refs_5_, ...), custom_call_target="tpu_custom_call" | custom-call | flops 1610612736 | bytes 1048576 | tf_op jit(solution)/shard_map/raw_right/pallas_call | solution.py:133
  74.4 1.5 collective-permute-start.13
  82.0 11.5 %collective-permute-done.15.refs_1_ = f32[128,256]{1,0:T(8,128)S(1)} collective-permute-done((f32[128,256]{1,0:T(8,128)S(1)}, f32[128,256]{1,0:T(8,128)S(1)}, u32[]{:S(2)}, u32[]{:S(2)}) %collective-permute-start.15) | collective-permute-done | bytes 131104 | tf_op jit(solution)/shard_map/ppermute | solution.py:438
  93.5 2.3 %collective-permute-done.17.refs_3_ = f32[128,256]{1,0:T(8,128)S(1)} collective-permute-done((f32[128,256]{1,0:T(8,128)S(1)}, f32[128,256]{1,0:T(8,128)S(1)}, u32[]{:S(2)}, u32[]{:S(2)}) %collective-permute-start.17) | collective-permute-done | bytes 131104 | tf_op jit(solution)/shard_map/ppermute | solution.py:438
  98.0 44.1 %factor.1 = (f32[256,256]{1,0:T(8,128)S(1)}, f32[1024,256]{1,0:T(8,128)S(1)}, bf16[1024,768]{1,0:T(8,128)(2,1)S(1)}) custom-call(s32[9]{0:T(128)S(1)} %compare_select_fusion.1.order_ref.refs_0_, f32[128,256]{1,0:T(8,128)S(1)} %add.67.refs_1_, f32[128,256]{1,0:T(8,128)S(1)} %collective-permute-done.18.refs_2_, f32[256,256]{1,0:T(8,128)S(1)} %choose.7.refs_1_.refs_3_, ...), custom_call_target="tpu_custom_call" | custom-call | flops 1 | bytes 1 | tf_op jit(solution)/shard_map/factor/pallas_call | solution.py:240
  142.4 1.5 collective-permute-start.23
  146.4 1.5 collective-permute-start.22
  148.4 3.7 %new_momentum.3 = (f32[1024,4096]{1,0:T(8,128)}, bf16[768,512]{1,0:T(8,128)(2,1)S(1)}, bf16[768,512]{1,0:T(8,128)(2,1)S(1)}) custom-call(s32[9]{0:T(128)S(1)} %compare_select_fusion.1.order_ref.refs_0_, bf16[1024,768]{1,0:T(8,128)(2,1)S(1)} %get-tuple-element.95.refs_1_, f32[256,256]{1,0:T(8,128)S(1)} %get-tuple-element.102.inv_ref.refs_2_, ...), custom_call_target="tpu_custom_call" | custom-call | flops 1610612736 | bytes 4194304 | tf_op jit(solution)/shard_map/new_momentum/pallas_call | solution.py:324
  152.9 2.4 %collective-permute-start.28 = (f32[1,256,512]{2,1,0:T(8,128)S(1)}, f32[1,256,512]{2,1,0:T(8,128)S(1)}, u32[]{:S(2)}, u32[]{:S(2)}) collective-permute-start(f32[1,256,512]{2,1,0:T(8,128)S(1)} %collective-permute-done.23.refs_4_), channel_id=1, source_target_pairs={{0,8},{4,20},{8,0},{12,28},{16,24},{20,4},{24,16},{28,12},{1,9},{5... | collective-permute-start | bytes 1572872 | tf_op jit(solution)/shard_map/ppermute | solution.py:438
  155.3 1.5 collective-permute-start.25
  157.1 3.7 %new_momentum.4 = (f32[1024,4096]{1,0:T(8,128)}, bf16[768,512]{1,0:T(8,128)(2,1)S(1)}, bf16[768,512]{1,0:T(8,128)(2,1)S(1)}) custom-call(s32[9]{0:T(128)S(1)} %compare_select_fusion.1.order_ref.refs_0_, bf16[1024,768]{1,0:T(8,128)(2,1)S(1)} %get-tuple-element.95.refs_1_, ...), custom_call_target="tpu_custom_call", output_to_operand_aliasing={{0}: (6, {})} | custom-call | flops 1610612736 | bytes 4194304 | tf_op jit(solution)/shard_map/new_momentum/pallas_call | solution.py:324
  160.9 1.9 %collective-permute-done.28.refs_6_ = f32[1,256,512]{2,1,0:T(8,128)S(1)} collective-permute-done((f32[1,256,512]{2,1,0:T(8,128)S(1)}, f32[1,256,512]{2,1,0:T(8,128)S(1)}, u32[]{:S(2)}, u32[]{:S(2)}) %collective-permute-start.28) | collective-permute-done | bytes 524320 | tf_op jit(solution)/shard_map/ppermute | solution.py:438
  163.3 2.1 %collective-permute-start.32 = (f32[8,256]{1,0:T(8,128)S(1)}, f32[8,256]{1,0:T(8,128)S(1)}, u32[]{:S(2)}, u32[]{:S(2)}) collective-permute-start(f32[8,256]{1,0:T(8,128)S(1)} %add.71.refs_0_), channel_id=1, source_target_pairs={{0,2},{1,3},{2,0},{3,1},{4,6},{5,7},{6,4},{7,5},{8,10},{9,11},{10,... | collective-permute-start | bytes 24584 | tf_op jit(solution)/shard_map/ppermute | solution.py:527
  165.4 2.3 %collective-permute-start.33 = (f32[8,256]{1,0:T(8,128)S(1)}, f32[8,256]{1,0:T(8,128)S(1)}, u32[]{:S(2)}, u32[]{:S(2)}) collective-permute-start(f32[8,256]{1,0:T(8,128)S(1)} %add.71.refs_0_), channel_id=1, source_target_pairs={{0,3},{1,2},{2,1},{3,0},{4,7},{5,6},{6,5},{7,4},{8,11},{9,10},{10,... | collective-permute-start | bytes 24584 | tf_op jit(solution)/shard_map/ppermute | solution.py:527
  167.9 3.0 %collective-permute-done.33.refs_3_ = f32[8,256]{1,0:T(8,128)S(1)} collective-permute-done((f32[8,256]{1,0:T(8,128)S(1)}, f32[8,256]{1,0:T(8,128)S(1)}, u32[]{:S(2)}, u32[]{:S(2)}) %collective-permute-start.33) | collective-permute-done | bytes 8224 | tf_op jit(solution)/shard_map/ppermute | solution.py:527
  171.0 5.8 %new_momentum.5 = (f32[1024,4096]{1,0:T(8,128)}, bf16[768,512]{1,0:T(8,128)(2,1)S(1)}, bf16[768,512]{1,0:T(8,128)(2,1)S(1)}, bf16[768,512]{1,0:T(8,128)(2,1)S(1)}, bf16[768,512]{1,0:T(8,128)(2,1)S(1)}) custom-call(s32[9]{0:T(128)S(1)} %compare_select_fusion.1.order_ref.refs_0_, ...), custom_call_target="tpu_custom_call", output_to_operand_aliasing={{0}: (8, {})} | custom-call | flops 3221225472 | bytes 8388608 | tf_op jit(solution)/shard_map/new_momentum/pallas_call | solution.py:324
  176.8 8.6 %update.1 = f32[1024,4096]{1,0:T(8,128)} custom-call(s32[9]{0:T(128)S(1)} %compare_select_fusion.1.order_ref.refs_0_, bf16[1024,768]{1,0:T(8,128)(2,1)S(1)} %operand.1.refs_1_, bf16[768,512]{1,0:T(8,128)(2,1)S(1)} %get-tuple-element.124.refs_2_, bf16[768,512]{1,0:T(8,128)(2,1)S(1)} %get-tuple-element.125.refs_3_, ...), custom_call_target="tpu_custom_call" | custom-call | flops 6442450944 | bytes 16777216 | tf_op jit(solution)/shard_map/update/pallas_call | solution.py:364
  (78 shorter events, 29.5 us)
Async XLA Ops:
  9.7 11.6 %collective-permute-start = (f32[256,256]{1,0:T(8,128)S(1)}, f32[256,256]{1,0:T(8,128)S(1)}, u32[]{:S(2)}, u32[]{:S(2)}) collective-permute-start(f32[256,256]{1,0:T(8,128)S(1)} %left.4.refs_0_), channel_id=1, source_target_pairs={{0,1},{3,2},{4,5},{7,6},{8,9},{11,10},{12,13},{15,14},{16,17},{19,... | collective-permute-start | bytes 786440 | tf_op jit(solution)/shard_map/ppermute | solution.py:463
  16.7 11.8 %collective-permute-start.5 = (f32[256,256]{1,0:T(8,128)S(1)}, f32[256,256]{1,0:T(8,128)S(1)}, u32[]{:S(2)}, u32[]{:S(2)}) collective-permute-start(f32[256,256]{1,0:T(8,128)S(1)} %left.6.refs_0_), channel_id=1, source_target_pairs={{0,1},{3,2},{4,5},{7,6},{8,9},{11,10},{12,13},{15,14},{16,17},{19,... | collective-permute-start | bytes 786440 | tf_op jit(solution)/shard_map/ppermute | solution.py:463
  20.0 12.7 %collective-permute-start.8 = (f32[256,256]{1,0:T(8,128)S(1)}, f32[256,256]{1,0:T(8,128)S(1)}, u32[]{:S(2)}, u32[]{:S(2)}) collective-permute-start(f32[256,256]{1,0:T(8,128)S(1)} %left.7.refs_0_), channel_id=1, source_target_pairs={{0,1},{3,2},{4,5},{7,6},{8,9},{11,10},{12,13},{15,14},{16,17},{19,... | collective-permute-start | bytes 786440 | tf_op jit(solution)/shard_map/ppermute | solution.py:463
  23.4 13.7 %collective-permute-start.1 = (f32[256,256]{1,0:T(8,128)S(1)}, f32[256,256]{1,0:T(8,128)S(1)}, u32[]{:S(2)}, u32[]{:S(2)}) collective-permute-start(f32[256,256]{1,0:T(8,128)S(1)} %left.5.refs_0_), channel_id=1, source_target_pairs={{0,1},{3,2},{4,5},{7,6},{8,9},{11,10},{12,13},{15,14},{16,17},{19,... | collective-permute-start | bytes 786440 | tf_op jit(solution)/shard_map/ppermute | solution.py:463
  27.8 9.3 %collective-permute-start.2 = (f32[256,256]{1,0:T(8,128)S(1)}, f32[256,256]{1,0:T(8,128)S(1)}, u32[]{:S(2)}, u32[]{:S(2)}) collective-permute-start(f32[256,256]{1,0:T(8,128)S(1)} %add.57.refs_0_), channel_id=1, source_target_pairs={{1,2},{2,1},{5,6},{6,5},{9,10},{10,9},{13,14},{14,13},{17,18},{18,... | collective-permute-start | bytes 786440 | tf_op jit(solution)/shard_map/ppermute | solution.py:466
  28.5 9.3 %collective-permute-start.6 = (f32[256,256]{1,0:T(8,128)S(1)}, f32[256,256]{1,0:T(8,128)S(1)}, u32[]{:S(2)}, u32[]{:S(2)}) collective-permute-start(f32[256,256]{1,0:T(8,128)S(1)} %add.61.refs_0_), channel_id=1, source_target_pairs={{1,2},{2,1},{5,6},{6,5},{9,10},{10,9},{13,14},{14,13},{17,18},{18,... | collective-permute-start | bytes 786440 | tf_op jit(solution)/shard_map/ppermute | solution.py:466
  32.6 7.9 %collective-permute-start.9 = (f32[256,256]{1,0:T(8,128)S(1)}, f32[256,256]{1,0:T(8,128)S(1)}, u32[]{:S(2)}, u32[]{:S(2)}) collective-permute-start(f32[256,256]{1,0:T(8,128)S(1)} %add.63.refs_0_), channel_id=1, source_target_pairs={{1,2},{2,1},{5,6},{6,5},{9,10},{10,9},{13,14},{14,13},{17,18},{18,... | collective-permute-start | bytes 786440 | tf_op jit(solution)/shard_map/ppermute | solution.py:466
  37.2 4.7 %collective-permute-start.3 = (f32[256,256]{1,0:T(8,128)S(1)}, f32[256,256]{1,0:T(8,128)S(1)}, u32[]{:S(2)}, u32[]{:S(2)}) collective-permute-start(f32[256,256]{1,0:T(8,128)S(1)} %add.58.refs_0_), channel_id=1, source_target_pairs={{1,2},{2,1},{5,6},{6,5},{9,10},{10,9},{13,14},{14,13},{17,18},{18,... | collective-permute-start | bytes 786440 | tf_op jit(solution)/shard_map/ppermute | solution.py:466
  37.9 14.4 %collective-permute-start.7 = (f32[256,256]{1,0:T(8,128)S(1)}, f32[256,256]{1,0:T(8,128)S(1)}, u32[]{:S(2)}, u32[]{:S(2)}) collective-permute-start(f32[256,256]{1,0:T(8,128)S(1)} %add.62.a_ref), channel_id=1, source_target_pairs={{1,0},{2,3},{5,4},{6,7},{9,8},{10,11},{13,12},{14,15},{17,16},{18,... | collective-permute-start | bytes 786440 | tf_op jit(solution)/shard_map/ppermute | solution.py:469
  39.2 18.7 %collective-permute-start.11 = (f32[256,256]{1,0:T(8,128)S(1)}, f32[256,256]{1,0:T(8,128)S(1)}, u32[]{:S(2)}, u32[]{:S(2)}) collective-permute-start(f32[256,256]{1,0:T(8,128)S(1)} %add.59.a_ref), channel_id=1, source_target_pairs={{1,0},{2,3},{5,4},{6,7},{9,8},{10,11},{13,12},{14,15},{17,16},{18,... | collective-permute-start | bytes 786440 | tf_op jit(solution)/shard_map/ppermute | solution.py:469
  40.6 23.0 %collective-permute-start.10 = (f32[256,256]{1,0:T(8,128)S(1)}, f32[256,256]{1,0:T(8,128)S(1)}, u32[]{:S(2)}, u32[]{:S(2)}) collective-permute-start(f32[256,256]{1,0:T(8,128)S(1)} %add.64.a_ref), channel_id=1, source_target_pairs={{1,0},{2,3},{5,4},{6,7},{9,8},{10,11},{13,12},{14,15},{17,16},{18,... | collective-permute-start | bytes 786440 | tf_op jit(solution)/shard_map/ppermute | solution.py:469
  41.9 27.6 %collective-permute-start.4 = (f32[256,256]{1,0:T(8,128)S(1)}, f32[256,256]{1,0:T(8,128)S(1)}, u32[]{:S(2)}, u32[]{:S(2)}) collective-permute-start(f32[256,256]{1,0:T(8,128)S(1)} %add.60.a_ref), channel_id=1, source_target_pairs={{1,0},{2,3},{5,4},{6,7},{9,8},{10,11},{13,12},{14,15},{17,16},{18,... | collective-permute-start | bytes 786440 | tf_op jit(solution)/shard_map/ppermute | solution.py:469
  71.4 2.9 %collective-permute-start.12 = (f32[2,256,512]{2,1,0:T(8,128)S(1)}, f32[2,256,512]{2,1,0:T(8,128)S(1)}, u32[]{:S(2)}, u32[]{:S(2)}) collective-permute-start(f32[2,256,512]{2,1,0:T(8,128)S(1)} %raw_right.10), channel_id=1, source_target_pairs={{0,4},{4,0},{8,12},{12,8},{16,20},{20,16},{24,28},{28,24},{1,5},{5... | collective-permute-start | bytes 3145736 | tf_op jit(solution)/shard_map/ppermute | solution.py:438
  72.4 1.8 collective-permute-start.14
  74.4 21.5 %collective-permute-start.13 = (f32[2,256,512]{2,1,0:T(8,128)S(1)}, f32[2,256,512]{2,1,0:T(8,128)S(1)}, u32[]{:S(2)}, u32[]{:S(2)}) collective-permute-start(f32[2,256,512]{2,1,0:T(8,128)S(1)} %add.65), channel_id=1, source_target_pairs={{0,8},{4,20},{8,0},{12,28},{16,24},{20,4},{24,16},{28,12},{1,9},{5... | collective-permute-start | bytes 3145736 | tf_op jit(solution)/shard_map/ppermute | solution.py:438
  77.2 18.7 %collective-permute-start.19 = (f32[2,256,512]{2,1,0:T(8,128)S(1)}, f32[2,256,512]{2,1,0:T(8,128)S(1)}, u32[]{:S(2)}, u32[]{:S(2)}) collective-permute-start(f32[2,256,512]{2,1,0:T(8,128)S(1)} %raw_right.13), channel_id=1, source_target_pairs={{0,4},{4,0},{8,12},{12,8},{16,20},{20,16},{24,28},{28,24},{1,5},{5... | collective-permute-start | bytes 3145736 | tf_op jit(solution)/shard_map/ppermute | solution.py:438
  77.3 16.2 %collective-permute-start.15 = (f32[128,256]{1,0:T(8,128)S(1)}, f32[128,256]{1,0:T(8,128)S(1)}, u32[]{:S(2)}, u32[]{:S(2)}) collective-permute-start(f32[128,256]{1,0:T(8,128)S(1)} %add.66.refs_0_), channel_id=1, source_target_pairs={{0,8},{4,20},{8,0},{12,28},{16,24},{20,4},{24,16},{28,12},{1,9},{5... | collective-permute-start | bytes 393224 | tf_op jit(solution)/shard_map/ppermute | solution.py:438
  78.6 14.9 %collective-permute-start.16 = (f32[128,256]{1,0:T(8,128)S(1)}, f32[128,256]{1,0:T(8,128)S(1)}, u32[]{:S(2)}, u32[]{:S(2)}) collective-permute-start(f32[128,256]{1,0:T(8,128)S(1)} %add.66.refs_0_), channel_id=1, source_target_pairs={{0,16},{4,12},{8,24},{12,4},{16,0},{20,28},{24,8},{28,20},{1,17},{... | collective-permute-start | bytes 393224 | tf_op jit(solution)/shard_map/ppermute | solution.py:438
  79.4 16.5 %collective-permute-start.17 = (f32[128,256]{1,0:T(8,128)S(1)}, f32[128,256]{1,0:T(8,128)S(1)}, u32[]{:S(2)}, u32[]{:S(2)}) collective-permute-start(f32[128,256]{1,0:T(8,128)S(1)} %add.66.refs_0_), channel_id=1, source_target_pairs={{0,24},{4,28},{8,16},{12,20},{16,8},{20,12},{24,0},{28,4},{1,25},{... | collective-permute-start | bytes 393224 | tf_op jit(solution)/shard_map/ppermute | solution.py:438
  96.1 46.0 %collective-permute-start.20 = (f32[1,256,512]{2,1,0:T(8,128)S(1)}, f32[1,256,512]{2,1,0:T(8,128)S(1)}, u32[]{:S(2)}, u32[]{:S(2)}) collective-permute-start(f32[1,256,512]{2,1,0:T(8,128)S(1)} %get-tuple-element.100), channel_id=1, source_target_pairs={{0,16},{4,12},{8,24},{12,4},{16,0},{20,28},{24,8},{28,20},{1,17},{... | collective-permute-start | bytes 1572872 | tf_op jit(solution)/shard_map/ppermute | solution.py:438
  142.1 6.3 %collective-permute-start.24 = (f32[1,256,512]{2,1,0:T(8,128)S(1)}, f32[1,256,512]{2,1,0:T(8,128)S(1)}, u32[]{:S(2)}, u32[]{:S(2)}) collective-permute-start(f32[1,256,512]{2,1,0:T(8,128)S(1)} %add.68.raw_ref.refs_4_), channel_id=1, source_target_pairs={{0,4},{4,0},{8,12},{12,8},{16,20},{20,16},{24,28},{28,24},{1,5},{5... | collective-permute-start | bytes 1572872 | tf_op jit(solution)/shard_map/ppermute | solution.py:438
  142.4 10.5 %collective-permute-start.23 = (f32[1,256,512]{2,1,0:T(8,128)S(1)}, f32[1,256,512]{2,1,0:T(8,128)S(1)}, u32[]{:S(2)}, u32[]{:S(2)}) collective-permute-start(f32[1,256,512]{2,1,0:T(8,128)S(1)} %add.68.raw_ref.refs_4_), channel_id=1, source_target_pairs={{0,16},{4,12},{8,24},{12,4},{16,0},{20,28},{24,8},{28,20},{1,17},{... | collective-permute-start | bytes 1572872 | tf_op jit(solution)/shard_map/ppermute | solution.py:438
  146.4 5.7 %collective-permute-start.22 = (f32[8,256]{1,0:T(8,128)S(1)}, f32[8,256]{1,0:T(8,128)S(1)}, u32[]{:S(2)}, u32[]{:S(2)}) collective-permute-start(f32[8,256]{1,0:T(8,128)S(1)} %add.69.refs_0_), channel_id=1, source_target_pairs={{0,8},{4,20},{8,0},{12,28},{16,24},{20,4},{24,16},{28,12},{1,9},{5... | collective-permute-start | bytes 24584 | tf_op jit(solution)/shard_map/ppermute | solution.py:438
  147.9 9.2 %collective-permute-start.27 = (f32[1,256,512]{2,1,0:T(8,128)S(1)}, f32[1,256,512]{2,1,0:T(8,128)S(1)}, u32[]{:S(2)}, u32[]{:S(2)}) collective-permute-start(f32[1,256,512]{2,1,0:T(8,128)S(1)} %add.68.raw_ref.refs_4_), channel_id=1, source_target_pairs={{0,8},{4,20},{8,0},{12,28},{16,24},{20,4},{24,16},{28,12},{1,9},{5... | collective-permute-start | bytes 1572872 | tf_op jit(solution)/shard_map/ppermute | solution.py:438
  152.9 4.2 %collective-permute-start.26 = (f32[1,256,512]{2,1,0:T(8,128)S(1)}, f32[1,256,512]{2,1,0:T(8,128)S(1)}, u32[]{:S(2)}, u32[]{:S(2)}) collective-permute-start(f32[1,256,512]{2,1,0:T(8,128)S(1)} %collective-permute-done.23.refs_4_), channel_id=1, source_target_pairs={{0,4},{4,0},{8,12},{12,8},{16,20},{20,16},{24,28},{28,24},{1,5},{5... | collective-permute-start | bytes 1572872 | tf_op jit(solution)/shard_map/ppermute | solution.py:438
  152.9 9.9 %collective-permute-start.28 = (f32[1,256,512]{2,1,0:T(8,128)S(1)}, f32[1,256,512]{2,1,0:T(8,128)S(1)}, u32[]{:S(2)}, u32[]{:S(2)}) collective-permute-start(f32[1,256,512]{2,1,0:T(8,128)S(1)} %collective-permute-done.23.refs_4_), channel_id=1, source_target_pairs={{0,8},{4,20},{8,0},{12,28},{16,24},{20,4},{24,16},{28,12},{1,9},{5... | collective-permute-start | bytes 1572872 | tf_op jit(solution)/shard_map/ppermute | solution.py:438
  155.3 5.6 %collective-permute-start.25 = (f32[8,256]{1,0:T(8,128)S(1)}, f32[8,256]{1,0:T(8,128)S(1)}, u32[]{:S(2)}, u32[]{:S(2)}) collective-permute-start(f32[8,256]{1,0:T(8,128)S(1)} %add.70.refs_0_), channel_id=1, source_target_pairs={{0,16},{4,12},{8,24},{12,4},{16,0},{20,28},{24,8},{28,20},{1,17},{... | collective-permute-start | bytes 24584 | tf_op jit(solution)/shard_map/ppermute | solution.py:438
  162.8 8.2 %collective-permute-start.29 = (f32[1,256,512]{2,1,0:T(8,128)S(1)}, f32[1,256,512]{2,1,0:T(8,128)S(1)}, u32[]{:S(2)}, u32[]{:S(2)}) collective-permute-start(f32[1,256,512]{2,1,0:T(8,128)S(1)} %collective-permute-done.27.refs_4_), channel_id=1, source_target_pairs={{0,4},{4,0},{8,12},{12,8},{16,20},{20,16},{24,28},{28,24},{1,5},{5... | collective-permute-start | bytes 1572872 | tf_op jit(solution)/shard_map/ppermute | solution.py:438
  162.9 8.1 %collective-permute-start.30 = (f32[1,256,512]{2,1,0:T(8,128)S(1)}, f32[1,256,512]{2,1,0:T(8,128)S(1)}, u32[]{:S(2)}, u32[]{:S(2)}) collective-permute-start(f32[1,256,512]{2,1,0:T(8,128)S(1)} %collective-permute-done.28.refs_6_), channel_id=1, source_target_pairs={{0,4},{4,0},{8,12},{12,8},{16,20},{20,16},{24,28},{28,24},{1,5},{5... | collective-permute-start | bytes 1572872 | tf_op jit(solution)/shard_map/ppermute | solution.py:438
  163.3 4.4 %collective-permute-start.31 = (f32[8,256]{1,0:T(8,128)S(1)}, f32[8,256]{1,0:T(8,128)S(1)}, u32[]{:S(2)}, u32[]{:S(2)}) collective-permute-start(f32[8,256]{1,0:T(8,128)S(1)} %add.71.refs_0_), channel_id=1, source_target_pairs={{0,1},{1,0},{2,3},{3,2},{4,5},{5,4},{6,7},{7,6},{8,9},{9,8},{10,11... | collective-permute-start | bytes 24584 | tf_op jit(solution)/shard_map/ppermute | solution.py:527
  163.3 4.5 %collective-permute-start.32 = (f32[8,256]{1,0:T(8,128)S(1)}, f32[8,256]{1,0:T(8,128)S(1)}, u32[]{:S(2)}, u32[]{:S(2)}) collective-permute-start(f32[8,256]{1,0:T(8,128)S(1)} %add.71.refs_0_), channel_id=1, source_target_pairs={{0,2},{1,3},{2,0},{3,1},{4,6},{5,7},{6,4},{7,5},{8,10},{9,11},{10,... | collective-permute-start | bytes 24584 | tf_op jit(solution)/shard_map/ppermute | solution.py:527
  165.4 5.4 %collective-permute-start.33 = (f32[8,256]{1,0:T(8,128)S(1)}, f32[8,256]{1,0:T(8,128)S(1)}, u32[]{:S(2)}, u32[]{:S(2)}) collective-permute-start(f32[8,256]{1,0:T(8,128)S(1)} %add.71.refs_0_), channel_id=1, source_target_pairs={{0,3},{1,2},{2,1},{3,0},{4,7},{5,6},{6,5},{7,4},{8,11},{9,10},{10,... | collective-permute-start | bytes 24584 | tf_op jit(solution)/shard_map/ppermute | solution.py:527
  (2 other events, 2.6 us)

commit v2 on v1

--- a/solution.py
+++ b/solution.py
@@ -17,6 +17,7 @@
 ANY = pl.BlockSpec(memory_space=pl.ANY)
 LINE = 4
 RING = 8
+SHARES = (3, 3, 2)
 
 
 def split(x):
@@ -171,6 +172,11 @@
     return lax.dot_general(a.astype(BF16), b.astype(BF16), (contract, ((), ())), preferred_element_type=F32)
 
 
+def split_dot(a, b, contract=((1,), (0,))):
+    (a_high, a_low), (b_high, b_low) = split(a), split(b)
+    return rough_dot(a_high, b_high, contract) + rough_dot(a_high, b_low, contract) + rough_dot(a_low, b_high, contract)
+
+
 def newton(gram_ref, x_ref):
     rank = gram_ref.shape[0]
     rows = lax.broadcasted_iota(jnp.int32, (rank, rank), 0)
@@ -178,7 +184,7 @@
     eye = jnp.where(rows == cols, 1.0, 0.0).astype(F32)
     gram = gram_ref[...]
     x = eye * lax.rsqrt(jnp.sum(gram * eye, axis=1, keepdims=True))
-    for times in (rough_dot, rough_dot, full_dot, full_dot):
+    for times in (rough_dot, rough_dot, split_dot, full_dot):
         error = times(times(x, gram), x, ((1,), (1,))) - eye
         x = x - times(jnp.where(rows > cols, error, 0.5 * eye * error), x)
     x_ref[...] = x
@@ -453,11 +459,12 @@
     order = jnp.where(slots < RING, order, (at > 0) & (at < LINE - 1)).astype(jnp.int32)
     order, right_factor = together(order, right_factor)
 
-    size = rows // 4
     resident, high, low = fetch(momentum, right_factor)
+    sizes = [rows // 8 * share for share in SHARES]
+    starts = [sum(sizes[:k]) for k in range(len(sizes))]
 
     def left_of(k, high):
-        return left_piece(resident, high, low, k * size, size)
+        return left_piece(resident, high, low, starts[k], sizes[k])
 
     def inward(x):
         return lax.ppermute(x, "col", [(0, 1), (3, 2)])
@@ -468,28 +475,29 @@
     def outward(x):
         return lax.ppermute(x, "col", [(1, 0), (2, 3)])
 
-    parts = [left_of(k, high) for k in range(3)]
+    *early, final = range(len(sizes))
+    parts = [left_of(k, high) for k in early]
     held = [add(part, inward(part)) for part in parts]
     high, held[0] = together(high, held[0])
-    part = left_of(3, high)
+    part = left_of(final, high)
     held.append(add(part, inward(part)))
-    crossed = [add(x, across(x)) for x in held[:3]]
-    held[3], crossed[0] = together(held[3], crossed[0])
-    crossed.append(add(held[3], across(held[3])))
+    crossed = [add(x, across(x)) for x in held[:-1]]
+    held[-1], crossed[0] = together(held[-1], crossed[0])
+    crossed.append(add(held[-1], across(held[-1])))
     lefts = [choose(order, x, outward(x)) for x in crossed]
 
     groups = ((7, 6), (3, 2), (5, 4), (1, 0))
     sums = []
-    for k in range(3):
-        sums = raw_pieces(order, groups, lefts[k], resident, k * size, sums, 1)
+    for k in early:
+        sums = raw_pieces(order, groups, lefts[k], resident, starts[k], sums, 1)
     *sums, gram = sums
 
     def last(order, g):
-        return raw_pieces(order, groups[g : g + 1], lefts[3], resident, 3 * size, [sums[g]], 0)[0]
+        return raw_pieces(order, groups[g : g + 1], lefts[-1], resident, starts[-1], [sums[g]], 0)[0]
 
     sent_far = last(order, 0)
     order_1, sent_far = together(order, sent_far)
-    halves = gram_halves(order_1, lefts[3], gram)
+    halves = gram_halves(order_1, lefts[-1], gram)
     order_2, halves = together(order_1, halves)
     kept_far = last(order_2, 1)
     kept_far = add(kept_far, along(sent_far, PAIR))

time: 186 us -> 181 us (0.973)
  waiting for transfers between devices: 46 us -> 43.2 us
    ppermute x4 -> x3, waiting for transfers between devices: 16.3 us -> 11.4 us  [outward(): return lax.ppermute(x, 'col', [(1, 0), (2, 3)])]
    ppermute x4 -> x3, starting transfers between devices: 12 us -> 13.5 us  [inward(): return lax.ppermute(x, 'col', [(0, 1), (3, 2)])]
    ppermute x4 -> x3, starting transfers between devices: 5.35 us -> 4.06 us  [outward(): return lax.ppermute(x, 'col', [(1, 0), (2, 3)])]
    ppermute x4 -> x3, waiting for transfers between devices: 7.27 us -> 8.46 us  [inward(): return lax.ppermute(x, 'col', [(0, 1), (3, 2)])]
    pallas_call x4 -> x3, Pallas kernels: 7.85 us -> 7.54 us  [left_piece(): pl.pallas_call(lambda *refs: left_kernel(at, *refs), in_specs=[VMEM] * 3,...]
    pallas_call x7 -> x6, Pallas kernels: 13 us -> 13.1 us  [raw_pieces(): pl.pallas_call(lambda *refs: raw_kernel(at, groups, bool(before), with_gr...]
  transfers between devices with their start and end apart: 34 -> 31, of which waited for: 15 -> 13; matrix products, arithmetic and copies ran while one was open for 0% -> 0% of each run, Pallas kernels for 40% -> 40%
where the time goes in v2:
time: 181 us
  Pallas kernels  97.9 us (54%)
  waiting for transfers between devices  43.2 us (24%)
  starting transfers between devices  38.6 us (21%)
    pallas_call x1, Pallas kernels, factor(): pl.pallas_call(lambda *refs: factor_kernel(len(lefts), RING // 2, *refs),...  43.5 us
    ppermute x19, waiting for transfers between devices, along(): return lax.ppermute(x, 'row', pairs)  19.3 us
    ppermute x19, starting transfers between devices, along(): return lax.ppermute(x, 'row', pairs)  14.6 us
    ppermute x3, starting transfers between devices, inward(): return lax.ppermute(x, 'col', [(0, 1), (3, 2)])  13.5 us
    pallas_call x3, Pallas kernels, new_chunks(): pl.pallas_call(lambda *refs: new_kernel(places, len(before), *refs), in_s...  13.2 us
    pallas_call x6, Pallas kernels, raw_pieces(): pl.pallas_call(lambda *refs: raw_kernel(at, groups, bool(before), with_gr...  13.1 us
    ppermute x3, waiting for transfers between devices, outward(): return lax.ppermute(x, 'col', [(1, 0), (2, 3)])  11.4 us
    pallas_call x1, Pallas kernels, update_chunks(): pl.pallas_call(lambda *refs: update_kernel(places, len(before), *refs), i...  8.58 us
  transfers between devices with their start and end apart: 31, of which 13 were waited for; matrix products, arithmetic and copies ran while one was open for 0% of the time, Pallas kernels for 40%

profile of v2, /device:TPU:0, one launch (start us, length us, event | category | flops | bytes accessed | tf_op | source)
XLA Modules:
  0.0 181.1 jit_solution(13671184085387909775)
XLA Ops:
  0.7 7.1 %fetch.1 = (f32[1024,4096]{1,0:T(8,128)S(1)}, bf16[4096,256]{1,0:T(8,128)(2,1)S(1)}, bf16[4096,256]{1,0:T(8,128)(2,1)S(1)}) custom-call(f32[1024,4096]{1,0:T(8,128)} %m_hbm.1, f32[4096,256]{1,0:T(8,128)} %q_hbm), custom_call_target="tpu_custom_call" | custom-call | flops 1048576 | bytes 20971520 | tf_op jit(solution)/shard_map/fetch/pallas_call | solution.py:72
  7.8 2.8 %left.3.refs_0_ = f32[384,256]{1,0:T(8,128)S(1)} custom-call(f32[1024,4096]{1,0:T(8,128)S(1)} %get-tuple-element.64.refs_0_.refs_2_.refs_3_, bf16[4096,256]{1,0:T(8,128)(2,1)S(1)} %get-tuple-element.67.refs_1_, bf16[4096,256]{1,0:T(8,128)(2,1)S(1)} %get-tuple-element.66.refs_2_), custom_call_target="tpu_custom_call" | custom-call | flops 2415919104 | bytes 1048576 | tf_op jit(solution)/shard_map/left/pallas_call | solution.py:101
  10.6 5.0 %collective-permute-start = (f32[384,256]{1,0:T(8,128)S(1)}, f32[384,256]{1,0:T(8,128)S(1)}, u32[]{:S(2)}, u32[]{:S(2)}) collective-permute-start(f32[384,256]{1,0:T(8,128)S(1)} %left.3.refs_0_), channel_id=1, source_target_pairs={{0,1},{3,2},{4,5},{7,6},{8,9},{11,10},{12,13},{15,14},{16,17},{19,... | collective-permute-start | bytes 1179656 | tf_op jit(solution)/shard_map/ppermute | solution.py:470
  15.5 2.8 %left.5.refs_0_ = f32[384,256]{1,0:T(8,128)S(1)} custom-call(f32[1024,4096]{1,0:T(8,128)S(1)} %get-tuple-element.64.refs_0_.refs_2_.refs_3_, bf16[4096,256]{1,0:T(8,128)(2,1)S(1)} %get-tuple-element.67.refs_1_, bf16[4096,256]{1,0:T(8,128)(2,1)S(1)} %get-tuple-element.66.refs_2_), custom_call_target="tpu_custom_call" | custom-call | flops 2415919104 | bytes 1048576 | tf_op jit(solution)/shard_map/left/pallas_call | solution.py:101
  19.7 5.4 %collective-permute-done.refs_1_ = f32[384,256]{1,0:T(8,128)S(1)} collective-permute-done((f32[384,256]{1,0:T(8,128)S(1)}, f32[384,256]{1,0:T(8,128)S(1)}, u32[]{:S(2)}, u32[]{:S(2)}) %collective-permute-start) | collective-permute-done | bytes 393248 | tf_op jit(solution)/shard_map/ppermute | solution.py:470
  25.8 2.0 %left.4.refs_0_ = f32[256,256]{1,0:T(8,128)S(1)} custom-call(f32[1024,4096]{1,0:T(8,128)S(1)} %get-tuple-element.64.refs_0_.refs_2_.refs_3_, bf16[4096,256]{1,0:T(8,128)(2,1)S(1)} %get-tuple-element.67.refs_1_, bf16[4096,256]{1,0:T(8,128)(2,1)S(1)} %get-tuple-element.66.refs_2_), custom_call_target="tpu_custom_call" | custom-call | flops 1610612736 | bytes 1048576 | tf_op jit(solution)/shard_map/left/pallas_call | solution.py:101
  27.7 7.2 %collective-permute-start.1 = (f32[256,256]{1,0:T(8,128)S(1)}, f32[256,256]{1,0:T(8,128)S(1)}, u32[]{:S(2)}, u32[]{:S(2)}) collective-permute-start(f32[256,256]{1,0:T(8,128)S(1)} %left.4.refs_0_), channel_id=1, source_target_pairs={{0,1},{3,2},{4,5},{7,6},{8,9},{11,10},{12,13},{15,14},{16,17},{19,... | collective-permute-start | bytes 786440 | tf_op jit(solution)/shard_map/ppermute | solution.py:470
  35.7 3.1 %collective-permute-done.1.refs_1_ = f32[256,256]{1,0:T(8,128)S(1)} collective-permute-done((f32[256,256]{1,0:T(8,128)S(1)}, f32[256,256]{1,0:T(8,128)S(1)}, u32[]{:S(2)}, u32[]{:S(2)}) %collective-permute-start.1) | collective-permute-done | bytes 262176 | tf_op jit(solution)/shard_map/ppermute | solution.py:470
  42.3 1.5 collective-permute-start.4
  43.8 6.8 %collective-permute-done.8.b_ref = f32[384,256]{1,0:T(8,128)S(1)} collective-permute-done((f32[384,256]{1,0:T(8,128)S(1)}, f32[384,256]{1,0:T(8,128)S(1)}, u32[]{:S(2)}, u32[]{:S(2)}) %collective-permute-start.8) | collective-permute-done | bytes 393248 | tf_op jit(solution)/shard_map/ppermute | solution.py:476
  51.2 4.1 %raw_right.6 = (f32[2,256,512]{2,1,0:T(8,128)S(1)}, f32[2,256,512]{2,1,0:T(8,128)S(1)}, f32[2,256,512]{2,1,0:T(8,128)S(1)}, f32[2,256,512]{2,1,0:T(8,128)S(1)}, f32[256,256]{1,0:T(8,128)S(1)}) custom-call(s32[9]{0:T(128)S(1)} %compare_select_fusion.1.order_ref.refs_0_, f32[384,256]{1,0:T(8,128)S(1)} %choose.5.refs_1_.refs_3_, ...), custom_call_target="tpu_custom_call" | custom-call | flops 2415919104 | bytes 1048576 | tf_op jit(solution)/shard_map/raw_right/pallas_call | solution.py:134
  55.3 4.6 %collective-permute-done.7.b_ref = f32[384,256]{1,0:T(8,128)S(1)} collective-permute-done((f32[384,256]{1,0:T(8,128)S(1)}, f32[384,256]{1,0:T(8,128)S(1)}, u32[]{:S(2)}, u32[]{:S(2)}) %collective-permute-start.7) | collective-permute-done | bytes 393248 | tf_op jit(solution)/shard_map/ppermute | solution.py:476
  60.4 4.2 %raw_right.7 = (f32[2,256,512]{2,1,0:T(8,128)S(1)}, f32[2,256,512]{2,1,0:T(8,128)S(1)}, f32[2,256,512]{2,1,0:T(8,128)S(1)}, f32[2,256,512]{2,1,0:T(8,128)S(1)}, f32[256,256]{1,0:T(8,128)S(1)}) custom-call(s32[9]{0:T(128)S(1)} %compare_select_fusion.1.order_ref.refs_0_, f32[384,256]{1,0:T(8,128)S(1)} %choose.4.refs_1_.refs_4_, ...), custom_call_target="tpu_custom_call" | custom-call | flops 2415919104 | bytes 1048576 | tf_op jit(solution)/shard_map/raw_right/pallas_call | solution.py:134
  69.5 1.5 collective-permute-start.10
  72.4 1.4 collective-permute-start.12
  74.5 1.4 collective-permute-start.14
  77.1 11.5 %collective-permute-done.12.refs_1_ = f32[128,256]{1,0:T(8,128)S(1)} collective-permute-done((f32[128,256]{1,0:T(8,128)S(1)}, f32[128,256]{1,0:T(8,128)S(1)}, u32[]{:S(2)}, u32[]{:S(2)}) %collective-permute-start.12) | collective-permute-done | bytes 131104 | tf_op jit(solution)/shard_map/ppermute | solution.py:444
  88.6 2.4 %collective-permute-done.14.refs_3_ = f32[128,256]{1,0:T(8,128)S(1)} collective-permute-done((f32[128,256]{1,0:T(8,128)S(1)}, f32[128,256]{1,0:T(8,128)S(1)}, u32[]{:S(2)}, u32[]{:S(2)}) %collective-permute-start.14) | collective-permute-done | bytes 131104 | tf_op jit(solution)/shard_map/ppermute | solution.py:444
  93.1 43.5 %factor.1 = (f32[256,256]{1,0:T(8,128)S(1)}, f32[1024,256]{1,0:T(8,128)S(1)}, bf16[1024,768]{1,0:T(8,128)(2,1)S(1)}) custom-call(s32[9]{0:T(128)S(1)} %compare_select_fusion.1.order_ref.refs_0_, f32[128,256]{1,0:T(8,128)S(1)} %add.63.refs_1_, f32[128,256]{1,0:T(8,128)S(1)} %collective-permute-done.15.refs_2_, f32[384,256]{1,0:T(8,128)S(1)} %choose.5.refs_1_.refs_3_, ...), custom_call_target="tpu_custom_call" | custom-call | flops 1 | bytes 1 | tf_op jit(solution)/shard_map/factor/pallas_call | solution.py:246
  136.9 1.5 collective-permute-start.20
  138.4 1.3 squares.1.refs_0_
  141.0 1.5 collective-permute-start.19
  143.0 3.7 %new_momentum.3 = (f32[1024,4096]{1,0:T(8,128)}, bf16[768,512]{1,0:T(8,128)(2,1)S(1)}, bf16[768,512]{1,0:T(8,128)(2,1)S(1)}) custom-call(s32[9]{0:T(128)S(1)} %compare_select_fusion.1.order_ref.refs_0_, bf16[1024,768]{1,0:T(8,128)(2,1)S(1)} %get-tuple-element.85.refs_1_, f32[256,256]{1,0:T(8,128)S(1)} %get-tuple-element.92.inv_ref.refs_2_, ...), custom_call_target="tpu_custom_call" | custom-call | flops 1610612736 | bytes 4194304 | tf_op jit(solution)/shard_map/new_momentum/pallas_call | solution.py:330
  147.4 2.4 %collective-permute-start.25 = (f32[1,256,512]{2,1,0:T(8,128)S(1)}, f32[1,256,512]{2,1,0:T(8,128)S(1)}, u32[]{:S(2)}, u32[]{:S(2)}) collective-permute-start(f32[1,256,512]{2,1,0:T(8,128)S(1)} %collective-permute-done.20.refs_4_), channel_id=1, source_target_pairs={{0,8},{4,20},{8,0},{12,28},{16,24},{20,4},{24,16},{28,12},{1,9},{5... | collective-permute-start | bytes 1572872 | tf_op jit(solution)/shard_map/ppermute | solution.py:444
  149.8 1.5 collective-permute-start.22
  151.6 3.7 %new_momentum.4 = (f32[1024,4096]{1,0:T(8,128)}, bf16[768,512]{1,0:T(8,128)(2,1)S(1)}, bf16[768,512]{1,0:T(8,128)(2,1)S(1)}) custom-call(s32[9]{0:T(128)S(1)} %compare_select_fusion.1.order_ref.refs_0_, bf16[1024,768]{1,0:T(8,128)(2,1)S(1)} %get-tuple-element.85.refs_1_, ...), custom_call_target="tpu_custom_call", output_to_operand_aliasing={{0}: (6, {})} | custom-call | flops 1610612736 | bytes 4194304 | tf_op jit(solution)/shard_map/new_momentum/pallas_call | solution.py:330
  155.4 1.9 %collective-permute-done.25.refs_6_ = f32[1,256,512]{2,1,0:T(8,128)S(1)} collective-permute-done((f32[1,256,512]{2,1,0:T(8,128)S(1)}, f32[1,256,512]{2,1,0:T(8,128)S(1)}, u32[]{:S(2)}, u32[]{:S(2)}) %collective-permute-start.25) | collective-permute-done | bytes 524320 | tf_op jit(solution)/shard_map/ppermute | solution.py:444
  157.9 3.0 %collective-permute-start.29 = (f32[8,256]{1,0:T(8,128)S(1)}, f32[8,256]{1,0:T(8,128)S(1)}, u32[]{:S(2)}, u32[]{:S(2)}) collective-permute-start(f32[8,256]{1,0:T(8,128)S(1)} %add.67.refs_0_), channel_id=1, source_target_pairs={{0,2},{1,3},{2,0},{3,1},{4,6},{5,7},{6,4},{7,5},{8,10},{9,11},{10,... | collective-permute-start | bytes 24584 | tf_op jit(solution)/shard_map/ppermute | solution.py:535
  160.8 1.4 collective-permute-start.30
  162.5 3.8 %collective-permute-done.30.refs_3_ = f32[8,256]{1,0:T(8,128)S(1)} collective-permute-done((f32[8,256]{1,0:T(8,128)S(1)}, f32[8,256]{1,0:T(8,128)S(1)}, u32[]{:S(2)}, u32[]{:S(2)}) %collective-permute-start.30) | collective-permute-done | bytes 8224 | tf_op jit(solution)/shard_map/ppermute | solution.py:535
  166.5 5.8 %new_momentum.5 = (f32[1024,4096]{1,0:T(8,128)}, bf16[768,512]{1,0:T(8,128)(2,1)S(1)}, bf16[768,512]{1,0:T(8,128)(2,1)S(1)}, bf16[768,512]{1,0:T(8,128)(2,1)S(1)}, bf16[768,512]{1,0:T(8,128)(2,1)S(1)}) custom-call(s32[9]{0:T(128)S(1)} %compare_select_fusion.1.order_ref.refs_0_, ...), custom_call_target="tpu_custom_call", output_to_operand_aliasing={{0}: (8, {})} | custom-call | flops 3221225472 | bytes 8388608 | tf_op jit(solution)/shard_map/new_momentum/pallas_call | solution.py:330
  172.3 8.6 %update.1 = f32[1024,4096]{1,0:T(8,128)} custom-call(s32[9]{0:T(128)S(1)} %compare_select_fusion.1.order_ref.refs_0_, bf16[1024,768]{1,0:T(8,128)(2,1)S(1)} %operand.1.refs_1_, bf16[768,512]{1,0:T(8,128)(2,1)S(1)} %get-tuple-element.114.refs_2_, bf16[768,512]{1,0:T(8,128)(2,1)S(1)} %get-tuple-element.115.refs_3_, ...), custom_call_target="tpu_custom_call" | custom-call | flops 6442450944 | bytes 16777216 | tf_op jit(solution)/shard_map/update/pallas_call | solution.py:370
  (67 shorter events, 21.5 us)
Async XLA Ops:
  10.6 14.4 %collective-permute-start = (f32[384,256]{1,0:T(8,128)S(1)}, f32[384,256]{1,0:T(8,128)S(1)}, u32[]{:S(2)}, u32[]{:S(2)}) collective-permute-start(f32[384,256]{1,0:T(8,128)S(1)} %left.3.refs_0_), channel_id=1, source_target_pairs={{0,1},{3,2},{4,5},{7,6},{8,9},{11,10},{12,13},{15,14},{16,17},{19,... | collective-permute-start | bytes 1179656 | tf_op jit(solution)/shard_map/ppermute | solution.py:470
  18.3 16.6 %collective-permute-start.5 = (f32[384,256]{1,0:T(8,128)S(1)}, f32[384,256]{1,0:T(8,128)S(1)}, u32[]{:S(2)}, u32[]{:S(2)}) collective-permute-start(f32[384,256]{1,0:T(8,128)S(1)} %left.5.refs_0_), channel_id=1, source_target_pairs={{0,1},{3,2},{4,5},{7,6},{8,9},{11,10},{12,13},{15,14},{16,17},{19,... | collective-permute-start | bytes 1179656 | tf_op jit(solution)/shard_map/ppermute | solution.py:470
  25.1 13.8 %collective-permute-start.2 = (f32[384,256]{1,0:T(8,128)S(1)}, f32[384,256]{1,0:T(8,128)S(1)}, u32[]{:S(2)}, u32[]{:S(2)}) collective-permute-start(f32[384,256]{1,0:T(8,128)S(1)} %add.55.refs_0_), channel_id=1, source_target_pairs={{1,2},{2,1},{5,6},{6,5},{9,10},{10,9},{13,14},{14,13},{17,18},{18,... | collective-permute-start | bytes 1179656 | tf_op jit(solution)/shard_map/ppermute | solution.py:473
  27.7 11.1 %collective-permute-start.1 = (f32[256,256]{1,0:T(8,128)S(1)}, f32[256,256]{1,0:T(8,128)S(1)}, u32[]{:S(2)}, u32[]{:S(2)}) collective-permute-start(f32[256,256]{1,0:T(8,128)S(1)} %left.4.refs_0_), channel_id=1, source_target_pairs={{0,1},{3,2},{4,5},{7,6},{8,9},{11,10},{12,13},{15,14},{16,17},{19,... | collective-permute-start | bytes 786440 | tf_op jit(solution)/shard_map/ppermute | solution.py:470
  35.0 5.9 %collective-permute-start.6 = (f32[384,256]{1,0:T(8,128)S(1)}, f32[384,256]{1,0:T(8,128)S(1)}, u32[]{:S(2)}, u32[]{:S(2)}) collective-permute-start(f32[384,256]{1,0:T(8,128)S(1)} %add.59.refs_0_), channel_id=1, source_target_pairs={{1,2},{2,1},{5,6},{6,5},{9,10},{10,9},{13,14},{14,13},{17,18},{18,... | collective-permute-start | bytes 1179656 | tf_op jit(solution)/shard_map/ppermute | solution.py:473
  38.9 11.7 %collective-permute-start.8 = (f32[384,256]{1,0:T(8,128)S(1)}, f32[384,256]{1,0:T(8,128)S(1)}, u32[]{:S(2)}, u32[]{:S(2)}) collective-permute-start(f32[384,256]{1,0:T(8,128)S(1)} %add.57.a_ref), channel_id=1, source_target_pairs={{1,0},{2,3},{5,4},{6,7},{9,8},{10,11},{13,12},{14,15},{17,16},{18,... | collective-permute-start | bytes 1179656 | tf_op jit(solution)/shard_map/ppermute | solution.py:476
  40.2 2.1 %collective-permute-start.3 = (f32[256,256]{1,0:T(8,128)S(1)}, f32[256,256]{1,0:T(8,128)S(1)}, u32[]{:S(2)}, u32[]{:S(2)}) collective-permute-start(f32[256,256]{1,0:T(8,128)S(1)} %add.56.refs_0_), channel_id=1, source_target_pairs={{1,2},{2,1},{5,6},{6,5},{9,10},{10,9},{13,14},{14,13},{17,18},{18,... | collective-permute-start | bytes 786440 | tf_op jit(solution)/shard_map/ppermute | solution.py:473
  40.9 18.9 %collective-permute-start.7 = (f32[384,256]{1,0:T(8,128)S(1)}, f32[384,256]{1,0:T(8,128)S(1)}, u32[]{:S(2)}, u32[]{:S(2)}) collective-permute-start(f32[384,256]{1,0:T(8,128)S(1)} %add.60.a_ref), channel_id=1, source_target_pairs={{1,0},{2,3},{5,4},{6,7},{9,8},{10,11},{13,12},{14,15},{17,16},{18,... | collective-permute-start | bytes 1179656 | tf_op jit(solution)/shard_map/ppermute | solution.py:476
  42.3 22.3 %collective-permute-start.4 = (f32[256,256]{1,0:T(8,128)S(1)}, f32[256,256]{1,0:T(8,128)S(1)}, u32[]{:S(2)}, u32[]{:S(2)}) collective-permute-start(f32[256,256]{1,0:T(8,128)S(1)} %add.58.a_ref), channel_id=1, source_target_pairs={{1,0},{2,3},{5,4},{6,7},{9,8},{10,11},{13,12},{14,15},{17,16},{18,... | collective-permute-start | bytes 786440 | tf_op jit(solution)/shard_map/ppermute | solution.py:476
  66.5 2.9 %collective-permute-start.9 = (f32[2,256,512]{2,1,0:T(8,128)S(1)}, f32[2,256,512]{2,1,0:T(8,128)S(1)}, u32[]{:S(2)}, u32[]{:S(2)}) collective-permute-start(f32[2,256,512]{2,1,0:T(8,128)S(1)} %raw_right.8), channel_id=1, source_target_pairs={{0,4},{4,0},{8,12},{12,8},{16,20},{20,16},{24,28},{28,24},{1,5},{5... | collective-permute-start | bytes 3145736 | tf_op jit(solution)/shard_map/ppermute | solution.py:444
  67.5 1.8 %collective-permute-start.11 = (f32[128,256]{1,0:T(8,128)S(1)}, f32[128,256]{1,0:T(8,128)S(1)}, u32[]{:S(2)}, u32[]{:S(2)}) collective-permute-start(f32[128,256]{1,0:T(8,128)S(1)} %get-tuple-element.122), channel_id=1, source_target_pairs={{0,4},{4,0},{8,12},{12,8},{16,20},{20,16},{24,28},{28,24},{1,5},{5... | collective-permute-start | bytes 393224 | tf_op jit(solution)/shard_map/ppermute | solution.py:444
  69.5 21.5 %collective-permute-start.10 = (f32[2,256,512]{2,1,0:T(8,128)S(1)}, f32[2,256,512]{2,1,0:T(8,128)S(1)}, u32[]{:S(2)}, u32[]{:S(2)}) collective-permute-start(f32[2,256,512]{2,1,0:T(8,128)S(1)} %add.61), channel_id=1, source_target_pairs={{0,8},{4,20},{8,0},{12,28},{16,24},{20,4},{24,16},{28,12},{1,9},{5... | collective-permute-start | bytes 3145736 | tf_op jit(solution)/shard_map/ppermute | solution.py:444
  72.3 18.7 %collective-permute-start.16 = (f32[2,256,512]{2,1,0:T(8,128)S(1)}, f32[2,256,512]{2,1,0:T(8,128)S(1)}, u32[]{:S(2)}, u32[]{:S(2)}) collective-permute-start(f32[2,256,512]{2,1,0:T(8,128)S(1)} %raw_right.11), channel_id=1, source_target_pairs={{0,4},{4,0},{8,12},{12,8},{16,20},{20,16},{24,28},{28,24},{1,5},{5... | collective-permute-start | bytes 3145736 | tf_op jit(solution)/shard_map/ppermute | solution.py:444
  72.4 16.2 %collective-permute-start.12 = (f32[128,256]{1,0:T(8,128)S(1)}, f32[128,256]{1,0:T(8,128)S(1)}, u32[]{:S(2)}, u32[]{:S(2)}) collective-permute-start(f32[128,256]{1,0:T(8,128)S(1)} %add.62.refs_0_), channel_id=1, source_target_pairs={{0,8},{4,20},{8,0},{12,28},{16,24},{20,4},{24,16},{28,12},{1,9},{5... | collective-permute-start | bytes 393224 | tf_op jit(solution)/shard_map/ppermute | solution.py:444
  73.7 14.9 %collective-permute-start.13 = (f32[128,256]{1,0:T(8,128)S(1)}, f32[128,256]{1,0:T(8,128)S(1)}, u32[]{:S(2)}, u32[]{:S(2)}) collective-permute-start(f32[128,256]{1,0:T(8,128)S(1)} %add.62.refs_0_), channel_id=1, source_target_pairs={{0,16},{4,12},{8,24},{12,4},{16,0},{20,28},{24,8},{28,20},{1,17},{... | collective-permute-start | bytes 393224 | tf_op jit(solution)/shard_map/ppermute | solution.py:444
  74.5 16.5 %collective-permute-start.14 = (f32[128,256]{1,0:T(8,128)S(1)}, f32[128,256]{1,0:T(8,128)S(1)}, u32[]{:S(2)}, u32[]{:S(2)}) collective-permute-start(f32[128,256]{1,0:T(8,128)S(1)} %add.62.refs_0_), channel_id=1, source_target_pairs={{0,24},{4,28},{8,16},{12,20},{16,8},{20,12},{24,0},{28,4},{1,25},{... | collective-permute-start | bytes 393224 | tf_op jit(solution)/shard_map/ppermute | solution.py:444
  91.2 45.5 %collective-permute-start.17 = (f32[1,256,512]{2,1,0:T(8,128)S(1)}, f32[1,256,512]{2,1,0:T(8,128)S(1)}, u32[]{:S(2)}, u32[]{:S(2)}) collective-permute-start(f32[1,256,512]{2,1,0:T(8,128)S(1)} %get-tuple-element.90), channel_id=1, source_target_pairs={{0,16},{4,12},{8,24},{12,4},{16,0},{20,28},{24,8},{28,20},{1,17},{... | collective-permute-start | bytes 1572872 | tf_op jit(solution)/shard_map/ppermute | solution.py:444
  91.7 1.3 collective-permute-start.15
  136.7 6.3 %collective-permute-start.21 = (f32[1,256,512]{2,1,0:T(8,128)S(1)}, f32[1,256,512]{2,1,0:T(8,128)S(1)}, u32[]{:S(2)}, u32[]{:S(2)}) collective-permute-start(f32[1,256,512]{2,1,0:T(8,128)S(1)} %add.64.raw_ref.refs_4_), channel_id=1, source_target_pairs={{0,4},{4,0},{8,12},{12,8},{16,20},{20,16},{24,28},{28,24},{1,5},{5... | collective-permute-start | bytes 1572872 | tf_op jit(solution)/shard_map/ppermute | solution.py:444
  136.9 10.5 %collective-permute-start.20 = (f32[1,256,512]{2,1,0:T(8,128)S(1)}, f32[1,256,512]{2,1,0:T(8,128)S(1)}, u32[]{:S(2)}, u32[]{:S(2)}) collective-permute-start(f32[1,256,512]{2,1,0:T(8,128)S(1)} %add.64.raw_ref.refs_4_), channel_id=1, source_target_pairs={{0,16},{4,12},{8,24},{12,4},{16,0},{20,28},{24,8},{28,20},{1,17},{... | collective-permute-start | bytes 1572872 | tf_op jit(solution)/shard_map/ppermute | solution.py:444
  139.8 1.2 collective-permute-start.18
  141.0 5.7 %collective-permute-start.19 = (f32[8,256]{1,0:T(8,128)S(1)}, f32[8,256]{1,0:T(8,128)S(1)}, u32[]{:S(2)}, u32[]{:S(2)}) collective-permute-start(f32[8,256]{1,0:T(8,128)S(1)} %add.65.refs_0_), channel_id=1, source_target_pairs={{0,8},{4,20},{8,0},{12,28},{16,24},{20,4},{24,16},{28,12},{1,9},{5... | collective-permute-start | bytes 24584 | tf_op jit(solution)/shard_map/ppermute | solution.py:444
  142.5 9.2 %collective-permute-start.24 = (f32[1,256,512]{2,1,0:T(8,128)S(1)}, f32[1,256,512]{2,1,0:T(8,128)S(1)}, u32[]{:S(2)}, u32[]{:S(2)}) collective-permute-start(f32[1,256,512]{2,1,0:T(8,128)S(1)} %add.64.raw_ref.refs_4_), channel_id=1, source_target_pairs={{0,8},{4,20},{8,0},{12,28},{16,24},{20,4},{24,16},{28,12},{1,9},{5... | collective-permute-start | bytes 1572872 | tf_op jit(solution)/shard_map/ppermute | solution.py:444
  147.4 4.2 %collective-permute-start.23 = (f32[1,256,512]{2,1,0:T(8,128)S(1)}, f32[1,256,512]{2,1,0:T(8,128)S(1)}, u32[]{:S(2)}, u32[]{:S(2)}) collective-permute-start(f32[1,256,512]{2,1,0:T(8,128)S(1)} %collective-permute-done.20.refs_4_), channel_id=1, source_target_pairs={{0,4},{4,0},{8,12},{12,8},{16,20},{20,16},{24,28},{28,24},{1,5},{5... | collective-permute-start | bytes 1572872 | tf_op jit(solution)/shard_map/ppermute | solution.py:444
  147.4 9.9 %collective-permute-start.25 = (f32[1,256,512]{2,1,0:T(8,128)S(1)}, f32[1,256,512]{2,1,0:T(8,128)S(1)}, u32[]{:S(2)}, u32[]{:S(2)}) collective-permute-start(f32[1,256,512]{2,1,0:T(8,128)S(1)} %collective-permute-done.20.refs_4_), channel_id=1, source_target_pairs={{0,8},{4,20},{8,0},{12,28},{16,24},{20,4},{24,16},{28,12},{1,9},{5... | collective-permute-start | bytes 1572872 | tf_op jit(solution)/shard_map/ppermute | solution.py:444
  149.8 5.6 %collective-permute-start.22 = (f32[8,256]{1,0:T(8,128)S(1)}, f32[8,256]{1,0:T(8,128)S(1)}, u32[]{:S(2)}, u32[]{:S(2)}) collective-permute-start(f32[8,256]{1,0:T(8,128)S(1)} %add.66.refs_0_), channel_id=1, source_target_pairs={{0,16},{4,12},{8,24},{12,4},{16,0},{20,28},{24,8},{28,20},{1,17},{... | collective-permute-start | bytes 24584 | tf_op jit(solution)/shard_map/ppermute | solution.py:444
  157.3 9.1 %collective-permute-start.26 = (f32[1,256,512]{2,1,0:T(8,128)S(1)}, f32[1,256,512]{2,1,0:T(8,128)S(1)}, u32[]{:S(2)}, u32[]{:S(2)}) collective-permute-start(f32[1,256,512]{2,1,0:T(8,128)S(1)} %collective-permute-done.24.refs_4_), channel_id=1, source_target_pairs={{0,4},{4,0},{8,12},{12,8},{16,20},{20,16},{24,28},{28,24},{1,5},{5... | collective-permute-start | bytes 1572872 | tf_op jit(solution)/shard_map/ppermute | solution.py:444
  157.5 9.0 %collective-permute-start.27 = (f32[1,256,512]{2,1,0:T(8,128)S(1)}, f32[1,256,512]{2,1,0:T(8,128)S(1)}, u32[]{:S(2)}, u32[]{:S(2)}) collective-permute-start(f32[1,256,512]{2,1,0:T(8,128)S(1)} %collective-permute-done.25.refs_6_), channel_id=1, source_target_pairs={{0,4},{4,0},{8,12},{12,8},{16,20},{20,16},{24,28},{28,24},{1,5},{5... | collective-permute-start | bytes 1572872 | tf_op jit(solution)/shard_map/ppermute | solution.py:444
  157.9 4.4 %collective-permute-start.28 = (f32[8,256]{1,0:T(8,128)S(1)}, f32[8,256]{1,0:T(8,128)S(1)}, u32[]{:S(2)}, u32[]{:S(2)}) collective-permute-start(f32[8,256]{1,0:T(8,128)S(1)} %add.67.refs_0_), channel_id=1, source_target_pairs={{0,1},{1,0},{2,3},{3,2},{4,5},{5,4},{6,7},{7,6},{8,9},{9,8},{10,11... | collective-permute-start | bytes 24584 | tf_op jit(solution)/shard_map/ppermute | solution.py:535
  157.9 4.6 %collective-permute-start.29 = (f32[8,256]{1,0:T(8,128)S(1)}, f32[8,256]{1,0:T(8,128)S(1)}, u32[]{:S(2)}, u32[]{:S(2)}) collective-permute-start(f32[8,256]{1,0:T(8,128)S(1)} %add.67.refs_0_), channel_id=1, source_target_pairs={{0,2},{1,3},{2,0},{3,1},{4,6},{5,7},{6,4},{7,5},{8,10},{9,11},{10,... | collective-permute-start | bytes 24584 | tf_op jit(solution)/shard_map/ppermute | solution.py:535
  160.8 5.4 %collective-permute-start.30 = (f32[8,256]{1,0:T(8,128)S(1)}, f32[8,256]{1,0:T(8,128)S(1)}, u32[]{:S(2)}, u32[]{:S(2)}) collective-permute-start(f32[8,256]{1,0:T(8,128)S(1)} %add.67.refs_0_), channel_id=1, source_target_pairs={{0,3},{1,2},{2,1},{3,0},{4,7},{5,6},{6,5},{7,4},{8,11},{9,10},{10,... | collective-permute-start | bytes 24584 | tf_op jit(solution)/shard_map/ppermute | solution.py:535

commit v3 on v2

--- a/solution.py
+++ b/solution.py
@@ -342,43 +342,63 @@
     return [outs[0]], list(outs[1:])
 
 
-def update_kernel(places, chained, order_ref, operand_ref, *refs):
+def finish_kernel(places, done, order_ref, operand_ref, scaled_ref, inv_ref, m_ref, *refs):
     count = len(places)
-    right_refs, (out_hbm, out_ref, sem) = refs[:count], refs[count + chained :]
-    _, rows, width = out_ref.shape
+    raw_refs, right_refs, refs = refs[:count], refs[count : count + len(done)], refs[count + len(done) + 1 :]
+    new_hbm, update_hbm, right_ref, out_ref, sem = refs
+    buffers, rows, width = out_ref.shape
     parts = sem.shape[1]
     tile = rows // parts
+    inverse = three(*split(inv_ref[...]), 1)
     copies = []
-    for s, right_ref in enumerate(right_refs):
-        span = pl.ds(pl.multiple_of(order_ref[places[s]] * width, width), width)
-        right = right_ref[...]
+
+    def store(place, lhs_ref, ref, out_hbm, added):
+        slot = len(copies) % buffers
+        if len(copies) >= buffers:
+            for copy in copies[-buffers]:
+                copy.wait()
+        span = pl.ds(pl.multiple_of(order_ref[place] * width, width), width)
+        right = ref[...]
+        copies.append([])
         for part in range(parts):
             at = pl.ds(part * tile, tile)
-            out_ref[s, at] = dot(operand_ref[at, :], right)
-            copies.append(pltpu.make_async_copy(out_ref.at[s, at], out_hbm.at[at, span], sem.at[s, part]))
-            copies[-1].start()
-    for copy in copies:
-        copy.wait()
-
-
-def update_chunks(order, places, operand, rights, before, cols):
-    rows = operand.shape[0]
-    width = rights[0].shape[1]
-    rank = rights[0].shape[0] // 3
-    count, parts = len(rights), 4
-    return [
-        pl.pallas_call(
-            lambda *refs: update_kernel(places, len(before), *refs),
-            in_specs=[SMEM] + [VMEM] * (1 + count) + [HBM] * len(before),
-            out_specs=HBM,
-            out_shape=jax.ShapeDtypeStruct((rows, cols), F32),
-            scratch_shapes=[pltpu.VMEM((count, rows, width), F32), pltpu.SemaphoreType.DMA((count, parts))],
-            input_output_aliases={2 + count: 0} if before else {},
-            compiler_params=params(),
-            cost_estimate=cost(6 * count * rows * rank * width, 4 * count * rows * width),
-            name="update",
-        )(order, operand, *rights, *before)
-    ]
+            total = dot(lhs_ref[at, :], right)
+            out_ref[slot, at] = m_ref[at, span] + total if added else total
+            copies[-1].append(pltpu.make_async_copy(out_ref.at[slot, at], out_hbm.at[at, span], sem.at[slot, part]))
+            copies[-1][-1].start()
+
+    for n, place in enumerate(places):
+        right = dot(inverse, three_other(*split(raw_refs[n][0]), 0))
+        right_ref[n % 2] = three_other(*split(right), 0)
+        store(place, operand_ref, right_ref.at[n % 2], new_hbm, True)
+        store(place, scaled_ref, right_ref.at[n % 2], update_hbm, False)
+        if n < len(done):
+            store(done[n], scaled_ref, right_refs[n], update_hbm, False)
+    for job in copies[-buffers:]:
+        for copy in job:
+            copy.wait()
+
+
+def finish(order, places, done, operand, scaled, inverse, momentum, raws, rights, new):
+    rows, cols = momentum.shape
+    _, rank, width = raws[0].shape
+    count, parts, buffers = len(raws), 4, 6
+    whole = jax.ShapeDtypeStruct((rows, cols), F32)
+    return pl.pallas_call(
+        lambda *refs: finish_kernel(places, done, *refs),
+        in_specs=[SMEM] + [VMEM] * (4 + count + len(rights)) + [HBM],
+        out_specs=[HBM, HBM],
+        out_shape=[whole, whole],
+        scratch_shapes=[
+            pltpu.VMEM((2, 3 * rank, width), BF16),
+            pltpu.VMEM((buffers, rows, width), F32),
+            pltpu.SemaphoreType.DMA((buffers, parts)),
+        ],
+        input_output_aliases={5 + count + len(rights): 0},
+        compiler_params=params(),
+        cost_estimate=cost(6 * 3 * count * rows * rank * width, 4 * 3 * count * rows * width),
+        name="finish",
+    )(order, operand, scaled, inverse, in_vmem(momentum), *raws, *rights, new)
 
 
 def add_kernel(*refs):
@@ -533,13 +553,11 @@
     pair_2, pair_3 = along(chunk_2, PAIR), along(chunk_3, PAIR)
     squares = add(squares, got)
     gots = [lax.ppermute(squares, "col", [(c, c ^ d) for c in range(LINE)]) for d in range(1, LINE)]
-    *gots, new[0] = together(*gots, new[0])
+    scaled = update_operand([squares] + gots, orth, scale)
     raws = [chunk_2, pair_2, chunk_3, pair_3]
-    new, right = new_chunks(order, (2, 6, 3, 7), operand, inverse, raws, resident, new)
-    rights += right
-    scaled = update_operand([squares] + gots, orth, scale)
-    update = update_chunks(order, (0, 4, 1, 5, 2, 6, 3, 7), scaled, rights, [], cols)
-    return new[0], update[0]
+    return tuple(
+        finish(order, (2, 6, 3, 7), (0, 4, 1, 5), operand, scaled, inverse, resident, raws, rights, new[0])
+    )
 
 
 def general(momentum, right_factor, scale):

time: 181 us -> 180 us (level)
    pallas_call x3 -> x2, Pallas kernels: 13.2 us -> 7.4 us  [new_chunks(): pl.pallas_call(lambda *refs: new_kernel(places, len(before), *refs), in_s...]
    pallas_call x1, Pallas kernels: 8.58 us -> 14 us  [finish(): pl.pallas_call(lambda *refs: finish_kernel(places, done, *refs), in_specs...]
where the time goes in v3:
time: 180 us; the launch traced here: 179 us
  Pallas kernels  97.5 us (54%)
  waiting for transfers between devices  42.9 us (24%)
  starting transfers between devices  37.7 us (21%)
    pallas_call x1, Pallas kernels, factor(): pl.pallas_call(lambda *refs: factor_kernel(len(lefts), RING // 2, *refs),...  43.5 us
    ppermute x19, waiting for transfers between devices, along(): return lax.ppermute(x, 'row', pairs)  20.5 us
    pallas_call x1, Pallas kernels, finish(): pl.pallas_call(lambda *refs: finish_kernel(places, done, *refs), in_specs...  14 us
    ppermute x19, starting transfers between devices, along(): return lax.ppermute(x, 'row', pairs)  13.7 us
    ppermute x3, starting transfers between devices, inward(): return lax.ppermute(x, 'col', [(0, 1), (3, 2)])  13.5 us
    pallas_call x6, Pallas kernels, raw_pieces(): pl.pallas_call(lambda *refs: raw_kernel(at, groups, bool(before), with_gr...  13.1 us
    ppermute x3, waiting for transfers between devices, outward(): return lax.ppermute(x, 'col', [(1, 0), (2, 3)])  11.4 us
    ppermute x3, waiting for transfers between devices, inward(): return lax.ppermute(x, 'col', [(0, 1), (3, 2)])  8.46 us
  transfers between devices with their start and end apart: 31, of which 13 were waited for; matrix products, arithmetic and copies ran while one was open for 0% of the time, Pallas kernels for 40%

profile of v3, /device:TPU:0, one launch (start us, length us, event | category | flops | bytes accessed | tf_op | source)
XLA Modules:
  0.0 179.4 jit_solution(8032909387318361163)
XLA Ops:
  0.7 7.1 %fetch.1 = (f32[1024,4096]{1,0:T(8,128)S(1)}, bf16[4096,256]{1,0:T(8,128)(2,1)S(1)}, bf16[4096,256]{1,0:T(8,128)(2,1)S(1)}) custom-call(f32[1024,4096]{1,0:T(8,128)} %m_hbm.1, f32[4096,256]{1,0:T(8,128)} %q_hbm), custom_call_target="tpu_custom_call" | custom-call | flops 1048576 | bytes 20971520 | tf_op jit(solution)/shard_map/fetch/pallas_call | solution.py:72
  7.8 2.8 %left.3.refs_0_ = f32[384,256]{1,0:T(8,128)S(1)} custom-call(f32[1024,4096]{1,0:T(8,128)S(1)} %get-tuple-element.55.refs_0_.refs_2_.refs_3_.refs_4_, bf16[4096,256]{1,0:T(8,128)(2,1)S(1)} %get-tuple-element.58.refs_1_, bf16[4096,256]{1,0:T(8,128)(2,1)S(1)} %get-tuple-element.57.refs_2_), custom_call_target="tpu_custom_call" | custom-call | flops 2415919104 | bytes 1048576 | tf_op jit(solution)/shard_map/left/pallas_call | solution.py:101
  10.6 5.0 %collective-permute-start = (f32[384,256]{1,0:T(8,128)S(1)}, f32[384,256]{1,0:T(8,128)S(1)}, u32[]{:S(2)}, u32[]{:S(2)}) collective-permute-start(f32[384,256]{1,0:T(8,128)S(1)} %left.3.refs_0_), channel_id=1, source_target_pairs={{0,1},{3,2},{4,5},{7,6},{8,9},{11,10},{12,13},{15,14},{16,17},{19,... | collective-permute-start | bytes 1179656 | tf_op jit(solution)/shard_map/ppermute | solution.py:490
  15.5 2.8 %left.5.refs_0_ = f32[384,256]{1,0:T(8,128)S(1)} custom-call(f32[1024,4096]{1,0:T(8,128)S(1)} %get-tuple-element.55.refs_0_.refs_2_.refs_3_.refs_4_, bf16[4096,256]{1,0:T(8,128)(2,1)S(1)} %get-tuple-element.58.refs_1_, bf16[4096,256]{1,0:T(8,128)(2,1)S(1)} %get-tuple-element.57.refs_2_), custom_call_target="tpu_custom_call" | custom-call | flops 2415919104 | bytes 1048576 | tf_op jit(solution)/shard_map/left/pallas_call | solution.py:101
  18.3 1.3 collective-permute-start.5
  19.7 5.4 %collective-permute-done.refs_1_ = f32[384,256]{1,0:T(8,128)S(1)} collective-permute-done((f32[384,256]{1,0:T(8,128)S(1)}, f32[384,256]{1,0:T(8,128)S(1)}, u32[]{:S(2)}, u32[]{:S(2)}) %collective-permute-start) | collective-permute-done | bytes 393248 | tf_op jit(solution)/shard_map/ppermute | solution.py:490
  25.8 2.0 %left.4.refs_0_ = f32[256,256]{1,0:T(8,128)S(1)} custom-call(f32[1024,4096]{1,0:T(8,128)S(1)} %get-tuple-element.55.refs_0_.refs_2_.refs_3_.refs_4_, bf16[4096,256]{1,0:T(8,128)(2,1)S(1)} %get-tuple-element.58.refs_1_, bf16[4096,256]{1,0:T(8,128)(2,1)S(1)} %get-tuple-element.57.refs_2_), custom_call_target="tpu_custom_call" | custom-call | flops 1610612736 | bytes 1048576 | tf_op jit(solution)/shard_map/left/pallas_call | solution.py:101
  27.7 7.2 %collective-permute-start.1 = (f32[256,256]{1,0:T(8,128)S(1)}, f32[256,256]{1,0:T(8,128)S(1)}, u32[]{:S(2)}, u32[]{:S(2)}) collective-permute-start(f32[256,256]{1,0:T(8,128)S(1)} %left.4.refs_0_), channel_id=1, source_target_pairs={{0,1},{3,2},{4,5},{7,6},{8,9},{11,10},{12,13},{15,14},{16,17},{19,... | collective-permute-start | bytes 786440 | tf_op jit(solution)/shard_map/ppermute | solution.py:490
  35.7 3.1 %collective-permute-done.1.refs_1_ = f32[256,256]{1,0:T(8,128)S(1)} collective-permute-done((f32[256,256]{1,0:T(8,128)S(1)}, f32[256,256]{1,0:T(8,128)S(1)}, u32[]{:S(2)}, u32[]{:S(2)}) %collective-permute-start.1) | collective-permute-done | bytes 262176 | tf_op jit(solution)/shard_map/ppermute | solution.py:490
  38.9 1.3 collective-permute-start.8
  40.9 1.3 collective-permute-start.7
  42.3 1.5 collective-permute-start.4
  43.8 6.8 %collective-permute-done.8.b_ref = f32[384,256]{1,0:T(8,128)S(1)} collective-permute-done((f32[384,256]{1,0:T(8,128)S(1)}, f32[384,256]{1,0:T(8,128)S(1)}, u32[]{:S(2)}, u32[]{:S(2)}) %collective-permute-start.8) | collective-permute-done | bytes 393248 | tf_op jit(solution)/shard_map/ppermute | solution.py:496
  51.2 4.1 %raw_right.6 = (f32[2,256,512]{2,1,0:T(8,128)S(1)}, f32[2,256,512]{2,1,0:T(8,128)S(1)}, f32[2,256,512]{2,1,0:T(8,128)S(1)}, f32[2,256,512]{2,1,0:T(8,128)S(1)}, f32[256,256]{1,0:T(8,128)S(1)}) custom-call(s32[9]{0:T(128)S(1)} %compare_select_fusion.1.order_ref.refs_0_, f32[384,256]{1,0:T(8,128)S(1)} %choose.5.refs_1_.refs_3_, ...), custom_call_target="tpu_custom_call" | custom-call | flops 2415919104 | bytes 1048576 | tf_op jit(solution)/shard_map/raw_right/pallas_call | solution.py:134
  55.3 4.6 %collective-permute-done.7.b_ref = f32[384,256]{1,0:T(8,128)S(1)} collective-permute-done((f32[384,256]{1,0:T(8,128)S(1)}, f32[384,256]{1,0:T(8,128)S(1)}, u32[]{:S(2)}, u32[]{:S(2)}) %collective-permute-start.7) | collective-permute-done | bytes 393248 | tf_op jit(solution)/shard_map/ppermute | solution.py:496
  60.4 4.2 %raw_right.7 = (f32[2,256,512]{2,1,0:T(8,128)S(1)}, f32[2,256,512]{2,1,0:T(8,128)S(1)}, f32[2,256,512]{2,1,0:T(8,128)S(1)}, f32[2,256,512]{2,1,0:T(8,128)S(1)}, f32[256,256]{1,0:T(8,128)S(1)}) custom-call(s32[9]{0:T(128)S(1)} %compare_select_fusion.1.order_ref.refs_0_, f32[384,256]{1,0:T(8,128)S(1)} %choose.4.refs_1_.refs_4_, ...), custom_call_target="tpu_custom_call" | custom-call | flops 2415919104 | bytes 1048576 | tf_op jit(solution)/shard_map/raw_right/pallas_call | solution.py:134
  69.5 1.5 collective-permute-start.10
  72.4 1.6 collective-permute-start.14
  77.1 12.4 %collective-permute-done.14.refs_3_ = f32[128,256]{1,0:T(8,128)S(1)} collective-permute-done((f32[128,256]{1,0:T(8,128)S(1)}, f32[128,256]{1,0:T(8,128)S(1)}, u32[]{:S(2)}, u32[]{:S(2)}) %collective-permute-start.14) | collective-permute-done | bytes 131104 | tf_op jit(solution)/shard_map/ppermute | solution.py:464
  90.3 1.5 collective-permute-start.17
  91.8 1.3 collective-permute-done.15.refs_2_
  93.1 43.5 %factor.1 = (f32[256,256]{1,0:T(8,128)S(1)}, f32[1024,256]{1,0:T(8,128)S(1)}, bf16[1024,768]{1,0:T(8,128)(2,1)S(1)}) custom-call(s32[9]{0:T(128)S(1)} %compare_select_fusion.1.order_ref.refs_0_, f32[128,256]{1,0:T(8,128)S(1)} %add.63.refs_1_, f32[128,256]{1,0:T(8,128)S(1)} %collective-permute-done.15.refs_2_, f32[384,256]{1,0:T(8,128)S(1)} %choose.5.refs_1_.refs_3_, ...), custom_call_target="tpu_custom_call" | custom-call | flops 1 | bytes 1 | tf_op jit(solution)/shard_map/factor/pallas_call | solution.py:246
  137.5 1.3 squares.1.refs_0_
  142.8 3.7 %new_momentum.2 = (f32[1024,4096]{1,0:T(8,128)}, bf16[768,512]{1,0:T(8,128)(2,1)S(1)}, bf16[768,512]{1,0:T(8,128)(2,1)S(1)}) custom-call(s32[9]{0:T(128)S(1)} %compare_select_fusion.1.order_ref.refs_0_, bf16[1024,768]{1,0:T(8,128)(2,1)S(1)} %get-tuple-element.76.refs_1_, f32[256,256]{1,0:T(8,128)S(1)} %get-tuple-element.83.inv_ref.refs_2_.refs_3_, ...), custom_call_target="tpu_custom_call" | custom-call | flops 1610612736 | bytes 4194304 | tf_op jit(solution)/shard_map/new_momentum/pallas_call | solution.py:330
  146.5 1.9 %collective-permute-done.20.refs_4_ = f32[1,256,512]{2,1,0:T(8,128)S(1)} collective-permute-done((f32[1,256,512]{2,1,0:T(8,128)S(1)}, f32[1,256,512]{2,1,0:T(8,128)S(1)}, u32[]{:S(2)}, u32[]{:S(2)}) %collective-permute-start.20) | collective-permute-done | bytes 524320 | tf_op jit(solution)/shard_map/ppermute | solution.py:464
  148.4 1.5 collective-permute-start.25
  151.2 3.7 %new_momentum.3 = (f32[1024,4096]{1,0:T(8,128)}, bf16[768,512]{1,0:T(8,128)(2,1)S(1)}, bf16[768,512]{1,0:T(8,128)(2,1)S(1)}) custom-call(s32[9]{0:T(128)S(1)} %compare_select_fusion.1.order_ref.refs_0_, bf16[1024,768]{1,0:T(8,128)(2,1)S(1)} %get-tuple-element.76.refs_1_, ...), custom_call_target="tpu_custom_call", output_to_operand_aliasing={{0}: (6, {})} | custom-call | flops 1610612736 | bytes 4194304 | tf_op jit(solution)/shard_map/new_momentum/pallas_call | solution.py:330
  154.9 2.6 %collective-permute-done.25.refs_7_ = f32[1,256,512]{2,1,0:T(8,128)S(1)} collective-permute-done((f32[1,256,512]{2,1,0:T(8,128)S(1)}, f32[1,256,512]{2,1,0:T(8,128)S(1)}, u32[]{:S(2)}, u32[]{:S(2)}) %collective-permute-start.25) | collective-permute-done | bytes 524320 | tf_op jit(solution)/shard_map/ppermute | solution.py:464
  158.1 2.4 %collective-permute-start.28 = (f32[8,256]{1,0:T(8,128)S(1)}, f32[8,256]{1,0:T(8,128)S(1)}, u32[]{:S(2)}, u32[]{:S(2)}) collective-permute-start(f32[8,256]{1,0:T(8,128)S(1)} %add.67.refs_0_), channel_id=1, source_target_pairs={{0,3},{1,2},{2,1},{3,0},{4,7},{5,6},{6,5},{7,4},{8,11},{9,10},{10,... | collective-permute-start | bytes 24584 | tf_op jit(solution)/shard_map/ppermute | solution.py:555
  160.5 2.0 %collective-permute-start.26 = (f32[8,256]{1,0:T(8,128)S(1)}, f32[8,256]{1,0:T(8,128)S(1)}, u32[]{:S(2)}, u32[]{:S(2)}) collective-permute-start(f32[8,256]{1,0:T(8,128)S(1)} %add.67.refs_0_), channel_id=1, source_target_pairs={{0,1},{1,0},{2,3},{3,2},{4,5},{5,4},{6,7},{7,6},{8,9},{9,8},{10,11... | collective-permute-start | bytes 24584 | tf_op jit(solution)/shard_map/ppermute | solution.py:555
  163.5 1.5 collective-permute-done.27.refs_2_
  165.2 14.0 %finish.1 = (f32[1024,4096]{1,0:T(8,128)}, f32[1024,4096]{1,0:T(8,128)}) custom-call(s32[9]{0:T(128)S(1)} %compare_select_fusion.1.order_ref.refs_0_, bf16[1024,768]{1,0:T(8,128)(2,1)S(1)} %get-tuple-element.76.refs_1_, bf16[1024,768]{1,0:T(8,128)(2,1)S(1)} %operand.1.refs_2_, ...), custom_call_target="tpu_custom_call", output_to_operand_aliasing={{0}: (13, {})} | custom-call | flops 9663676416 | bytes 25165824 | tf_op jit(solution)/shard_map/finish/pallas_call | solution.py:387
  (66 shorter events, 21.3 us)
Async XLA Ops:
  10.6 14.4 %collective-permute-start = (f32[384,256]{1,0:T(8,128)S(1)}, f32[384,256]{1,0:T(8,128)S(1)}, u32[]{:S(2)}, u32[]{:S(2)}) collective-permute-start(f32[384,256]{1,0:T(8,128)S(1)} %left.3.refs_0_), channel_id=1, source_target_pairs={{0,1},{3,2},{4,5},{7,6},{8,9},{11,10},{12,13},{15,14},{16,17},{19,... | collective-permute-start | bytes 1179656 | tf_op jit(solution)/shard_map/ppermute | solution.py:490
  18.3 16.6 %collective-permute-start.5 = (f32[384,256]{1,0:T(8,128)S(1)}, f32[384,256]{1,0:T(8,128)S(1)}, u32[]{:S(2)}, u32[]{:S(2)}) collective-permute-start(f32[384,256]{1,0:T(8,128)S(1)} %left.5.refs_0_), channel_id=1, source_target_pairs={{0,1},{3,2},{4,5},{7,6},{8,9},{11,10},{12,13},{15,14},{16,17},{19,... | collective-permute-start | bytes 1179656 | tf_op jit(solution)/shard_map/ppermute | solution.py:490
  25.1 13.8 %collective-permute-start.2 = (f32[384,256]{1,0:T(8,128)S(1)}, f32[384,256]{1,0:T(8,128)S(1)}, u32[]{:S(2)}, u32[]{:S(2)}) collective-permute-start(f32[384,256]{1,0:T(8,128)S(1)} %add.55.refs_0_), channel_id=1, source_target_pairs={{1,2},{2,1},{5,6},{6,5},{9,10},{10,9},{13,14},{14,13},{17,18},{18,... | collective-permute-start | bytes 1179656 | tf_op jit(solution)/shard_map/ppermute | solution.py:493
  27.7 11.1 %collective-permute-start.1 = (f32[256,256]{1,0:T(8,128)S(1)}, f32[256,256]{1,0:T(8,128)S(1)}, u32[]{:S(2)}, u32[]{:S(2)}) collective-permute-start(f32[256,256]{1,0:T(8,128)S(1)} %left.4.refs_0_), channel_id=1, source_target_pairs={{0,1},{3,2},{4,5},{7,6},{8,9},{11,10},{12,13},{15,14},{16,17},{19,... | collective-permute-start | bytes 786440 | tf_op jit(solution)/shard_map/ppermute | solution.py:490
  35.0 5.9 %collective-permute-start.6 = (f32[384,256]{1,0:T(8,128)S(1)}, f32[384,256]{1,0:T(8,128)S(1)}, u32[]{:S(2)}, u32[]{:S(2)}) collective-permute-start(f32[384,256]{1,0:T(8,128)S(1)} %add.59.refs_0_), channel_id=1, source_target_pairs={{1,2},{2,1},{5,6},{6,5},{9,10},{10,9},{13,14},{14,13},{17,18},{18,... | collective-permute-start | bytes 1179656 | tf_op jit(solution)/shard_map/ppermute | solution.py:493
  38.9 11.7 %collective-permute-start.8 = (f32[384,256]{1,0:T(8,128)S(1)}, f32[384,256]{1,0:T(8,128)S(1)}, u32[]{:S(2)}, u32[]{:S(2)}) collective-permute-start(f32[384,256]{1,0:T(8,128)S(1)} %add.57.a_ref), channel_id=1, source_target_pairs={{1,0},{2,3},{5,4},{6,7},{9,8},{10,11},{13,12},{14,15},{17,16},{18,... | collective-permute-start | bytes 1179656 | tf_op jit(solution)/shard_map/ppermute | solution.py:496
  40.2 2.1 %collective-permute-start.3 = (f32[256,256]{1,0:T(8,128)S(1)}, f32[256,256]{1,0:T(8,128)S(1)}, u32[]{:S(2)}, u32[]{:S(2)}) collective-permute-start(f32[256,256]{1,0:T(8,128)S(1)} %add.56.refs_0_), channel_id=1, source_target_pairs={{1,2},{2,1},{5,6},{6,5},{9,10},{10,9},{13,14},{14,13},{17,18},{18,... | collective-permute-start | bytes 786440 | tf_op jit(solution)/shard_map/ppermute | solution.py:493
  40.9 18.9 %collective-permute-start.7 = (f32[384,256]{1,0:T(8,128)S(1)}, f32[384,256]{1,0:T(8,128)S(1)}, u32[]{:S(2)}, u32[]{:S(2)}) collective-permute-start(f32[384,256]{1,0:T(8,128)S(1)} %add.60.a_ref), channel_id=1, source_target_pairs={{1,0},{2,3},{5,4},{6,7},{9,8},{10,11},{13,12},{14,15},{17,16},{18,... | collective-permute-start | bytes 1179656 | tf_op jit(solution)/shard_map/ppermute | solution.py:496
  42.3 22.3 %collective-permute-start.4 = (f32[256,256]{1,0:T(8,128)S(1)}, f32[256,256]{1,0:T(8,128)S(1)}, u32[]{:S(2)}, u32[]{:S(2)}) collective-permute-start(f32[256,256]{1,0:T(8,128)S(1)} %add.58.a_ref), channel_id=1, source_target_pairs={{1,0},{2,3},{5,4},{6,7},{9,8},{10,11},{13,12},{14,15},{17,16},{18,... | collective-permute-start | bytes 786440 | tf_op jit(solution)/shard_map/ppermute | solution.py:496
  66.5 2.9 %collective-permute-start.9 = (f32[2,256,512]{2,1,0:T(8,128)S(1)}, f32[2,256,512]{2,1,0:T(8,128)S(1)}, u32[]{:S(2)}, u32[]{:S(2)}) collective-permute-start(f32[2,256,512]{2,1,0:T(8,128)S(1)} %raw_right.8), channel_id=1, source_target_pairs={{0,4},{4,0},{8,12},{12,8},{16,20},{20,16},{24,28},{28,24},{1,5},{5... | collective-permute-start | bytes 3145736 | tf_op jit(solution)/shard_map/ppermute | solution.py:464
  67.5 1.8 %collective-permute-start.11 = (f32[128,256]{1,0:T(8,128)S(1)}, f32[128,256]{1,0:T(8,128)S(1)}, u32[]{:S(2)}, u32[]{:S(2)}) collective-permute-start(f32[128,256]{1,0:T(8,128)S(1)} %get-tuple-element.104), channel_id=1, source_target_pairs={{0,4},{4,0},{8,12},{12,8},{16,20},{20,16},{24,28},{28,24},{1,5},{5... | collective-permute-start | bytes 393224 | tf_op jit(solution)/shard_map/ppermute | solution.py:464
  69.5 20.6 %collective-permute-start.10 = (f32[2,256,512]{2,1,0:T(8,128)S(1)}, f32[2,256,512]{2,1,0:T(8,128)S(1)}, u32[]{:S(2)}, u32[]{:S(2)}) collective-permute-start(f32[2,256,512]{2,1,0:T(8,128)S(1)} %add.61), channel_id=1, source_target_pairs={{0,8},{4,20},{8,0},{12,28},{16,24},{20,4},{24,16},{28,12},{1,9},{5... | collective-permute-start | bytes 3145736 | tf_op jit(solution)/shard_map/ppermute | solution.py:464
  72.3 17.8 %collective-permute-start.16 = (f32[2,256,512]{2,1,0:T(8,128)S(1)}, f32[2,256,512]{2,1,0:T(8,128)S(1)}, u32[]{:S(2)}, u32[]{:S(2)}) collective-permute-start(f32[2,256,512]{2,1,0:T(8,128)S(1)} %raw_right.11), channel_id=1, source_target_pairs={{0,4},{4,0},{8,12},{12,8},{16,20},{20,16},{24,28},{28,24},{1,5},{5... | collective-permute-start | bytes 3145736 | tf_op jit(solution)/shard_map/ppermute | solution.py:464
  72.4 17.2 %collective-permute-start.14 = (f32[128,256]{1,0:T(8,128)S(1)}, f32[128,256]{1,0:T(8,128)S(1)}, u32[]{:S(2)}, u32[]{:S(2)}) collective-permute-start(f32[128,256]{1,0:T(8,128)S(1)} %add.62.refs_0_), channel_id=1, source_target_pairs={{0,24},{4,28},{8,16},{12,20},{16,8},{20,12},{24,0},{28,4},{1,25},{... | collective-permute-start | bytes 393224 | tf_op jit(solution)/shard_map/ppermute | solution.py:464
  73.9 15.6 %collective-permute-start.13 = (f32[128,256]{1,0:T(8,128)S(1)}, f32[128,256]{1,0:T(8,128)S(1)}, u32[]{:S(2)}, u32[]{:S(2)}) collective-permute-start(f32[128,256]{1,0:T(8,128)S(1)} %add.62.refs_0_), channel_id=1, source_target_pairs={{0,16},{4,12},{8,24},{12,4},{16,0},{20,28},{24,8},{28,20},{1,17},{... | collective-permute-start | bytes 393224 | tf_op jit(solution)/shard_map/ppermute | solution.py:464
  75.2 14.9 %collective-permute-start.12 = (f32[128,256]{1,0:T(8,128)S(1)}, f32[128,256]{1,0:T(8,128)S(1)}, u32[]{:S(2)}, u32[]{:S(2)}) collective-permute-start(f32[128,256]{1,0:T(8,128)S(1)} %add.62.refs_0_), channel_id=1, source_target_pairs={{0,8},{4,20},{8,0},{12,28},{16,24},{20,4},{24,16},{28,12},{1,9},{5... | collective-permute-start | bytes 393224 | tf_op jit(solution)/shard_map/ppermute | solution.py:464
  90.3 46.4 %collective-permute-start.17 = (f32[1,256,512]{2,1,0:T(8,128)S(1)}, f32[1,256,512]{2,1,0:T(8,128)S(1)}, u32[]{:S(2)}, u32[]{:S(2)}) collective-permute-start(f32[1,256,512]{2,1,0:T(8,128)S(1)} %get-tuple-element.81), channel_id=1, source_target_pairs={{0,16},{4,12},{8,24},{12,4},{16,0},{20,28},{24,8},{28,20},{1,17},{... | collective-permute-start | bytes 1572872 | tf_op jit(solution)/shard_map/ppermute | solution.py:464
  91.8 1.3 collective-permute-start.15
  136.7 6.0 %collective-permute-start.21 = (f32[1,256,512]{2,1,0:T(8,128)S(1)}, f32[1,256,512]{2,1,0:T(8,128)S(1)}, u32[]{:S(2)}, u32[]{:S(2)}) collective-permute-start(f32[1,256,512]{2,1,0:T(8,128)S(1)} %add.64.raw_ref.refs_4_), channel_id=1, source_target_pairs={{0,4},{4,0},{8,12},{12,8},{16,20},{20,16},{24,28},{28,24},{1,5},{5... | collective-permute-start | bytes 1572872 | tf_op jit(solution)/shard_map/ppermute | solution.py:464
  137.0 11.4 %collective-permute-start.20 = (f32[1,256,512]{2,1,0:T(8,128)S(1)}, f32[1,256,512]{2,1,0:T(8,128)S(1)}, u32[]{:S(2)}, u32[]{:S(2)}) collective-permute-start(f32[1,256,512]{2,1,0:T(8,128)S(1)} %add.64.raw_ref.refs_4_), channel_id=1, source_target_pairs={{0,16},{4,12},{8,24},{12,4},{16,0},{20,28},{24,8},{28,20},{1,17},{... | collective-permute-start | bytes 1572872 | tf_op jit(solution)/shard_map/ppermute | solution.py:464
  138.8 1.9 %collective-permute-start.18 = (f32[8,256]{1,0:T(8,128)S(1)}, f32[8,256]{1,0:T(8,128)S(1)}, u32[]{:S(2)}, u32[]{:S(2)}) collective-permute-start(f32[8,256]{1,0:T(8,128)S(1)} %squares.1.refs_0_), channel_id=1, source_target_pairs={{0,4},{4,0},{8,12},{12,8},{16,20},{20,16},{24,28},{28,24},{1,5},{5... | collective-permute-start | bytes 24584 | tf_op jit(solution)/shard_map/ppermute | solution.py:464
  140.7 5.8 %collective-permute-start.19 = (f32[8,256]{1,0:T(8,128)S(1)}, f32[8,256]{1,0:T(8,128)S(1)}, u32[]{:S(2)}, u32[]{:S(2)}) collective-permute-start(f32[8,256]{1,0:T(8,128)S(1)} %add.65.refs_0_), channel_id=1, source_target_pairs={{0,8},{4,20},{8,0},{12,28},{16,24},{20,4},{24,16},{28,12},{1,9},{5... | collective-permute-start | bytes 24584 | tf_op jit(solution)/shard_map/ppermute | solution.py:464
  141.5 9.7 %collective-permute-start.24 = (f32[1,256,512]{2,1,0:T(8,128)S(1)}, f32[1,256,512]{2,1,0:T(8,128)S(1)}, u32[]{:S(2)}, u32[]{:S(2)}) collective-permute-start(f32[1,256,512]{2,1,0:T(8,128)S(1)} %add.64.raw_ref.refs_4_), channel_id=1, source_target_pairs={{0,8},{4,20},{8,0},{12,28},{16,24},{20,4},{24,16},{28,12},{1,9},{5... | collective-permute-start | bytes 1572872 | tf_op jit(solution)/shard_map/ppermute | solution.py:464
  148.4 2.9 %collective-permute-start.23 = (f32[1,256,512]{2,1,0:T(8,128)S(1)}, f32[1,256,512]{2,1,0:T(8,128)S(1)}, u32[]{:S(2)}, u32[]{:S(2)}) collective-permute-start(f32[1,256,512]{2,1,0:T(8,128)S(1)} %collective-permute-done.20.refs_4_), channel_id=1, source_target_pairs={{0,4},{4,0},{8,12},{12,8},{16,20},{20,16},{24,28},{28,24},{1,5},{5... | collective-permute-start | bytes 1572872 | tf_op jit(solution)/shard_map/ppermute | solution.py:464
  148.4 9.2 %collective-permute-start.25 = (f32[1,256,512]{2,1,0:T(8,128)S(1)}, f32[1,256,512]{2,1,0:T(8,128)S(1)}, u32[]{:S(2)}, u32[]{:S(2)}) collective-permute-start(f32[1,256,512]{2,1,0:T(8,128)S(1)} %collective-permute-done.20.refs_4_), channel_id=1, source_target_pairs={{0,8},{4,20},{8,0},{12,28},{16,24},{20,4},{24,16},{28,12},{1,9},{5... | collective-permute-start | bytes 1572872 | tf_op jit(solution)/shard_map/ppermute | solution.py:464
  149.8 5.1 %collective-permute-start.22 = (f32[8,256]{1,0:T(8,128)S(1)}, f32[8,256]{1,0:T(8,128)S(1)}, u32[]{:S(2)}, u32[]{:S(2)}) collective-permute-start(f32[8,256]{1,0:T(8,128)S(1)} %add.66.refs_0_), channel_id=1, source_target_pairs={{0,16},{4,12},{8,24},{12,4},{16,0},{20,28},{24,8},{28,20},{1,17},{... | collective-permute-start | bytes 24584 | tf_op jit(solution)/shard_map/ppermute | solution.py:464
  157.5 7.7 %collective-permute-start.29 = (f32[1,256,512]{2,1,0:T(8,128)S(1)}, f32[1,256,512]{2,1,0:T(8,128)S(1)}, u32[]{:S(2)}, u32[]{:S(2)}) collective-permute-start(f32[1,256,512]{2,1,0:T(8,128)S(1)} %collective-permute-done.24.refs_5_), channel_id=1, source_target_pairs={{0,4},{4,0},{8,12},{12,8},{16,20},{20,16},{24,28},{28,24},{1,5},{5... | collective-permute-start | bytes 1572872 | tf_op jit(solution)/shard_map/ppermute | solution.py:464
  157.7 7.6 %collective-permute-start.30 = (f32[1,256,512]{2,1,0:T(8,128)S(1)}, f32[1,256,512]{2,1,0:T(8,128)S(1)}, u32[]{:S(2)}, u32[]{:S(2)}) collective-permute-start(f32[1,256,512]{2,1,0:T(8,128)S(1)} %collective-permute-done.25.refs_7_), channel_id=1, source_target_pairs={{0,4},{4,0},{8,12},{12,8},{16,20},{20,16},{24,28},{28,24},{1,5},{5... | collective-permute-start | bytes 1572872 | tf_op jit(solution)/shard_map/ppermute | solution.py:464
  158.1 5.4 %collective-permute-start.28 = (f32[8,256]{1,0:T(8,128)S(1)}, f32[8,256]{1,0:T(8,128)S(1)}, u32[]{:S(2)}, u32[]{:S(2)}) collective-permute-start(f32[8,256]{1,0:T(8,128)S(1)} %add.67.refs_0_), channel_id=1, source_target_pairs={{0,3},{1,2},{2,1},{3,0},{4,7},{5,6},{6,5},{7,4},{8,11},{9,10},{10,... | collective-permute-start | bytes 24584 | tf_op jit(solution)/shard_map/ppermute | solution.py:555
  160.5 4.5 %collective-permute-start.27 = (f32[8,256]{1,0:T(8,128)S(1)}, f32[8,256]{1,0:T(8,128)S(1)}, u32[]{:S(2)}, u32[]{:S(2)}) collective-permute-start(f32[8,256]{1,0:T(8,128)S(1)} %add.67.refs_0_), channel_id=1, source_target_pairs={{0,2},{1,3},{2,0},{3,1},{4,6},{5,7},{6,4},{7,5},{8,10},{9,11},{10,... | collective-permute-start | bytes 24584 | tf_op jit(solution)/shard_map/ppermute | solution.py:555
  160.5 4.5 %collective-permute-start.26 = (f32[8,256]{1,0:T(8,128)S(1)}, f32[8,256]{1,0:T(8,128)S(1)}, u32[]{:S(2)}, u32[]{:S(2)}) collective-permute-start(f32[8,256]{1,0:T(8,128)S(1)} %add.67.refs_0_), channel_id=1, source_target_pairs={{0,1},{1,0},{2,3},{3,2},{4,5},{5,4},{6,7},{7,6},{8,9},{9,8},{10,11... | collective-permute-start | bytes 24584 | tf_op jit(solution)/shard_map/ppermute | solution.py:555

commit v4 on v3

--- a/solution.py
+++ b/solution.py
@@ -545,15 +545,14 @@
     got, chunk_1, new[0] = together(got, chunk_1, new[0])
     chunk_3, pair_1 = along(chunk_1, NEAR), along(chunk_1, PAIR)
     squares = add(squares, got)
-    got = along(squares, FAR)
+    gots = [lax.ppermute(squares, "col", [(c, c ^ d) for c in range(LINE)]) for d in range(1, LINE)]
     pair_1, chunk_2 = together(pair_1, chunk_2)
     new, right = new_chunks(order, (1, 5), operand, inverse, [chunk_1, pair_1], resident, new)
     rights += right
-    got, chunk_2, chunk_3, new[0] = together(got, chunk_2, chunk_3, new[0])
+    *gots, chunk_2, chunk_3, new[0] = together(*gots, chunk_2, chunk_3, new[0])
     pair_2, pair_3 = along(chunk_2, PAIR), along(chunk_3, PAIR)
-    squares = add(squares, got)
-    gots = [lax.ppermute(squares, "col", [(c, c ^ d) for c in range(LINE)]) for d in range(1, LINE)]
-    scaled = update_operand([squares] + gots, orth, scale)
+    squares = add(squares, *gots)
+    scaled = update_operand([squares, along(squares, FAR)], orth, scale)
     raws = [chunk_2, pair_2, chunk_3, pair_3]
     return tuple(
         finish(order, (2, 6, 3, 7), (0, 4, 1, 5), operand, scaled, inverse, resident, raws, rights, new[0])

time: 180 us -> 177 us (0.983)
  waiting for transfers between devices: 42.9 us -> 40 us
    ppermute x3, waiting for transfers between devices: 2.57 us -> 0.01 us  [local(): lax.ppermute(squares, 'col', [(c, c ^ d) for c in range(LINE)])]
  transfers between devices with their start and end apart: 31 -> 31, of which waited for: 13 -> 10; matrix products, arithmetic and copies ran while one was open for 0% -> 0% of each run, Pallas kernels for 40% -> 41%
where the time goes in v4:
time: 177 us
  Pallas kernels  97.5 us (55%)
  waiting for transfers between devices  40 us (23%)
  starting transfers between devices  37.7 us (21%)
    pallas_call x1, Pallas kernels, factor(): pl.pallas_call(lambda *refs: factor_kernel(len(lefts), RING // 2, *refs),...  43.5 us
    ppermute x19, waiting for transfers between devices, along(): return lax.ppermute(x, 'row', pairs)  20.1 us
    pallas_call x1, Pallas kernels, finish(): pl.pallas_call(lambda *refs: finish_kernel(places, done, *refs), in_specs...  14 us
    ppermute x19, starting transfers between devices, along(): return lax.ppermute(x, 'row', pairs)  13.8 us
    ppermute x3, starting transfers between devices, inward(): return lax.ppermute(x, 'col', [(0, 1), (3, 2)])  13.5 us
    pallas_call x6, Pallas kernels, raw_pieces(): pl.pallas_call(lambda *refs: raw_kernel(at, groups, bool(before), with_gr...  13.1 us
    ppermute x3, waiting for transfers between devices, outward(): return lax.ppermute(x, 'col', [(1, 0), (2, 3)])  11.4 us
    ppermute x3, waiting for transfers between devices, inward(): return lax.ppermute(x, 'col', [(0, 1), (3, 2)])  8.46 us
  transfers between devices with their start and end apart: 31, of which 10 were waited for; matrix products, arithmetic and copies ran while one was open for 0% of the time, Pallas kernels for 41%

profile of v4, /device:TPU:0, one launch (start us, length us, event | category | flops | bytes accessed | tf_op | source)
XLA Modules:
  0.0 176.6 jit_solution(1185420112374001525)
XLA Ops:
  0.7 7.1 %fetch.1 = (f32[1024,4096]{1,0:T(8,128)S(1)}, bf16[4096,256]{1,0:T(8,128)(2,1)S(1)}, bf16[4096,256]{1,0:T(8,128)(2,1)S(1)}) custom-call(f32[1024,4096]{1,0:T(8,128)} %m_hbm.1, f32[4096,256]{1,0:T(8,128)} %q_hbm), custom_call_target="tpu_custom_call" | custom-call | flops 1048576 | bytes 20971520 | tf_op jit(solution)/shard_map/fetch/pallas_call | solution.py:72
  7.8 2.8 %left.3.refs_0_ = f32[384,256]{1,0:T(8,128)S(1)} custom-call(f32[1024,4096]{1,0:T(8,128)S(1)} %get-tuple-element.57.refs_0_.refs_2_.refs_3_.refs_4_, bf16[4096,256]{1,0:T(8,128)(2,1)S(1)} %get-tuple-element.60.refs_1_, bf16[4096,256]{1,0:T(8,128)(2,1)S(1)} %get-tuple-element.59.refs_2_), custom_call_target="tpu_custom_call" | custom-call | flops 2415919104 | bytes 1048576 | tf_op jit(solution)/shard_map/left/pallas_call | solution.py:101
  10.6 5.0 %collective-permute-start = (f32[384,256]{1,0:T(8,128)S(1)}, f32[384,256]{1,0:T(8,128)S(1)}, u32[]{:S(2)}, u32[]{:S(2)}) collective-permute-start(f32[384,256]{1,0:T(8,128)S(1)} %left.3.refs_0_), channel_id=1, source_target_pairs={{0,1},{3,2},{4,5},{7,6},{8,9},{11,10},{12,13},{15,14},{16,17},{19,... | collective-permute-start | bytes 1179656 | tf_op jit(solution)/shard_map/ppermute | solution.py:490
  15.5 2.8 %left.5.refs_0_ = f32[384,256]{1,0:T(8,128)S(1)} custom-call(f32[1024,4096]{1,0:T(8,128)S(1)} %get-tuple-element.57.refs_0_.refs_2_.refs_3_.refs_4_, bf16[4096,256]{1,0:T(8,128)(2,1)S(1)} %get-tuple-element.60.refs_1_, bf16[4096,256]{1,0:T(8,128)(2,1)S(1)} %get-tuple-element.59.refs_2_), custom_call_target="tpu_custom_call" | custom-call | flops 2415919104 | bytes 1048576 | tf_op jit(solution)/shard_map/left/pallas_call | solution.py:101
  18.3 1.3 collective-permute-start.5
  19.7 5.4 %collective-permute-done.refs_1_ = f32[384,256]{1,0:T(8,128)S(1)} collective-permute-done((f32[384,256]{1,0:T(8,128)S(1)}, f32[384,256]{1,0:T(8,128)S(1)}, u32[]{:S(2)}, u32[]{:S(2)}) %collective-permute-start) | collective-permute-done | bytes 393248 | tf_op jit(solution)/shard_map/ppermute | solution.py:490
  25.8 2.0 %left.4.refs_0_ = f32[256,256]{1,0:T(8,128)S(1)} custom-call(f32[1024,4096]{1,0:T(8,128)S(1)} %get-tuple-element.57.refs_0_.refs_2_.refs_3_.refs_4_, bf16[4096,256]{1,0:T(8,128)(2,1)S(1)} %get-tuple-element.60.refs_1_, bf16[4096,256]{1,0:T(8,128)(2,1)S(1)} %get-tuple-element.59.refs_2_), custom_call_target="tpu_custom_call" | custom-call | flops 1610612736 | bytes 1048576 | tf_op jit(solution)/shard_map/left/pallas_call | solution.py:101
  27.7 7.2 %collective-permute-start.1 = (f32[256,256]{1,0:T(8,128)S(1)}, f32[256,256]{1,0:T(8,128)S(1)}, u32[]{:S(2)}, u32[]{:S(2)}) collective-permute-start(f32[256,256]{1,0:T(8,128)S(1)} %left.4.refs_0_), channel_id=1, source_target_pairs={{0,1},{3,2},{4,5},{7,6},{8,9},{11,10},{12,13},{15,14},{16,17},{19,... | collective-permute-start | bytes 786440 | tf_op jit(solution)/shard_map/ppermute | solution.py:490
  35.7 3.1 %collective-permute-done.1.refs_1_ = f32[256,256]{1,0:T(8,128)S(1)} collective-permute-done((f32[256,256]{1,0:T(8,128)S(1)}, f32[256,256]{1,0:T(8,128)S(1)}, u32[]{:S(2)}, u32[]{:S(2)}) %collective-permute-start.1) | collective-permute-done | bytes 262176 | tf_op jit(solution)/shard_map/ppermute | solution.py:490
  38.9 1.3 collective-permute-start.8
  40.9 1.3 collective-permute-start.7
  42.3 1.5 collective-permute-start.4
  43.8 6.8 %collective-permute-done.8.b_ref = f32[384,256]{1,0:T(8,128)S(1)} collective-permute-done((f32[384,256]{1,0:T(8,128)S(1)}, f32[384,256]{1,0:T(8,128)S(1)}, u32[]{:S(2)}, u32[]{:S(2)}) %collective-permute-start.8) | collective-permute-done | bytes 393248 | tf_op jit(solution)/shard_map/ppermute | solution.py:496
  51.2 4.1 %raw_right.6 = (f32[2,256,512]{2,1,0:T(8,128)S(1)}, f32[2,256,512]{2,1,0:T(8,128)S(1)}, f32[2,256,512]{2,1,0:T(8,128)S(1)}, f32[2,256,512]{2,1,0:T(8,128)S(1)}, f32[256,256]{1,0:T(8,128)S(1)}) custom-call(s32[9]{0:T(128)S(1)} %compare_select_fusion.1.order_ref.refs_0_, f32[384,256]{1,0:T(8,128)S(1)} %choose.5.refs_1_.refs_3_, ...), custom_call_target="tpu_custom_call" | custom-call | flops 2415919104 | bytes 1048576 | tf_op jit(solution)/shard_map/raw_right/pallas_call | solution.py:134
  55.3 4.6 %collective-permute-done.7.b_ref = f32[384,256]{1,0:T(8,128)S(1)} collective-permute-done((f32[384,256]{1,0:T(8,128)S(1)}, f32[384,256]{1,0:T(8,128)S(1)}, u32[]{:S(2)}, u32[]{:S(2)}) %collective-permute-start.7) | collective-permute-done | bytes 393248 | tf_op jit(solution)/shard_map/ppermute | solution.py:496
  60.4 4.2 %raw_right.7 = (f32[2,256,512]{2,1,0:T(8,128)S(1)}, f32[2,256,512]{2,1,0:T(8,128)S(1)}, f32[2,256,512]{2,1,0:T(8,128)S(1)}, f32[2,256,512]{2,1,0:T(8,128)S(1)}, f32[256,256]{1,0:T(8,128)S(1)}) custom-call(s32[9]{0:T(128)S(1)} %compare_select_fusion.1.order_ref.refs_0_, f32[384,256]{1,0:T(8,128)S(1)} %choose.4.refs_1_.refs_4_, ...), custom_call_target="tpu_custom_call" | custom-call | flops 2415919104 | bytes 1048576 | tf_op jit(solution)/shard_map/raw_right/pallas_call | solution.py:134
  69.5 1.5 collective-permute-start.10
  72.4 1.6 collective-permute-start.14
  73.9 1.3 collective-permute-start.13
  77.1 12.4 %collective-permute-done.14.refs_3_ = f32[128,256]{1,0:T(8,128)S(1)} collective-permute-done((f32[128,256]{1,0:T(8,128)S(1)}, f32[128,256]{1,0:T(8,128)S(1)}, u32[]{:S(2)}, u32[]{:S(2)}) %collective-permute-start.14) | collective-permute-done | bytes 131104 | tf_op jit(solution)/shard_map/ppermute | solution.py:464
  90.3 1.5 collective-permute-start.17
  91.8 1.3 collective-permute-done.15.refs_2_
  93.1 43.5 %factor.1 = (f32[256,256]{1,0:T(8,128)S(1)}, f32[1024,256]{1,0:T(8,128)S(1)}, bf16[1024,768]{1,0:T(8,128)(2,1)S(1)}) custom-call(s32[9]{0:T(128)S(1)} %compare_select_fusion.1.order_ref.refs_0_, f32[128,256]{1,0:T(8,128)S(1)} %add.63.refs_1_, f32[128,256]{1,0:T(8,128)S(1)} %collective-permute-done.15.refs_2_, f32[384,256]{1,0:T(8,128)S(1)} %choose.5.refs_1_.refs_3_, ...), custom_call_target="tpu_custom_call" | custom-call | flops 1 | bytes 1 | tf_op jit(solution)/shard_map/factor/pallas_call | solution.py:246
  137.5 1.3 squares.1.refs_0_
  142.8 3.7 %new_momentum.2 = (f32[1024,4096]{1,0:T(8,128)}, bf16[768,512]{1,0:T(8,128)(2,1)S(1)}, bf16[768,512]{1,0:T(8,128)(2,1)S(1)}) custom-call(s32[9]{0:T(128)S(1)} %compare_select_fusion.1.order_ref.refs_0_, bf16[1024,768]{1,0:T(8,128)(2,1)S(1)} %get-tuple-element.78.refs_1_, f32[256,256]{1,0:T(8,128)S(1)} %get-tuple-element.85.inv_ref.refs_2_.refs_3_, ...), custom_call_target="tpu_custom_call" | custom-call | flops 1610612736 | bytes 4194304 | tf_op jit(solution)/shard_map/new_momentum/pallas_call | solution.py:330
  146.5 1.9 %collective-permute-done.20.refs_4_ = f32[1,256,512]{2,1,0:T(8,128)S(1)} collective-permute-done((f32[1,256,512]{2,1,0:T(8,128)S(1)}, f32[1,256,512]{2,1,0:T(8,128)S(1)}, u32[]{:S(2)}, u32[]{:S(2)}) %collective-permute-start.20) | collective-permute-done | bytes 524320 | tf_op jit(solution)/shard_map/ppermute | solution.py:464
  148.4 1.5 collective-permute-start.27
  149.8 2.4 %collective-permute-start.24 = (f32[8,256]{1,0:T(8,128)S(1)}, f32[8,256]{1,0:T(8,128)S(1)}, u32[]{:S(2)}, u32[]{:S(2)}) collective-permute-start(f32[8,256]{1,0:T(8,128)S(1)} %add.66.refs_0_), channel_id=1, source_target_pairs={{0,3},{1,2},{2,1},{3,0},{4,7},{5,6},{6,5},{7,4},{8,11},{9,10},{10,... | collective-permute-start | bytes 24584 | tf_op jit(solution)/shard_map/ppermute | solution.py:548
  152.3 2.0 %collective-permute-start.22 = (f32[8,256]{1,0:T(8,128)S(1)}, f32[8,256]{1,0:T(8,128)S(1)}, u32[]{:S(2)}, u32[]{:S(2)}) collective-permute-start(f32[8,256]{1,0:T(8,128)S(1)} %add.66.refs_0_), channel_id=1, source_target_pairs={{0,1},{1,0},{2,3},{3,2},{4,5},{5,4},{6,7},{7,6},{8,9},{9,8},{10,11... | collective-permute-start | bytes 24584 | tf_op jit(solution)/shard_map/ppermute | solution.py:548
  154.2 3.7 %new_momentum.3 = (f32[1024,4096]{1,0:T(8,128)}, bf16[768,512]{1,0:T(8,128)(2,1)S(1)}, bf16[768,512]{1,0:T(8,128)(2,1)S(1)}) custom-call(s32[9]{0:T(128)S(1)} %compare_select_fusion.1.order_ref.refs_0_, bf16[1024,768]{1,0:T(8,128)(2,1)S(1)} %get-tuple-element.78.refs_1_, ...), custom_call_target="tpu_custom_call", output_to_operand_aliasing={{0}: (6, {})} | custom-call | flops 1610612736 | bytes 4194304 | tf_op jit(solution)/shard_map/new_momentum/pallas_call | solution.py:330
  159.1 3.1 %collective-permute-done.28.refs_1_ = f32[8,256]{1,0:T(8,128)S(1)} collective-permute-done((f32[8,256]{1,0:T(8,128)S(1)}, f32[8,256]{1,0:T(8,128)S(1)}, u32[]{:S(2)}, u32[]{:S(2)}) %collective-permute-start.28) | collective-permute-done | bytes 8224 | tf_op jit(solution)/shard_map/ppermute | solution.py:464
  162.4 14.0 %finish.1 = (f32[1024,4096]{1,0:T(8,128)}, f32[1024,4096]{1,0:T(8,128)}) custom-call(s32[9]{0:T(128)S(1)} %compare_select_fusion.1.order_ref.refs_0_, bf16[1024,768]{1,0:T(8,128)(2,1)S(1)} %get-tuple-element.78.refs_1_, bf16[1024,768]{1,0:T(8,128)(2,1)S(1)} %operand.1.refs_2_, ...), custom_call_target="tpu_custom_call", output_to_operand_aliasing={{0}: (13, {})} | custom-call | flops 9663676416 | bytes 25165824 | tf_op jit(solution)/shard_map/finish/pallas_call | solution.py:387
  (66 shorter events, 18.3 us)
Async XLA Ops:
  10.6 14.4 %collective-permute-start = (f32[384,256]{1,0:T(8,128)S(1)}, f32[384,256]{1,0:T(8,128)S(1)}, u32[]{:S(2)}, u32[]{:S(2)}) collective-permute-start(f32[384,256]{1,0:T(8,128)S(1)} %left.3.refs_0_), channel_id=1, source_target_pairs={{0,1},{3,2},{4,5},{7,6},{8,9},{11,10},{12,13},{15,14},{16,17},{19,... | collective-permute-start | bytes 1179656 | tf_op jit(solution)/shard_map/ppermute | solution.py:490
  18.3 16.6 %collective-permute-start.5 = (f32[384,256]{1,0:T(8,128)S(1)}, f32[384,256]{1,0:T(8,128)S(1)}, u32[]{:S(2)}, u32[]{:S(2)}) collective-permute-start(f32[384,256]{1,0:T(8,128)S(1)} %left.5.refs_0_), channel_id=1, source_target_pairs={{0,1},{3,2},{4,5},{7,6},{8,9},{11,10},{12,13},{15,14},{16,17},{19,... | collective-permute-start | bytes 1179656 | tf_op jit(solution)/shard_map/ppermute | solution.py:490
  25.1 13.8 %collective-permute-start.2 = (f32[384,256]{1,0:T(8,128)S(1)}, f32[384,256]{1,0:T(8,128)S(1)}, u32[]{:S(2)}, u32[]{:S(2)}) collective-permute-start(f32[384,256]{1,0:T(8,128)S(1)} %add.55.refs_0_), channel_id=1, source_target_pairs={{1,2},{2,1},{5,6},{6,5},{9,10},{10,9},{13,14},{14,13},{17,18},{18,... | collective-permute-start | bytes 1179656 | tf_op jit(solution)/shard_map/ppermute | solution.py:493
  27.7 11.1 %collective-permute-start.1 = (f32[256,256]{1,0:T(8,128)S(1)}, f32[256,256]{1,0:T(8,128)S(1)}, u32[]{:S(2)}, u32[]{:S(2)}) collective-permute-start(f32[256,256]{1,0:T(8,128)S(1)} %left.4.refs_0_), channel_id=1, source_target_pairs={{0,1},{3,2},{4,5},{7,6},{8,9},{11,10},{12,13},{15,14},{16,17},{19,... | collective-permute-start | bytes 786440 | tf_op jit(solution)/shard_map/ppermute | solution.py:490
  35.0 5.9 %collective-permute-start.6 = (f32[384,256]{1,0:T(8,128)S(1)}, f32[384,256]{1,0:T(8,128)S(1)}, u32[]{:S(2)}, u32[]{:S(2)}) collective-permute-start(f32[384,256]{1,0:T(8,128)S(1)} %add.59.refs_0_), channel_id=1, source_target_pairs={{1,2},{2,1},{5,6},{6,5},{9,10},{10,9},{13,14},{14,13},{17,18},{18,... | collective-permute-start | bytes 1179656 | tf_op jit(solution)/shard_map/ppermute | solution.py:493
  38.9 11.7 %collective-permute-start.8 = (f32[384,256]{1,0:T(8,128)S(1)}, f32[384,256]{1,0:T(8,128)S(1)}, u32[]{:S(2)}, u32[]{:S(2)}) collective-permute-start(f32[384,256]{1,0:T(8,128)S(1)} %add.57.a_ref), channel_id=1, source_target_pairs={{1,0},{2,3},{5,4},{6,7},{9,8},{10,11},{13,12},{14,15},{17,16},{18,... | collective-permute-start | bytes 1179656 | tf_op jit(solution)/shard_map/ppermute | solution.py:496
  40.2 2.1 %collective-permute-start.3 = (f32[256,256]{1,0:T(8,128)S(1)}, f32[256,256]{1,0:T(8,128)S(1)}, u32[]{:S(2)}, u32[]{:S(2)}) collective-permute-start(f32[256,256]{1,0:T(8,128)S(1)} %add.56.refs_0_), channel_id=1, source_target_pairs={{1,2},{2,1},{5,6},{6,5},{9,10},{10,9},{13,14},{14,13},{17,18},{18,... | collective-permute-start | bytes 786440 | tf_op jit(solution)/shard_map/ppermute | solution.py:493
  40.9 18.9 %collective-permute-start.7 = (f32[384,256]{1,0:T(8,128)S(1)}, f32[384,256]{1,0:T(8,128)S(1)}, u32[]{:S(2)}, u32[]{:S(2)}) collective-permute-start(f32[384,256]{1,0:T(8,128)S(1)} %add.60.a_ref), channel_id=1, source_target_pairs={{1,0},{2,3},{5,4},{6,7},{9,8},{10,11},{13,12},{14,15},{17,16},{18,... | collective-permute-start | bytes 1179656 | tf_op jit(solution)/shard_map/ppermute | solution.py:496
  42.3 22.3 %collective-permute-start.4 = (f32[256,256]{1,0:T(8,128)S(1)}, f32[256,256]{1,0:T(8,128)S(1)}, u32[]{:S(2)}, u32[]{:S(2)}) collective-permute-start(f32[256,256]{1,0:T(8,128)S(1)} %add.58.a_ref), channel_id=1, source_target_pairs={{1,0},{2,3},{5,4},{6,7},{9,8},{10,11},{13,12},{14,15},{17,16},{18,... | collective-permute-start | bytes 786440 | tf_op jit(solution)/shard_map/ppermute | solution.py:496
  66.5 2.9 %collective-permute-start.9 = (f32[2,256,512]{2,1,0:T(8,128)S(1)}, f32[2,256,512]{2,1,0:T(8,128)S(1)}, u32[]{:S(2)}, u32[]{:S(2)}) collective-permute-start(f32[2,256,512]{2,1,0:T(8,128)S(1)} %raw_right.8), channel_id=1, source_target_pairs={{0,4},{4,0},{8,12},{12,8},{16,20},{20,16},{24,28},{28,24},{1,5},{5... | collective-permute-start | bytes 3145736 | tf_op jit(solution)/shard_map/ppermute | solution.py:464
  67.5 1.8 %collective-permute-start.11 = (f32[128,256]{1,0:T(8,128)S(1)}, f32[128,256]{1,0:T(8,128)S(1)}, u32[]{:S(2)}, u32[]{:S(2)}) collective-permute-start(f32[128,256]{1,0:T(8,128)S(1)} %get-tuple-element.108), channel_id=1, source_target_pairs={{0,4},{4,0},{8,12},{12,8},{16,20},{20,16},{24,28},{28,24},{1,5},{5... | collective-permute-start | bytes 393224 | tf_op jit(solution)/shard_map/ppermute | solution.py:464
  69.5 20.6 %collective-permute-start.10 = (f32[2,256,512]{2,1,0:T(8,128)S(1)}, f32[2,256,512]{2,1,0:T(8,128)S(1)}, u32[]{:S(2)}, u32[]{:S(2)}) collective-permute-start(f32[2,256,512]{2,1,0:T(8,128)S(1)} %add.61), channel_id=1, source_target_pairs={{0,8},{4,20},{8,0},{12,28},{16,24},{20,4},{24,16},{28,12},{1,9},{5... | collective-permute-start | bytes 3145736 | tf_op jit(solution)/shard_map/ppermute | solution.py:464
  72.3 17.8 %collective-permute-start.16 = (f32[2,256,512]{2,1,0:T(8,128)S(1)}, f32[2,256,512]{2,1,0:T(8,128)S(1)}, u32[]{:S(2)}, u32[]{:S(2)}) collective-permute-start(f32[2,256,512]{2,1,0:T(8,128)S(1)} %raw_right.11), channel_id=1, source_target_pairs={{0,4},{4,0},{8,12},{12,8},{16,20},{20,16},{24,28},{28,24},{1,5},{5... | collective-permute-start | bytes 3145736 | tf_op jit(solution)/shard_map/ppermute | solution.py:464
  72.4 17.2 %collective-permute-start.14 = (f32[128,256]{1,0:T(8,128)S(1)}, f32[128,256]{1,0:T(8,128)S(1)}, u32[]{:S(2)}, u32[]{:S(2)}) collective-permute-start(f32[128,256]{1,0:T(8,128)S(1)} %add.62.refs_0_), channel_id=1, source_target_pairs={{0,24},{4,28},{8,16},{12,20},{16,8},{20,12},{24,0},{28,4},{1,25},{... | collective-permute-start | bytes 393224 | tf_op jit(solution)/shard_map/ppermute | solution.py:464
  73.9 15.6 %collective-permute-start.13 = (f32[128,256]{1,0:T(8,128)S(1)}, f32[128,256]{1,0:T(8,128)S(1)}, u32[]{:S(2)}, u32[]{:S(2)}) collective-permute-start(f32[128,256]{1,0:T(8,128)S(1)} %add.62.refs_0_), channel_id=1, source_target_pairs={{0,16},{4,12},{8,24},{12,4},{16,0},{20,28},{24,8},{28,20},{1,17},{... | collective-permute-start | bytes 393224 | tf_op jit(solution)/shard_map/ppermute | solution.py:464
  75.2 14.9 %collective-permute-start.12 = (f32[128,256]{1,0:T(8,128)S(1)}, f32[128,256]{1,0:T(8,128)S(1)}, u32[]{:S(2)}, u32[]{:S(2)}) collective-permute-start(f32[128,256]{1,0:T(8,128)S(1)} %add.62.refs_0_), channel_id=1, source_target_pairs={{0,8},{4,20},{8,0},{12,28},{16,24},{20,4},{24,16},{28,12},{1,9},{5... | collective-permute-start | bytes 393224 | tf_op jit(solution)/shard_map/ppermute | solution.py:464
  90.3 46.4 %collective-permute-start.17 = (f32[1,256,512]{2,1,0:T(8,128)S(1)}, f32[1,256,512]{2,1,0:T(8,128)S(1)}, u32[]{:S(2)}, u32[]{:S(2)}) collective-permute-start(f32[1,256,512]{2,1,0:T(8,128)S(1)} %get-tuple-element.83), channel_id=1, source_target_pairs={{0,16},{4,12},{8,24},{12,4},{16,0},{20,28},{24,8},{28,20},{1,17},{... | collective-permute-start | bytes 1572872 | tf_op jit(solution)/shard_map/ppermute | solution.py:464
  91.8 1.3 collective-permute-start.15
  136.7 6.0 %collective-permute-start.21 = (f32[1,256,512]{2,1,0:T(8,128)S(1)}, f32[1,256,512]{2,1,0:T(8,128)S(1)}, u32[]{:S(2)}, u32[]{:S(2)}) collective-permute-start(f32[1,256,512]{2,1,0:T(8,128)S(1)} %add.64.raw_ref.refs_4_), channel_id=1, source_target_pairs={{0,4},{4,0},{8,12},{12,8},{16,20},{20,16},{24,28},{28,24},{1,5},{5... | collective-permute-start | bytes 1572872 | tf_op jit(solution)/shard_map/ppermute | solution.py:464
  137.0 11.4 %collective-permute-start.20 = (f32[1,256,512]{2,1,0:T(8,128)S(1)}, f32[1,256,512]{2,1,0:T(8,128)S(1)}, u32[]{:S(2)}, u32[]{:S(2)}) collective-permute-start(f32[1,256,512]{2,1,0:T(8,128)S(1)} %add.64.raw_ref.refs_4_), channel_id=1, source_target_pairs={{0,16},{4,12},{8,24},{12,4},{16,0},{20,28},{24,8},{28,20},{1,17},{... | collective-permute-start | bytes 1572872 | tf_op jit(solution)/shard_map/ppermute | solution.py:464
  138.8 1.9 %collective-permute-start.18 = (f32[8,256]{1,0:T(8,128)S(1)}, f32[8,256]{1,0:T(8,128)S(1)}, u32[]{:S(2)}, u32[]{:S(2)}) collective-permute-start(f32[8,256]{1,0:T(8,128)S(1)} %squares.1.refs_0_), channel_id=1, source_target_pairs={{0,4},{4,0},{8,12},{12,8},{16,20},{20,16},{24,28},{28,24},{1,5},{5... | collective-permute-start | bytes 24584 | tf_op jit(solution)/shard_map/ppermute | solution.py:464
  140.7 5.8 %collective-permute-start.19 = (f32[8,256]{1,0:T(8,128)S(1)}, f32[8,256]{1,0:T(8,128)S(1)}, u32[]{:S(2)}, u32[]{:S(2)}) collective-permute-start(f32[8,256]{1,0:T(8,128)S(1)} %add.65.refs_0_), channel_id=1, source_target_pairs={{0,8},{4,20},{8,0},{12,28},{16,24},{20,4},{24,16},{28,12},{1,9},{5... | collective-permute-start | bytes 24584 | tf_op jit(solution)/shard_map/ppermute | solution.py:464
  141.5 10.7 %collective-permute-start.26 = (f32[1,256,512]{2,1,0:T(8,128)S(1)}, f32[1,256,512]{2,1,0:T(8,128)S(1)}, u32[]{:S(2)}, u32[]{:S(2)}) collective-permute-start(f32[1,256,512]{2,1,0:T(8,128)S(1)} %add.64.raw_ref.refs_4_), channel_id=1, source_target_pairs={{0,8},{4,20},{8,0},{12,28},{16,24},{20,4},{24,16},{28,12},{1,9},{5... | collective-permute-start | bytes 1572872 | tf_op jit(solution)/shard_map/ppermute | solution.py:464
  148.4 5.9 %collective-permute-start.25 = (f32[1,256,512]{2,1,0:T(8,128)S(1)}, f32[1,256,512]{2,1,0:T(8,128)S(1)}, u32[]{:S(2)}, u32[]{:S(2)}) collective-permute-start(f32[1,256,512]{2,1,0:T(8,128)S(1)} %collective-permute-done.20.refs_4_), channel_id=1, source_target_pairs={{0,4},{4,0},{8,12},{12,8},{16,20},{20,16},{24,28},{28,24},{1,5},{5... | collective-permute-start | bytes 1572872 | tf_op jit(solution)/shard_map/ppermute | solution.py:464
  148.4 9.6 %collective-permute-start.27 = (f32[1,256,512]{2,1,0:T(8,128)S(1)}, f32[1,256,512]{2,1,0:T(8,128)S(1)}, u32[]{:S(2)}, u32[]{:S(2)}) collective-permute-start(f32[1,256,512]{2,1,0:T(8,128)S(1)} %collective-permute-done.20.refs_4_), channel_id=1, source_target_pairs={{0,8},{4,20},{8,0},{12,28},{16,24},{20,4},{24,16},{28,12},{1,9},{5... | collective-permute-start | bytes 1572872 | tf_op jit(solution)/shard_map/ppermute | solution.py:464
  149.8 8.1 %collective-permute-start.24 = (f32[8,256]{1,0:T(8,128)S(1)}, f32[8,256]{1,0:T(8,128)S(1)}, u32[]{:S(2)}, u32[]{:S(2)}) collective-permute-start(f32[8,256]{1,0:T(8,128)S(1)} %add.66.refs_0_), channel_id=1, source_target_pairs={{0,3},{1,2},{2,1},{3,0},{4,7},{5,6},{6,5},{7,4},{8,11},{9,10},{10,... | collective-permute-start | bytes 24584 | tf_op jit(solution)/shard_map/ppermute | solution.py:548
  152.3 5.7 %collective-permute-start.23 = (f32[8,256]{1,0:T(8,128)S(1)}, f32[8,256]{1,0:T(8,128)S(1)}, u32[]{:S(2)}, u32[]{:S(2)}) collective-permute-start(f32[8,256]{1,0:T(8,128)S(1)} %add.66.refs_0_), channel_id=1, source_target_pairs={{0,2},{1,3},{2,0},{3,1},{4,6},{5,7},{6,4},{7,5},{8,10},{9,11},{10,... | collective-permute-start | bytes 24584 | tf_op jit(solution)/shard_map/ppermute | solution.py:548
  152.3 5.7 %collective-permute-start.22 = (f32[8,256]{1,0:T(8,128)S(1)}, f32[8,256]{1,0:T(8,128)S(1)}, u32[]{:S(2)}, u32[]{:S(2)}) collective-permute-start(f32[8,256]{1,0:T(8,128)S(1)} %add.66.refs_0_), channel_id=1, source_target_pairs={{0,1},{1,0},{2,3},{3,2},{4,5},{5,4},{6,7},{7,6},{8,9},{9,8},{10,11... | collective-permute-start | bytes 24584 | tf_op jit(solution)/shard_map/ppermute | solution.py:548
  158.0 4.4 %collective-permute-start.29 = (f32[1,256,512]{2,1,0:T(8,128)S(1)}, f32[1,256,512]{2,1,0:T(8,128)S(1)}, u32[]{:S(2)}, u32[]{:S(2)}) collective-permute-start(f32[1,256,512]{2,1,0:T(8,128)S(1)} %collective-permute-done.26.refs_5_), channel_id=1, source_target_pairs={{0,4},{4,0},{8,12},{12,8},{16,20},{20,16},{24,28},{28,24},{1,5},{5... | collective-permute-start | bytes 1572872 | tf_op jit(solution)/shard_map/ppermute | solution.py:464
  158.0 4.4 %collective-permute-start.30 = (f32[1,256,512]{2,1,0:T(8,128)S(1)}, f32[1,256,512]{2,1,0:T(8,128)S(1)}, u32[]{:S(2)}, u32[]{:S(2)}) collective-permute-start(f32[1,256,512]{2,1,0:T(8,128)S(1)} %collective-permute-done.27.refs_7_), channel_id=1, source_target_pairs={{0,4},{4,0},{8,12},{12,8},{16,20},{20,16},{24,28},{28,24},{1,5},{5... | collective-permute-start | bytes 1572872 | tf_op jit(solution)/shard_map/ppermute | solution.py:464
  158.6 3.7 %collective-permute-start.28 = (f32[8,256]{1,0:T(8,128)S(1)}, f32[8,256]{1,0:T(8,128)S(1)}, u32[]{:S(2)}, u32[]{:S(2)}) collective-permute-start(f32[8,256]{1,0:T(8,128)S(1)} %add.67.refs_0_), channel_id=1, source_target_pairs={{0,16},{4,12},{8,24},{12,4},{16,0},{20,28},{24,8},{28,20},{1,17},{... | collective-permute-start | bytes 24584 | tf_op jit(solution)/shard_map/ppermute | solution.py:464
